TPU v7x, 1024 devices: a whole 4x4x32 slice. The times are simulated.
1024 devices in a mesh: fsdp: 128 (over x, z), rep: 8 (over y, core).
Axes of the slice: x: 4, y: 4, z: 32, core: 2. Of those that a mesh axis runs over, the one named last changes fastest.
Arguments:
- grads: bfloat16 [8, 128, 512, 512], P('rep', None, 'fsdp'), may hold values from -0.099609375 to 0.099609375
- owner: int32 [128], replicated, may hold values from 0 to 127, as said below
- left_stat: float32 [128, 2, 512, 512], P('fsdp', None, 'rep'), may hold values from -0.1 to 2.1, as said below
- right_stat: float32 [128, 2, 512, 512], P('fsdp', None, 'rep'), may hold values from -0.1 to 2.1, as said below
- left_root: bfloat16 [128, 2, 512, 512], P('fsdp', None, 'rep'), as said below
- right_root: bfloat16 [128, 2, 512, 512], P('fsdp', None, 'rep'), as said below
Outputs:
- left_new: float32 [128, 2, 512, 512], P('fsdp', None, 'rep')
- right_new: float32 [128, 2, 512, 512], P('fsdp', None, 'rep')
- update: bfloat16 [128, 512, 512], P(None, 'fsdp', 'rep')
Inputs may be any that keep to these rules, and one draw needn't show every extreme that they name: `owner`: every fsdp rank owns at most 2 blocks, and some rank owns exactly 2; rank 128 - 1 owns at least one block. `left_stat`: each matrix is symmetric. `right_stat`: each matrix is symmetric. `left_root`: each matrix is symmetric. `right_root`: each matrix is symmetric.
All inputs are finite; a program needn't handle non-finite values.
Results may differ from a plain program's by a relative error of at most 0.023.
Values may be sent and summed in bfloat16 or wider, within the bound.
No kernel may reach another device: no remote copies, remote signals or barrier semaphores. Data moves between devices by JAX's collectives and lax.ppermute only.
A program may use at most 32 MiB of HBM per device.

v0:
```python
import jax
import jax.numpy as jnp
from jax import lax
from jax.sharding import PartitionSpec as P

GROUP = 128
SLOTS = 2


stat_decay = 0.95


def hadamard(length):
    counter = jnp.arange(length, dtype=jnp.int32)
    correlation = counter[:, None] & counter[None, :]
    parity = jnp.zeros((length, length), jnp.int32)
    for bit_pos in range(length.bit_length() - 1):
        parity = parity ^ correlation >> bit_pos & 1
    return (1 - 2 * parity).astype(jnp.bfloat16)


def on_device(grads, owner, left_stat, right_stat, left_root, right_root):
    fsdp_count = lax.axis_size("fsdp")
    rep_count = lax.axis_size("rep")
    signs = hadamard(GROUP)
    norm_factor = GROUP ** (-0.5)
    partial_value = grads[0]
    blocks_all, rows_fsdp, width = partial_value.shape
    slab = width // rep_count
    lroot_rows = left_root[0]
    shaped = partial_value.reshape(blocks_all, rows_fsdp, width // GROUP, GROUP)
    turned = (
        jnp.einsum("bfgk,kj->bfgj", shaped, signs, preferred_element_type=jnp.float32) * norm_factor
    )
    peak_abs = jnp.max(jnp.abs(turned), axis=-1) + 1e-06
    scales_low = lax.optimization_barrier(peak_abs.astype(jnp.bfloat16))
    scales = scales_low.astype(jnp.float32)
    quantized = (turned / scales[..., None]).astype(jnp.bfloat16)
    terms = (quantized.astype(jnp.float32) * scales[..., None]).reshape(
        blocks_all, rows_fsdp, width
    )
    summed = lax.psum_scatter(terms.astype(jnp.bfloat16), "rep", scatter_dimension=2, tiled=True)
    counter = jnp.arange(blocks_all, dtype=jnp.int32)
    same_owner = owner[:, None] == owner[None, :]
    slot_of = jnp.sum(same_owner & (counter[None, :] < counter[:, None]), axis=1)
    target = slot_of * fsdp_count + owner
    routing = (target[None, :] == jnp.arange(SLOTS * fsdp_count, dtype=jnp.int32)[:, None]).astype(
        jnp.bfloat16
    )
    outgoing = jnp.dot(
        routing, summed.reshape(blocks_all, rows_fsdp * slab), preferred_element_type=jnp.float32
    )
    outgoing = outgoing.astype(jnp.bfloat16).reshape(SLOTS, fsdp_count, rows_fsdp, slab)
    arrived = lax.all_to_all(outgoing, "fsdp", split_axis=1, concat_axis=1, tiled=True).reshape(
        SLOTS, width, slab
    )
    rotated, lroot_full = (
        lax.all_gather(arrived, "rep", axis=2, tiled=True),
        lax.all_gather(lroot_rows, "rep", axis=1, tiled=True),
    )
    restored = (
        jnp.einsum(
            "sigk,kj->sigj",
            rotated.reshape(SLOTS, width, width // GROUP, GROUP),
            signs,
            preferred_element_type=jnp.float32,
        )
        * norm_factor
    )
    gradient = restored.reshape(SLOTS, width, width).astype(jnp.bfloat16)
    rep_rank = lax.axis_index("rep")
    own_rows = lax.dynamic_slice_in_dim(gradient, rep_rank * slab, slab, axis=1)
    own_cols = lax.dynamic_slice_in_dim(gradient, rep_rank * slab, slab, axis=2)
    left_gram = jnp.einsum("sik,sjk->sij", own_rows, gradient, preferred_element_type=jnp.float32)
    right_gram = jnp.einsum("ski,skj->sij", own_cols, gradient, preferred_element_type=jnp.float32)
    left_new = stat_decay * left_stat[0] + (1 - stat_decay) * left_gram
    right_new = stat_decay * right_stat[0] + (1 - stat_decay) * right_gram
    middle = jnp.einsum(
        "sik,sck->sic", gradient, right_root[0], preferred_element_type=jnp.float32
    ).astype(jnp.bfloat16)
    direction = jnp.einsum(
        "sik,skc->sic", lroot_full, middle, preferred_element_type=jnp.float32
    ).astype(jnp.bfloat16)
    returned = lax.all_to_all(
        direction.reshape(SLOTS, fsdp_count, rows_fsdp, slab),
        "fsdp",
        split_axis=1,
        concat_axis=1,
        tiled=True,
    )
    picked = lax.dot_general(
        routing,
        returned.reshape(SLOTS * fsdp_count, rows_fsdp * slab),
        (((0,), (0,)), ((), ())),
        preferred_element_type=jnp.float32,
    )
    update = picked.astype(jnp.bfloat16).reshape(blocks_all, rows_fsdp, slab)
    return (left_new[None], right_new[None], update)


def solution(mesh):
    in_specs = (
        P("rep", None, "fsdp", None),
        P(),
        P("fsdp", None, "rep", None),
        P("fsdp", None, "rep", None),
        P("fsdp", None, "rep", None),
        P("fsdp", None, "rep", None),
    )
    out_specs = (P("fsdp", None, "rep", None), P("fsdp", None, "rep", None), P(None, "fsdp", "rep"))
    return jax.shard_map(
        on_device, mesh=mesh, in_specs=in_specs, out_specs=out_specs, check_vma=False
    )
```

profile of v0, /device:TPU:1, one launch (start us, length us, event | category | flops | bytes accessed | tf_op | source)
XLA Modules:
  0.0 263.9 jit_solution(17010525167286083771)
XLA Ops:
  7.2 0.0 copy-start
  7.2 0.0 reduce-scatter.2.cloned.1.call-start
  7.2 1.3 reshape_squeeze.3
  8.5 0.3 abs_reduce_fusion
  8.9 0.0 copy-start.3
  8.9 0.9 multiply_convert_fusion.1
  9.8 0.0 reduce-scatter.2.cloned.1.call-update
  9.8 0.0 all-gather.4.cloned.1.call-start
  9.9 0.0 copy-done.3
  9.9 0.2 convert_reduce_fusion
  10.1 58.4 %reduce-scatter.2.cloned.1.call-done = bf16[128,4,64]{0,2,1:T(8,128)(2,1)} async-done(((bf16[128,4,512]{0,2,1:T(8,128)(2,1)}), bf16[128,4,64]{0,2,1:T(8,128)(2,1)}) %reduce-scatter.2.cloned.1.call-update) | async-done | bytes 65552 | tf_op jit(solution)/shard_map/reduce_scatter | solution.py:42
  68.5 1.0 convolution_convert_fusion.2
  69.5 0.2 reshape.48
  69.7 0.1 copy.104
  69.8 0.2 reshape.49
  70.0 51.8 %all_to_all.10 = bf16[128,2,256]{2,1,0:T(2,128)(2,1)S(1)} all-to-all(bf16[128,2,256]{2,1,0:T(2,128)(2,1)S(1)} %reshape.49), channel_id=1, replica_groups=mesh['fsdp'=128,'rep'=8] {'fsdp'}, dimensions={0} | all-to-all | bytes 262144 | tf_op jit(solution)/shard_map/all_to_all | solution.py:54
  121.7 0.2 reshape.50
  121.9 0.1 copy.68
  122.0 0.8 copy.69
  122.9 0.0 all-gather.4.cloned.1.call-update
  122.9 0.0 all-gather.6.cloned.1.call-start
  122.9 0.7 all-gather.6.cloned.1.call-update
  123.6 26.8 %all-gather.4.cloned.1.call-done = bf16[2,512,512]{1,0,2:T(2,128)(2,1)} async-done(((bf16[2,512,64]{1,0,2:T(2,128)(2,1)}), bf16[2,512,512]{1,0,2:T(2,128)(2,1)}) %all-gather.4.cloned.1.call-update) | async-done | bytes 1048592 | tf_op jit(solution)/shard_map/all_gather | solution.py:58
  150.4 1.7 multiply_convert_fusion
  152.1 42.8 %all-gather.6.cloned.1.call-done = bf16[1,2,512,512]{3,2,1,0:T(8,128)(2,1)} async-done(((bf16[1,2,64,512]{3,2,1,0:T(8,128)(2,1)}), bf16[1,2,512,512]{3,2,1,0:T(8,128)(2,1)}) %all-gather.6.cloned.1.call-update) | async-done | bytes 1048592 | tf_op jit(solution)/shard_map/all_gather | solution.py:59
  194.8 0.0 copy-done
  194.8 1.8 fusion.4
  196.7 0.0 copy-start.1
  196.7 0.2 copy.76
  196.9 0.1 copy.105
  197.0 0.0 copy-start.2
  197.0 0.9 reshape.51
  197.9 26.7 %all-to-all-start.1 = ((bf16[128,2,256]{2,1,0:T(2,128)(2,1)}), bf16[128,2,256]{2,1,0:T(2,128)(2,1)S(1)}, u32[]{:S(2)}, u32[]{:S(2)}) async-start(bf16[128,2,256]{2,1,0:T(2,128)(2,1)} %reshape.51), calls=%async_computation.2 | async-start | bytes 262144 | tf_op jit(solution)/shard_map/all_to_all | solution.py:84
  224.6 0.0 copy-done.1
  224.6 1.2 fusion.1
  225.8 0.0 copy-done.2
  225.8 1.1 fusion.3
  226.9 29.1 %all-to-all-done.1 = bf16[128,2,256]{2,1,0:T(2,128)(2,1)S(1)} async-done(((bf16[128,2,256]{2,1,0:T(2,128)(2,1)}), bf16[128,2,256]{2,1,0:T(2,128)(2,1)S(1)}, u32[]{:S(2)}, u32[]{:S(2)}) %all-to-all-start.1) | async-done | bytes 131104 | tf_op jit(solution)/shard_map/all_to_all | solution.py:84
  256.0 0.2 reshape.52
  256.2 0.2 copy.78
  256.4 0.2 convolution_convert_fusion.3
  256.6 0.7 copy.79
  (3 shorter events, 0.0 us)
Async XLA Ops:
  7.2 187.7 %copy-start = (bf16[1,2,64,512]{3,2,1,0:T(8,128)(2,1)S(1)}, bf16[1,2,64,512]{3,2,1,0:T(8,128)(2,1)}, u32[]{:S(2)}) copy-start(bf16[1,2,64,512]{3,2,1,0:T(8,128)(2,1)} %param.11) | copy-start | bytes 393220
  7.2 61.3 %reduce-scatter.2.cloned.1.call-start = ((), (), s32[]{:S(2)}) async-start(), calls=%async_computation.3 | async-start | bytes 589824 | tf_op jit(solution)/shard_map/reduce_scatter | solution.py:42
  8.9 1.0 copy-start.3
  9.8 140.5 %all-gather.4.cloned.1.call-start = ((), (), s32[]{:S(2)}) async-start(), calls=%async_computation.4 | async-start | bytes 1179648 | tf_op jit(solution)/shard_map/all_gather | solution.py:58
  122.9 72.0 %all-gather.6.cloned.1.call-start = ((), (), s32[]{:S(2)}) async-start(), calls=%async_computation.5 | async-start | bytes 1179648 | tf_op jit(solution)/shard_map/all_gather | solution.py:59
  196.7 27.9 %copy-start.1 = (f32[1,2,64,512]{3,2,1,0:T(8,128)S(1)}, f32[1,2,64,512]{3,2,1,0:T(8,128)}, u32[]{:S(2)}) copy-start(f32[1,2,64,512]{3,2,1,0:T(8,128)} %param.9) | copy-start | bytes 786436
  197.0 28.8 %copy-start.2 = (f32[1,2,64,512]{3,2,1,0:T(8,128)S(1)}, f32[1,2,64,512]{3,2,1,0:T(8,128)}, u32[]{:S(2)}) copy-start(f32[1,2,64,512]{3,2,1,0:T(8,128)} %param.8) | copy-start | bytes 786436
  197.9 58.1 %all-to-all-start.1 = ((bf16[128,2,256]{2,1,0:T(2,128)(2,1)}), bf16[128,2,256]{2,1,0:T(2,128)(2,1)S(1)}, u32[]{:S(2)}, u32[]{:S(2)}) async-start(bf16[128,2,256]{2,1,0:T(2,128)(2,1)} %reshape.51), calls=%async_computation.2 | async-start | bytes 262144 | tf_op jit(solution)/shard_map/all_to_all | solution.py:84
Sparse Core Ops, SparseCore 0:
  11.4 57.0 reduce-scatter.1
  123.0 27.3 all-gather.3
  153.5 41.3 all-gather.5
where the time goes:
time: 264 us
  waiting for transfers between devices  158 us (60%)
  blocking collectives  51.8 us (20%)
  starting transfers between devices  26.9 us (10%)
  between operations  13.9 us (5%)
  matrix products  7.37 us (3%)
  local copies, waits for them, and re-layouts  5.16 us (2%)
    reduce_scatter x1, waiting for transfers between devices, on_device(): lax.psum_scatter(terms.astype(jnp.bfloat16), 'rep', scatter_dimension=2,...  58.4 us
    all_to_all x1, blocking collectives, on_device(): lax.all_to_all(outgoing, 'fsdp', split_axis=1, concat_axis=1, tiled=True)  51.8 us
    all_gather x1, waiting for transfers between devices, on_device(): lax.all_gather(lroot_rows, 'rep', axis=1, tiled=True)  42.8 us
    all_to_all x1, waiting for transfers between devices, on_device(): lax.all_to_all(direction.reshape(SLOTS, fsdp_count, rows_fsdp, slab), 'fs...  29.1 us
    all_gather x1, waiting for transfers between devices, on_device(): lax.all_gather(arrived, 'rep', axis=2, tiled=True)  26.8 us
    all_to_all x1, starting transfers between devices, on_device(): lax.all_to_all(direction.reshape(SLOTS, fsdp_count, rows_fsdp, slab), 'fs...  26.7 us
  transfers between devices with their start and end apart: 4, of which 4 were waited for; matrix products, arithmetic and copies ran while one was open for 2% of the time, Pallas kernels for 0%

commit v1 on v0

v1 whole, which is shorter than its diff:
```python
import jax
import jax.numpy as jnp
from jax import lax
from jax.sharding import PartitionSpec as P

GROUP = 128
SLOTS = 2
DECAY = 0.95


def hadamard(length):
    counter = jnp.arange(length, dtype=jnp.int32)
    correlation = counter[:, None] & counter[None, :]
    parity = jnp.zeros((length, length), jnp.int32)
    for bit_pos in range(length.bit_length() - 1):
        parity = parity ^ correlation >> bit_pos & 1
    return (1 - 2 * parity).astype(jnp.bfloat16)


def mm(a, b):
    return jnp.dot(a, b, preferred_element_type=jnp.float32)


def on_device(grads, owner, left_stat, right_stat, left_root, right_root):
    bf, f32, i32 = jnp.bfloat16, jnp.float32, jnp.int32
    signs = hadamard(GROUP)
    norm = GROUP ** (-0.5)
    x = grads[0]
    nb, rows, width = x.shape
    nf = lax.axis_size("fsdp")
    nrep = lax.axis_size("rep")
    groups = width // GROUP
    halves = nrep // groups
    per = rows // halves
    slab = width // nrep

    lroot = lax.all_gather(left_root[0], "rep", axis=1, tiled=True)

    turned = jnp.einsum("brgk,kj->brgj", x.reshape(nb, rows, groups, GROUP), signs,
                        preferred_element_type=f32) * norm
    peak = jnp.max(jnp.abs(turned), axis=-1) + 1e-06
    scales = lax.optimization_barrier(peak.astype(bf)).astype(f32)
    codes = (turned / scales[..., None]).astype(bf)
    terms = (codes.astype(f32) * scales[..., None]).astype(bf)
    send = terms.reshape(nb, halves, per, groups, GROUP).transpose(3, 1, 0, 2, 4)
    send = send.reshape(nrep, nb * per, GROUP)
    got = lax.all_to_all(send, "rep", split_axis=0, concat_axis=0, tiled=True)
    summed = jnp.sum(got.astype(f32), axis=0).astype(bf)

    counter = jnp.arange(nb, dtype=i32)
    same = owner[:, None] == owner[None, :]
    slot_of = jnp.sum(same & (counter[None, :] < counter[:, None]), axis=1)
    place = owner * SLOTS + slot_of
    out_row = jnp.arange(nf * SLOTS * per, dtype=i32)
    in_row = jnp.arange(nb * per, dtype=i32)
    key_in = jnp.repeat(place, per) * per + in_row % per
    route = (out_row[:, None] == key_in[None, :]).astype(bf)
    outgoing = mm(route, summed).astype(bf).reshape(nf, SLOTS * per, GROUP)
    arrived = lax.all_to_all(outgoing, "fsdp", split_axis=0, concat_axis=0, tiled=True)

    copies = jnp.broadcast_to(arrived.reshape(1, nf * SLOTS * per, GROUP), (nrep, nf * SLOTS * per, GROUP))
    whole = lax.all_to_all(copies, "rep", split_axis=0, concat_axis=0, tiled=True)
    whole = whole.reshape(groups, halves, nf, SLOTS, per, GROUP).transpose(3, 2, 1, 4, 0, 5)
    restored = jnp.einsum("sigk,kj->sigj", whole.reshape(SLOTS, width, groups, GROUP), signs,
                          preferred_element_type=f32) * norm
    gradient = restored.reshape(SLOTS, width, width).astype(bf)

    rank = lax.axis_index("rep")
    own_rows = lax.dynamic_slice_in_dim(gradient, rank * slab, slab, axis=1)
    own_cols = lax.dynamic_slice_in_dim(gradient, rank * slab, slab, axis=2)
    middle = jnp.einsum("sik,sck->sic", gradient, right_root[0], preferred_element_type=f32).astype(bf)
    direction = jnp.einsum("sik,skc->isc", lroot, middle, preferred_element_type=f32).astype(bf)
    packed = direction.reshape(nf, rows, SLOTS * slab)
    back = lax.all_to_all(packed, "fsdp", split_axis=0, concat_axis=0, tiled=True)

    left_gram = jnp.einsum("sik,sjk->sij", own_rows, gradient, preferred_element_type=f32)
    right_gram = jnp.einsum("ski,skj->sij", own_cols, gradient, preferred_element_type=f32)
    left_new = DECAY * left_stat[0] + (1 - DECAY) * left_gram
    right_new = DECAY * right_stat[0] + (1 - DECAY) * right_gram

    pick = (place[:, None] == jnp.arange(nf * SLOTS, dtype=i32)[None, :]).astype(bf).reshape(nb, nf, SLOTS)
    update = jnp.einsum("bfs,frsc->brc", pick, back.reshape(nf, rows, SLOTS, slab),
                        preferred_element_type=f32).astype(bf)
    return (left_new[None], right_new[None], update)


def solution(mesh):
    in_specs = (
        P("rep", None, "fsdp", None),
        P(),
        P("fsdp", None, "rep", None),
        P("fsdp", None, "rep", None),
        P("fsdp", None, "rep", None),
        P("fsdp", None, "rep", None),
    )
    out_specs = (P("fsdp", None, "rep", None), P("fsdp", None, "rep", None), P(None, "fsdp", "rep"))
    return jax.shard_map(on_device, mesh=mesh, in_specs=in_specs, out_specs=out_specs, check_vma=False)
```

time: 264 us -> 173 us (0.66)
  waiting for transfers between devices: 158 us -> 68.1 us
  blocking collectives: 51.8 us -> 21.4 us
  starting transfers between devices: 26.9 us -> 56.7 us
    all_gather x2 -> x1, waiting for transfers between devices: 69.5 us -> 0.02 us  [on_device(): lroot = lax.all_gather(left_root[0], 'rep', axis=1, tiled=True)]
    reduce_scatter x1 -> x0, waiting for transfers between devices: 58.4 us -> none  [on_device(): lax.psum_scatter(terms.astype(jnp.bfloat16), 'rep', scatter_dimension=2,...]
    all_to_all x1 -> x3, waiting for transfers between devices: 29.1 us -> 67.4 us  [the longest x1 29.4 us: on_device(): lax.all_to_all(outgoing, 'fsdp', split_axis=0, concat_axis=0, tiled=True)]
    all_to_all x1, blocking collectives: 51.8 us -> 21.4 us  [on_device(): lax.all_to_all(copies, 'rep', split_axis=0, concat_axis=0, tiled=True)]
    all_to_all x1 -> x3, starting transfers between devices: 26.7 us -> 56.7 us  [the longest x1 21.2 us: on_device(): lax.all_to_all(outgoing, 'fsdp', split_axis=0, concat_axis=0, tiled=True)]
  transfers between devices with their start and end apart: 4 -> 4, of which waited for: 4 -> 3; matrix products, arithmetic and copies ran while one was open for 2% -> 2% of each run, Pallas kernels for 0% -> 0%
where the time goes in v1:
time: 173 us
  waiting for transfers between devices  68.1 us (39%)
  starting transfers between devices  56.7 us (33%)
  blocking collectives  21.4 us (12%)
  between operations  14.2 us (8%)
  matrix products  6.94 us (4%)
  local copies, waits for them, and re-layouts  4.83 us (3%)
    all_to_all x1, waiting for transfers between devices, on_device(): lax.all_to_all(outgoing, 'fsdp', split_axis=0, concat_axis=0, tiled=True)  29.4 us
    all_to_all x1, waiting for transfers between devices, on_device(): lax.all_to_all(packed, 'fsdp', split_axis=0, concat_axis=0, tiled=True)  28.9 us
    all_to_all x1, blocking collectives, on_device(): lax.all_to_all(copies, 'rep', split_axis=0, concat_axis=0, tiled=True)  21.4 us
    all_to_all x1, starting transfers between devices, on_device(): lax.all_to_all(outgoing, 'fsdp', split_axis=0, concat_axis=0, tiled=True)  21.2 us
    all_to_all x1, starting transfers between devices, on_device(): lax.all_to_all(packed, 'fsdp', split_axis=0, concat_axis=0, tiled=True)  18 us
    all_to_all x1, starting transfers between devices, on_device(): got = lax.all_to_all(send, 'rep', split_axis=0, concat_axis=0, tiled=True)  17.5 us
    all_to_all x1, waiting for transfers between devices, on_device(): got = lax.all_to_all(send, 'rep', split_axis=0, concat_axis=0, tiled=True)  9.07 us
  transfers between devices with their start and end apart: 4, of which 3 were waited for; matrix products, arithmetic and copies ran while one was open for 2% of the time, Pallas kernels for 0%

profile of v1, /device:TPU:1, one launch (start us, length us, event | category | flops | bytes accessed | tf_op | source)
XLA Modules:
  0.0 172.8 jit_solution(12767594247813096231)
XLA Ops:
  7.2 0.0 copy-start
  7.2 1.3 reshape_squeeze.3
  8.5 0.6 abs_reduce_fusion
  9.1 0.3 multiply_convert_fusion.1
  9.4 0.0 copy-start.3
  9.4 1.3 copy.26
  10.8 17.5 %all-to-all-start = ((bf16[8,256,128]{2,1,0:T(8,128)(2,1)}), bf16[8,256,128]{2,1,0:T(8,128)(2,1)S(1)}, u32[]{:S(2)}, u32[]{:S(2)}) async-start(bf16[8,256,128]{2,1,0:T(8,128)(2,1)} %bitcast.4), calls=%async_computation | async-start | bytes 1048576 | tf_op jit(solution)/shard_map/all_to_all | solution.py:47
  28.3 0.0 copy-done.3
  28.3 0.2 convert_reduce_fusion
  28.5 0.1 broadcast_in_dim.10
  28.6 0.2 mul.71
  28.7 9.1 %all-to-all-done = bf16[8,256,128]{2,1,0:T(8,128)(2,1)S(1)} async-done(((bf16[8,256,128]{2,1,0:T(8,128)(2,1)}), bf16[8,256,128]{2,1,0:T(8,128)(2,1)S(1)}, u32[]{:S(2)}, u32[]{:S(2)}) %all-to-all-start) | async-done | bytes 524320 | tf_op jit(solution)/shard_map/all_to_all | solution.py:47
  37.8 0.1 reduce_sum.22
  37.9 0.9 convolution_convert_fusion.2
  38.8 21.2 %all-to-all-start.1 = ((bf16[128,4,128]{2,1,0:T(4,128)(2,1)}), bf16[128,4,128]{2,1,0:T(4,128)(2,1)S(1)}, u32[]{:S(2)}, u32[]{:S(2)}) async-start(bf16[128,4,128]{2,1,0:T(4,128)(2,1)} %bitcast.5), calls=%async_computation.1 | async-start | bytes 262144 | tf_op jit(solution)/shard_map/all_to_all | solution.py:59
  59.9 0.0 all-gather.3.cloned.1.call-start
  60.0 0.7 all-gather.3.cloned.1.call-update
  60.7 29.4 %all-to-all-done.1 = bf16[128,4,128]{2,1,0:T(4,128)(2,1)S(1)} async-done(((bf16[128,4,128]{2,1,0:T(4,128)(2,1)}), bf16[128,4,128]{2,1,0:T(4,128)(2,1)S(1)}, u32[]{:S(2)}, u32[]{:S(2)}) %all-to-all-start.1) | async-done | bytes 131104 | tf_op jit(solution)/shard_map/all_to_all | solution.py:59
  90.1 0.1 broadcast_in_dim.12
  90.3 21.4 %all_to_all.20 = bf16[8,512,128]{2,1,0:T(8,128)(2,1)S(1)} all-to-all(bf16[8,512,128]{2,1,0:T(8,128)(2,1)S(1)} %broadcast_in_dim.12), channel_id=1, replica_groups=mesh['fsdp'=128,'rep'=8] {'rep'}, dimensions={0} | all-to-all | bytes 2097152 | tf_op jit(solution)/shard_map/all_to_all | solution.py:62
  111.7 0.7 copy.27
  112.4 0.4 multiply_convert_fusion
  112.8 0.0 all-gather.3.cloned.1.call-done
  112.9 0.0 copy-done
  112.9 1.8 %fusion.4 = bf16[512,2,64]{0,2,1:T(8,128)(2,1)S(1)} fusion(bf16[2,512,512]{1,2,0:T(8,128)(2,1)S(1)} %bitcast.55, bf16[1,2,512,512]{3,2,1,0:T(8,128)(2,1)} %all-gather.3.cloned.1.call-done, bf16[1,2,64,512]{3,2,1,0:T(8,128)(2,1)S(1)} %copy-done), kind=kOutput, calls=%fused_computation.11 | convolution fusion | flops 134348800 | bytes 2359296 | tf_op jit(solution)/shard_map/sik,skc->isc/dot_general | solution.py:72
  114.7 0.0 copy-start.1
  114.7 0.2 copy.32
  114.9 0.0 copy-start.2
  114.9 0.8 reshape.80
  115.7 18.0 %all-to-all-start.3 = ((bf16[128,4,128]{2,1,0:T(4,128)(2,1)}), bf16[128,4,128]{2,1,0:T(4,128)(2,1)S(1)}, u32[]{:S(2)}, u32[]{:S(2)}) async-start(bf16[128,4,128]{2,1,0:T(4,128)(2,1)} %reshape.80), calls=%async_computation.3 | async-start | bytes 262144 | tf_op jit(solution)/shard_map/all_to_all | solution.py:74
  133.7 0.0 copy-done.1
  133.7 1.2 fusion.1
  134.9 0.0 copy-done.2
  134.9 1.1 fusion.3
  136.0 28.9 %all-to-all-done.3 = bf16[128,4,128]{2,1,0:T(4,128)(2,1)S(1)} async-done(((bf16[128,4,128]{2,1,0:T(4,128)(2,1)}), bf16[128,4,128]{2,1,0:T(4,128)(2,1)S(1)}, u32[]{:S(2)}, u32[]{:S(2)}) %all-to-all-start.3) | async-done | bytes 131104 | tf_op jit(solution)/shard_map/all_to_all | solution.py:74
  165.0 0.1 copy.33
  165.1 0.9 fusion.5
  (5 shorter events, 0.0 us)
Async XLA Ops:
  7.2 105.7 %copy-start = (bf16[1,2,64,512]{3,2,1,0:T(8,128)(2,1)S(1)}, bf16[1,2,64,512]{3,2,1,0:T(8,128)(2,1)}, u32[]{:S(2)}) copy-start(bf16[1,2,64,512]{3,2,1,0:T(8,128)(2,1)} %param.11) | copy-start | bytes 393220
  9.4 18.9 %copy-start.3 = (s32[128]{0:T(128)S(1)}, s32[128]{0:T(128)}, u32[]{:S(2)}) copy-start(s32[128]{0:T(128)} %param.7) | copy-start | bytes 1540
  10.8 27.0 %all-to-all-start = ((bf16[8,256,128]{2,1,0:T(8,128)(2,1)}), bf16[8,256,128]{2,1,0:T(8,128)(2,1)S(1)}, u32[]{:S(2)}, u32[]{:S(2)}) async-start(bf16[8,256,128]{2,1,0:T(8,128)(2,1)} %bitcast.4), calls=%async_computation | async-start | bytes 1048576 | tf_op jit(solution)/shard_map/all_to_all | solution.py:47
  38.8 51.3 %all-to-all-start.1 = ((bf16[128,4,128]{2,1,0:T(4,128)(2,1)}), bf16[128,4,128]{2,1,0:T(4,128)(2,1)S(1)}, u32[]{:S(2)}, u32[]{:S(2)}) async-start(bf16[128,4,128]{2,1,0:T(4,128)(2,1)} %bitcast.5), calls=%async_computation.1 | async-start | bytes 262144 | tf_op jit(solution)/shard_map/all_to_all | solution.py:59
  59.9 52.9 %all-gather.3.cloned.1.call-start = ((), (), s32[]{:S(2)}) async-start(), calls=%async_computation.4 | async-start | bytes 1179648 | tf_op jit(solution)/shard_map/all_gather | solution.py:37
  114.7 19.0 %copy-start.1 = (f32[1,2,64,512]{3,2,1,0:T(8,128)S(1)}, f32[1,2,64,512]{3,2,1,0:T(8,128)}, u32[]{:S(2)}) copy-start(f32[1,2,64,512]{3,2,1,0:T(8,128)} %param.9) | copy-start | bytes 786436
  114.9 20.0 %copy-start.2 = (f32[1,2,64,512]{3,2,1,0:T(8,128)S(1)}, f32[1,2,64,512]{3,2,1,0:T(8,128)}, u32[]{:S(2)}) copy-start(f32[1,2,64,512]{3,2,1,0:T(8,128)} %param.8) | copy-start | bytes 786436
  115.7 49.2 %all-to-all-start.3 = ((bf16[128,4,128]{2,1,0:T(4,128)(2,1)}), bf16[128,4,128]{2,1,0:T(4,128)(2,1)S(1)}, u32[]{:S(2)}, u32[]{:S(2)}) async-start(bf16[128,4,128]{2,1,0:T(4,128)(2,1)} %reshape.80), calls=%async_computation.3 | async-start | bytes 262144 | tf_op jit(solution)/shard_map/all_to_all | solution.py:74
Sparse Core Ops, SparseCore 0:
  63.5 42.7 all-gather.2

commit v2 on v1

--- a/solution.py
+++ b/solution.py
@@ -34,8 +34,6 @@
     per = rows // halves
     slab = width // nrep
 
-    lroot = lax.all_gather(left_root[0], "rep", axis=1, tiled=True)
-
     turned = jnp.einsum("brgk,kj->brgj", x.reshape(nb, rows, groups, GROUP), signs,
                         preferred_element_type=f32) * norm
     peak = jnp.max(jnp.abs(turned), axis=-1) + 1e-06
@@ -56,16 +54,25 @@
     key_in = jnp.repeat(place, per) * per + in_row % per
     route = (out_row[:, None] == key_in[None, :]).astype(bf)
     outgoing = mm(route, summed).astype(bf).reshape(nf, SLOTS * per, GROUP)
+    outgoing, lroot_rows = lax.optimization_barrier((outgoing, left_root[0]))
+    lroot_flat = lroot_rows.reshape(1, SLOTS * slab * groups, GROUP)
+    lroot_copies = jnp.broadcast_to(lroot_flat, (nrep, SLOTS * slab * groups, GROUP))
     arrived = lax.all_to_all(outgoing, "fsdp", split_axis=0, concat_axis=0, tiled=True)
+    lroot = lax.all_to_all(lroot_copies, "rep", split_axis=0, concat_axis=0, tiled=True)
+    lroot = lroot.reshape(nrep, SLOTS, slab, width).transpose(1, 0, 2, 3).reshape(SLOTS, width, width)
 
-    copies = jnp.broadcast_to(arrived.reshape(1, nf * SLOTS * per, GROUP), (nrep, nf * SLOTS * per, GROUP))
-    whole = lax.all_to_all(copies, "rep", split_axis=0, concat_axis=0, tiled=True)
+    chip_mates = [[h + halves * g for g in range(groups)] for h in range(halves)]
+    copies = jnp.broadcast_to(arrived.reshape(1, nf * SLOTS * per, GROUP), (groups, nf * SLOTS * per, GROUP))
+    mine = lax.all_to_all(copies, "rep", split_axis=0, concat_axis=0, axis_index_groups=chip_mates, tiled=True)
+    other = lax.ppermute(mine, "rep", [(j, j + 1 - 2 * (j % 2)) for j in range(nrep)])
+    rank = lax.axis_index("rep")
+    first = rank % halves == 0
+    whole = jnp.stack([jnp.where(first, mine, other), jnp.where(first, other, mine)], axis=1)
     whole = whole.reshape(groups, halves, nf, SLOTS, per, GROUP).transpose(3, 2, 1, 4, 0, 5)
     restored = jnp.einsum("sigk,kj->sigj", whole.reshape(SLOTS, width, groups, GROUP), signs,
                           preferred_element_type=f32) * norm
     gradient = restored.reshape(SLOTS, width, width).astype(bf)
 
-    rank = lax.axis_index("rep")
     own_rows = lax.dynamic_slice_in_dim(gradient, rank * slab, slab, axis=1)
     own_cols = lax.dynamic_slice_in_dim(gradient, rank * slab, slab, axis=2)
     middle = jnp.einsum("sik,sck->sic", gradient, right_root[0], preferred_element_type=f32).astype(bf)

time: 173 us -> 164 us (0.948)
  blocking collectives: 21.4 us -> 50.9 us
  starting transfers between devices: 56.7 us -> 38.1 us
  between operations: 14.2 us -> 0.86 us
  waiting for transfers between devices: 68.1 us -> 56.9 us
  other arithmetic: 0.62 us -> 3.37 us
  local copies, waits for them, and re-layouts: 4.83 us -> 7.51 us
  matrix products: 6.94 us -> 5.06 us
    all_to_all x1, blocking collectives: 21.4 us -> 50.9 us  [on_device(): lax.all_to_all(outgoing, 'fsdp', split_axis=0, concat_axis=0, tiled=True)]
    all_to_all x1, starting transfers between devices: 18 us -> 6.3 us  [on_device(): lax.all_to_all(packed, 'fsdp', split_axis=0, concat_axis=0, tiled=True)]
    all_to_all x1 -> x2, waiting for transfers between devices: 29.4 us -> 20 us  [the longest x1 13.1 us: on_device(): lax.all_to_all(lroot_copies, 'rep', split_axis=0, concat_axis=0, tiled=True)]
    all_to_all x1 -> x2, starting transfers between devices: 21.2 us -> 12.2 us  [the longest x1 8.1 us: on_device(): lax.all_to_all(lroot_copies, 'rep', split_axis=0, concat_axis=0, tiled=True)]
    ppermute x0 -> x1, starting transfers between devices: none -> 2.02 us  [on_device(): lax.ppermute(mine, 'rep', [(j, j + 1 - 2 * (j % 2)) for j in range(nrep)])]
    broadcast_in_dim x1 -> x3, local copies, waits for them, and re-layouts: 0.14 us -> 2.06 us  [the longest x2 1.19 us: on_device(): jnp.broadcast_to(lroot_flat, (nrep, SLOTS * slab * groups, GROUP))]
  transfers between devices with their start and end apart: 4 -> 5, of which waited for: 3 -> 4; matrix products, arithmetic and copies ran while one was open for 2% -> 2% of each run, Pallas kernels for 0% -> 0%
where the time goes in v2:
time: 164 us; the launch traced here: 163 us
  waiting for transfers between devices  56.9 us (35%)
  blocking collectives  50.9 us (31%)
  starting transfers between devices  38.1 us (23%)
  local copies, waits for them, and re-layouts  7.51 us (5%)
  matrix products  5.06 us (3%)
  other arithmetic  3.37 us (2%)
    all_to_all x1, blocking collectives, on_device(): lax.all_to_all(outgoing, 'fsdp', split_axis=0, concat_axis=0, tiled=True)  50.9 us
    all_to_all x1, waiting for transfers between devices, on_device(): lax.all_to_all(packed, 'fsdp', split_axis=0, concat_axis=0, tiled=True)  27.8 us
    all_to_all x1, starting transfers between devices, on_device(): got = lax.all_to_all(send, 'rep', split_axis=0, concat_axis=0, tiled=True)  17.5 us
    all_to_all x1, waiting for transfers between devices, on_device(): lax.all_to_all(lroot_copies, 'rep', split_axis=0, concat_axis=0, tiled=True)  13.1 us
    all_to_all x1, waiting for transfers between devices, on_device(): got = lax.all_to_all(send, 'rep', split_axis=0, concat_axis=0, tiled=True)  9.07 us
    all_to_all x1, starting transfers between devices, on_device(): lax.all_to_all(lroot_copies, 'rep', split_axis=0, concat_axis=0, tiled=True)  8.1 us
    all_to_all x1, waiting for transfers between devices, on_device(): lax.all_to_all(copies, 'rep', split_axis=0, concat_axis=0, axis_index_gro...  6.89 us
    all_to_all x1, starting transfers between devices, on_device(): lax.all_to_all(packed, 'fsdp', split_axis=0, concat_axis=0, tiled=True)  6.3 us
  transfers between devices with their start and end apart: 5, of which 4 were waited for; matrix products, arithmetic and copies ran while one was open for 2% of the time, Pallas kernels for 0%

profile of v2, /device:TPU:1, one launch (start us, length us, event | category | flops | bytes accessed | tf_op | source)
XLA Modules:
  0.0 162.7 jit_solution(7507757132216848301)
XLA Ops:
  0.6 0.0 copy-start
  0.6 1.3 reshape_squeeze.3
  1.9 0.6 abs_reduce_fusion
  2.5 0.3 multiply_convert_fusion.1
  2.9 0.0 copy-start.4
  2.9 1.3 copy.27
  4.2 17.5 %all-to-all-start = ((bf16[8,256,128]{2,1,0:T(8,128)(2,1)}), bf16[8,256,128]{2,1,0:T(8,128)(2,1)S(1)}, u32[]{:S(2)}, u32[]{:S(2)}) async-start(bf16[8,256,128]{2,1,0:T(8,128)(2,1)} %bitcast.4), calls=%async_computation | async-start | bytes 1048576 | tf_op jit(solution)/shard_map/all_to_all | solution.py:45
  21.8 0.0 copy-done.4
  21.8 0.2 convert_reduce_fusion
  22.0 0.1 broadcast_in_dim.14
  22.0 0.2 mul.71
  22.2 9.1 %all-to-all-done = bf16[8,256,128]{2,1,0:T(8,128)(2,1)S(1)} async-done(((bf16[8,256,128]{2,1,0:T(8,128)(2,1)}), bf16[8,256,128]{2,1,0:T(8,128)(2,1)S(1)}, u32[]{:S(2)}, u32[]{:S(2)}) %all-to-all-start) | async-done | bytes 524320 | tf_op jit(solution)/shard_map/all_to_all | solution.py:45
  31.3 0.1 reduce_sum.22
  31.4 0.0 copy-start.3
  31.4 0.2 convolution_convert_fusion.2
  31.6 50.9 %all_to_all.25 = bf16[128,4,128]{2,1,0:T(4,128)(2,1)S(1)} all-to-all(bf16[128,4,128]{2,1,0:T(4,128)(2,1)S(1)} %bitcast.69), channel_id=1, replica_groups=mesh['fsdp'=128,'rep'=8] {'fsdp'}, dimensions={0} | all-to-all | bytes 262144 | tf_op jit(solution)/shard_map/all_to_all | solution.py:60
  82.6 0.9 broadcast_in_dim.16
  83.4 4.1 %all-to-all-start.2 = ((bf16[4,512,128]{2,1,0:T(8,128)(2,1)}), bf16[4,512,128]{2,1,0:T(8,128)(2,1)}, u32[]{:S(2)}, u32[]{:S(2)}) async-start(bf16[4,512,128]{2,1,0:T(8,128)(2,1)} %broadcast_in_dim.16), calls=%async_computation.2 | async-start | bytes 1048576 | tf_op jit(solution)/shard_map/all_to_all | solution.py:66
  87.6 0.0 copy-done.3
  87.6 0.1 broadcast_in_dim.19
  87.7 6.9 %all-to-all-done.2 = bf16[4,512,128]{2,1,0:T(8,128)(2,1)} async-done(((bf16[4,512,128]{2,1,0:T(8,128)(2,1)}), bf16[4,512,128]{2,1,0:T(8,128)(2,1)}, u32[]{:S(2)}, u32[]{:S(2)}) %all-to-all-start.2) | async-done | bytes 524320 | tf_op jit(solution)/shard_map/all_to_all | solution.py:66
  94.6 1.1 broadcast_in_dim.20
  95.7 8.1 %all-to-all-start.3 = ((bf16[8,512,128]{2,1,0:T(8,128)(2,1)}), bf16[8,512,128]{2,1,0:T(8,128)(2,1)S(1)}, u32[]{:S(2)}, u32[]{:S(2)}) async-start(bf16[8,512,128]{2,1,0:T(8,128)(2,1)} %broadcast_in_dim.20), calls=%async_computation.3 | async-start | bytes 2097152 | tf_op jit(solution)/shard_map/all_to_all | solution.py:61
  103.8 2.0 %collective-permute-start = (bf16[4,512,128]{2,1,0:T(8,128)(2,1)}, bf16[4,512,128]{2,1,0:T(8,128)(2,1)}, u32[]{:S(2)}, u32[]{:S(2)}) collective-permute-start(bf16[4,512,128]{2,1,0:T(8,128)(2,1)} %all-to-all-done.2), channel_id=1, source_target_pairs={{0,1},{1,0},{2,3},{3,2},{4,5},{5,4},{6,7},{7,6},{8,9},{9,8},{10,11... | collective-permute-start | bytes 1572872 | tf_op jit(solution)/shard_map/ppermute | solution.py:67
  105.8 13.1 %all-to-all-done.3 = bf16[8,512,128]{2,1,0:T(8,128)(2,1)S(1)} async-done(((bf16[8,512,128]{2,1,0:T(8,128)(2,1)}), bf16[8,512,128]{2,1,0:T(8,128)(2,1)S(1)}, u32[]{:S(2)}, u32[]{:S(2)}) %all-to-all-start.3) | async-done | bytes 1048608 | tf_op jit(solution)/shard_map/all_to_all | solution.py:61
  118.9 0.6 reshape.89
  119.6 0.1 copy.33
  119.7 0.0 collective-permute-done
  119.7 1.3 broadcast_select_fusion.1
  120.9 1.5 maximum_bitcast_fusion
  122.4 0.7 copy.28
  123.2 0.4 multiply_convert_fusion
  123.6 0.0 copy-done
  123.6 0.6 fusion.4
  124.2 0.0 copy-start.1
  124.2 0.2 copy.34
  124.4 0.0 copy-start.2
  124.4 0.8 reshape.91
  125.2 6.3 %all-to-all-start.4 = ((bf16[128,4,128]{2,1,0:T(4,128)(2,1)}), bf16[128,4,128]{2,1,0:T(4,128)(2,1)S(1)}, u32[]{:S(2)}, u32[]{:S(2)}) async-start(bf16[128,4,128]{2,1,0:T(4,128)(2,1)} %reshape.91), calls=%async_computation.4 | async-start | bytes 262144 | tf_op jit(solution)/shard_map/all_to_all | solution.py:81
  131.6 0.0 copy-done.1
  131.6 1.2 fusion.1
  132.7 0.0 copy-done.2
  132.7 1.1 fusion.3
  133.9 27.8 %all-to-all-done.4 = bf16[128,4,128]{2,1,0:T(4,128)(2,1)S(1)} async-done(((bf16[128,4,128]{2,1,0:T(4,128)(2,1)}), bf16[128,4,128]{2,1,0:T(4,128)(2,1)S(1)}, u32[]{:S(2)}, u32[]{:S(2)}) %all-to-all-start.4) | async-done | bytes 131104 | tf_op jit(solution)/shard_map/all_to_all | solution.py:81
  161.7 0.1 copy.35
  161.8 0.9 fusion.5
  (5 shorter events, 0.0 us)
Async XLA Ops:
  0.6 123.0 %copy-start = (bf16[1,2,64,512]{3,2,1,0:T(8,128)(2,1)S(1)}, bf16[1,2,64,512]{3,2,1,0:T(8,128)(2,1)}, u32[]{:S(2)}) copy-start(bf16[1,2,64,512]{3,2,1,0:T(8,128)(2,1)} %param.11) | copy-start | bytes 393220
  2.9 18.9 %copy-start.4 = (s32[128]{0:T(128)S(1)}, s32[128]{0:T(128)}, u32[]{:S(2)}) copy-start(s32[128]{0:T(128)} %param.7) | copy-start | bytes 1540
  4.2 27.0 %all-to-all-start = ((bf16[8,256,128]{2,1,0:T(8,128)(2,1)}), bf16[8,256,128]{2,1,0:T(8,128)(2,1)S(1)}, u32[]{:S(2)}, u32[]{:S(2)}) async-start(bf16[8,256,128]{2,1,0:T(8,128)(2,1)} %bitcast.4), calls=%async_computation | async-start | bytes 1048576 | tf_op jit(solution)/shard_map/all_to_all | solution.py:45
  31.4 56.2 %copy-start.3 = (bf16[1,2,64,512]{3,2,1,0:T(8,128)(2,1)S(1)}, bf16[1,2,64,512]{3,2,1,0:T(8,128)(2,1)}, u32[]{:S(2)}) copy-start(bf16[1,2,64,512]{3,2,1,0:T(8,128)(2,1)} %param.10) | copy-start | bytes 393220
  83.4 11.1 %all-to-all-start.2 = ((bf16[4,512,128]{2,1,0:T(8,128)(2,1)}), bf16[4,512,128]{2,1,0:T(8,128)(2,1)}, u32[]{:S(2)}, u32[]{:S(2)}) async-start(bf16[4,512,128]{2,1,0:T(8,128)(2,1)} %broadcast_in_dim.16), calls=%async_computation.2 | async-start | bytes 1048576 | tf_op jit(solution)/shard_map/all_to_all | solution.py:66
  95.7 23.2 %all-to-all-start.3 = ((bf16[8,512,128]{2,1,0:T(8,128)(2,1)}), bf16[8,512,128]{2,1,0:T(8,128)(2,1)S(1)}, u32[]{:S(2)}, u32[]{:S(2)}) async-start(bf16[8,512,128]{2,1,0:T(8,128)(2,1)} %broadcast_in_dim.20), calls=%async_computation.3 | async-start | bytes 2097152 | tf_op jit(solution)/shard_map/all_to_all | solution.py:61
  103.8 15.9 %collective-permute-start = (bf16[4,512,128]{2,1,0:T(8,128)(2,1)}, bf16[4,512,128]{2,1,0:T(8,128)(2,1)}, u32[]{:S(2)}, u32[]{:S(2)}) collective-permute-start(bf16[4,512,128]{2,1,0:T(8,128)(2,1)} %all-to-all-done.2), channel_id=1, source_target_pairs={{0,1},{1,0},{2,3},{3,2},{4,5},{5,4},{6,7},{7,6},{8,9},{9,8},{10,11... | collective-permute-start | bytes 1572872 | tf_op jit(solution)/shard_map/ppermute | solution.py:67
  124.2 7.3 %copy-start.1 = (f32[1,2,64,512]{3,2,1,0:T(8,128)S(1)}, f32[1,2,64,512]{3,2,1,0:T(8,128)}, u32[]{:S(2)}) copy-start(f32[1,2,64,512]{3,2,1,0:T(8,128)} %param.9) | copy-start | bytes 786436
  124.4 8.3 %copy-start.2 = (f32[1,2,64,512]{3,2,1,0:T(8,128)S(1)}, f32[1,2,64,512]{3,2,1,0:T(8,128)}, u32[]{:S(2)}) copy-start(f32[1,2,64,512]{3,2,1,0:T(8,128)} %param.8) | copy-start | bytes 786436
  125.2 36.5 %all-to-all-start.4 = ((bf16[128,4,128]{2,1,0:T(4,128)(2,1)}), bf16[128,4,128]{2,1,0:T(4,128)(2,1)S(1)}, u32[]{:S(2)}, u32[]{:S(2)}) async-start(bf16[128,4,128]{2,1,0:T(4,128)(2,1)} %reshape.91), calls=%async_computation.4 | async-start | bytes 262144 | tf_op jit(solution)/shard_map/all_to_all | solution.py:81

commit v3 on v1

v3 whole, which is shorter than its diff:
```python
import jax
import jax.numpy as jnp
from jax import lax
from jax.experimental import pallas as pl
from jax.experimental.pallas import tpu as pltpu
from jax.sharding import PartitionSpec as P

GROUP = 128
SLOTS = 2
DECAY = 0.95
NORM = GROUP ** (-0.5)
BF, F32, I32 = jnp.bfloat16, jnp.float32, jnp.int32
VMEM_BYTES = 48 * 1024 * 1024


def hadamard():
    i = lax.broadcasted_iota(I32, (GROUP, GROUP), 0)
    j = lax.broadcasted_iota(I32, (GROUP, GROUP), 1)
    bits = i & j
    parity = jnp.zeros((GROUP, GROUP), I32)
    for k in range(GROUP.bit_length() - 1):
        parity = parity ^ ((bits >> k) & 1)
    return (1 - 2 * parity).astype(F32).astype(BF)


def mm(a, b):
    return jnp.dot(a, b, preferred_element_type=F32)


def mm_t(a, b):
    return lax.dot_general(a, b, (((1,), (1,)), ((), ())), preferred_element_type=F32)


def code_kernel(x_ref, out_ref):
    blocks, rows, width = x_ref.shape
    nrep, _, _ = out_ref.shape
    groups = width // GROUP
    halves = nrep // groups
    per = rows // halves
    signs = hadamard()
    step = 256 // rows
    o = lax.broadcasted_iota(I32, (256, 256), 0)
    i = lax.broadcasted_iota(I32, (256, 256), 1)
    perm = ((i // rows == o % step) & (i % rows == o // step)).astype(F32).astype(BF)
    for t in range(blocks // step):
        x = x_ref[t * step:(t + 1) * step].reshape(256, width)
        x = mm(perm, x).astype(BF)
        for g in range(groups):
            turned = mm(x[:, g * GROUP:(g + 1) * GROUP], signs) * NORM
            peak = jnp.max(jnp.abs(turned), axis=1, keepdims=True) + 1e-06
            scale = peak.astype(BF).astype(F32)
            codes = (turned / scale).astype(BF).astype(F32)
            terms = (codes * scale).astype(BF)
            for h in range(halves):
                for r in range(per):
                    row = (h * per + r) * step
                    out_ref[g * halves + h, r * blocks + t * step:r * blocks + (t + 1) * step, :] = (
                        terms[row:row + step])


def root_kernel(rank_ref, mine_ref, other_ref, rroot_ref, *refs):
    *hop_refs, grad_ref, out_ref = refs
    groups, _, _ = mine_ref.shape
    slots, width, _ = grad_ref.shape
    slab = rroot_ref.shape[1]
    rank = rank_ref[0]
    core = rank % 2
    chip = rank // 2
    signs = hadamard()
    o = lax.broadcasted_iota(I32, (256, 256), 0)
    i = lax.broadcasted_iota(I32, (256, 256), 1)
    half = jnp.where(i < 128, core, 1 - core)
    from_row = ((i % 128) // 4) * 4 + half * 2 + i % 2
    perm = ((o % 128 == from_row) & (o // 128 == (i // 2) % 2)).astype(F32).astype(BF)
    for t in range(width // 128):
        rows = slice(t * 128, (t + 1) * 128)
        for g in range(groups):
            both = jnp.concatenate([mine_ref[g, rows, :], other_ref[g, rows, :]], axis=0)
            placed = mm(perm, both).astype(BF)
            block = (mm(placed, signs) * NORM).astype(BF)
            for s in range(slots):
                grad_ref[s, rows, g * GROUP:(g + 1) * GROUP] = block[s * 128:(s + 1) * 128]
    for s in range(slots):
        middle = mm_t(grad_ref[s], rroot_ref[s]).astype(BF)
        for d, hop_ref in enumerate(hop_refs):
            from_chip = (chip + groups - d) % groups
            left = hop_ref[:, s * slab:(s + 1) * slab, :].reshape(2 * slab, width)
            rows = mm(left, middle).astype(BF)
            for k in range(2):
                start = pl.multiple_of((from_chip * 2 + (core + k) % 2) * slab, slab)
                out_ref[pl.ds(start, slab), s * slab:(s + 1) * slab] = rows[k * slab:(k + 1) * slab]


def kernel_params():
    return pltpu.CompilerParams(vmem_limit_bytes=VMEM_BYTES)


def in_vmem():
    return pl.BlockSpec(memory_space=pltpu.VMEM)


def code_call(x, nrep):
    nb, rows, width = x.shape
    per = rows * width // GROUP // nrep
    return pl.pallas_call(
        code_kernel,
        out_shape=jax.ShapeDtypeStruct((nrep, nb * per, GROUP), BF),
        in_specs=[in_vmem()],
        out_specs=in_vmem(),
        compiler_params=kernel_params(),
    )(x)


def root_call(rank, mine, other, hops, rroot):
    slots, slab, width = rroot.shape
    return pl.pallas_call(
        root_kernel,
        out_shape=(jax.ShapeDtypeStruct((slots, width, width), BF),
                   jax.ShapeDtypeStruct((width, slots * slab), BF)),
        in_specs=[pl.BlockSpec(memory_space=pltpu.SMEM)] + [in_vmem()] * (3 + len(hops)),
        out_specs=(in_vmem(), in_vmem()),
        compiler_params=kernel_params(),
    )(rank, mine, other, rroot, *hops)


def on_device(grads, owner, left_stat, right_stat, left_root, right_root):
    x = grads[0]
    nb, rows, width = x.shape
    nf = lax.axis_size("fsdp")
    nrep = lax.axis_size("rep")
    groups = width // GROUP
    halves = nrep // groups
    per = rows // halves
    slab = width // nrep
    part = nf * SLOTS * per
    rank = lax.axis_index("rep")

    got = lax.all_to_all(code_call(x, nrep), "rep", split_axis=0, concat_axis=0, tiled=True)
    summed = jnp.sum(got.astype(F32), axis=0).astype(BF)

    counter = jnp.arange(nb, dtype=I32)
    same = owner[:, None] == owner[None, :]
    slot_of = jnp.sum(same & (counter[None, :] < counter[:, None]), axis=1)
    place = owner * SLOTS + slot_of
    key_in = jnp.concatenate([place * per + r for r in range(per)])
    route = (jnp.arange(part, dtype=I32)[:, None] == key_in[None, :]).astype(BF)
    outgoing = mm(route, summed).astype(BF).reshape(nf, SLOTS * per, GROUP)

    outgoing, lroot_rows = lax.optimization_barrier((outgoing, left_root[0]))
    arrived = lax.all_to_all(outgoing, "fsdp", split_axis=0, concat_axis=0, tiled=True)
    own = lroot_rows.reshape(SLOTS * slab, width)
    swap = [(j, j + 1 - 2 * (j % 2)) for j in range(nrep)]
    pair = jnp.stack([own, lax.ppermute(own, "rep", swap)])
    hops = [pair]
    for d in range(1, groups):
        hops.append(lax.ppermute(pair, "rep", [(j, (j + halves * d) % nrep) for j in range(nrep)]))
    arrived, hops = lax.optimization_barrier((arrived, hops))

    chip_mates = [[h + halves * g for g in range(groups)] for h in range(halves)]
    copies = jnp.broadcast_to(arrived.reshape(1, part, GROUP), (groups, part, GROUP))
    mine = lax.all_to_all(copies, "rep", split_axis=0, concat_axis=0, axis_index_groups=chip_mates, tiled=True)
    other = lax.ppermute(mine, "rep", swap)
    gradient, direction = root_call(rank.reshape(1), mine, other, hops, right_root[0])
    packed = direction.reshape(nf, rows, SLOTS * slab)
    back = lax.all_to_all(packed, "fsdp", split_axis=0, concat_axis=0, tiled=True)

    own_rows = lax.dynamic_slice_in_dim(gradient, rank * slab, slab, axis=1)
    own_cols = lax.dynamic_slice_in_dim(gradient, rank * slab, slab, axis=2)
    left_gram = jnp.einsum("sik,sjk->sij", own_rows, gradient, preferred_element_type=F32)
    right_gram = jnp.einsum("ski,skj->sij", own_cols, gradient, preferred_element_type=F32)
    left_new = DECAY * left_stat[0] + (1 - DECAY) * left_gram
    right_new = DECAY * right_stat[0] + (1 - DECAY) * right_gram

    pick = (place[:, None] == jnp.arange(nf * SLOTS, dtype=I32)[None, :]).astype(BF).reshape(nb, nf, SLOTS)
    update = jnp.einsum("bfs,frsc->brc", pick, back.reshape(nf, rows, SLOTS, slab),
                        preferred_element_type=F32).astype(BF)
    return (left_new[None], right_new[None], update)


def solution(mesh):
    in_specs = (
        P("rep", None, "fsdp", None),
        P(),
        P("fsdp", None, "rep", None),
        P("fsdp", None, "rep", None),
        P("fsdp", None, "rep", None),
        P("fsdp", None, "rep", None),
    )
    out_specs = (P("fsdp", None, "rep", None), P("fsdp", None, "rep", None), P(None, "fsdp", "rep"))
    return jax.shard_map(on_device, mesh=mesh, in_specs=in_specs, out_specs=out_specs, check_vma=False)
```

time: 173 us -> 157 us (0.908)
  starting transfers between devices: 56.7 us -> 75.9 us
  between operations: 14.2 us -> 0.79 us
  blocking collectives: 21.4 us -> 9.46 us
  waiting for transfers between devices: 68.1 us -> 57.8 us
  Pallas kernels: 0 us -> 6.35 us
  local copies, waits for them, and re-layouts: 4.83 us -> 1.26 us
  matrix products: 6.94 us -> 4.09 us
    all_to_all x1, waiting for transfers between devices: 29.4 us -> 7.64 us  [on_device(): lax.all_to_all(outgoing, 'fsdp', split_axis=0, concat_axis=0, tiled=True)]
    ppermute x0 -> x5, starting transfers between devices: none -> 17.8 us  [the longest x3 8.42 us: on_device(): lax.ppermute(pair, 'rep', [(j, (j + halves * d) % nrep) for j in range(nr...]
    ppermute x0 -> x5, waiting for transfers between devices: none -> 12.5 us  [the longest x3 10 us: on_device(): lax.ppermute(pair, 'rep', [(j, (j + halves * d) % nrep) for j in range(nr...]
    all_to_all x1, blocking collectives: 21.4 us -> 9.46 us  [on_device(): lax.all_to_all(copies, 'rep', split_axis=0, concat_axis=0, axis_index_gro...]
    pallas_call x0 -> x2, Pallas kernels: none -> 6.35 us  [the longest x1 4.75 us: root_call(): pl.pallas_call(root_kernel, out_shape=(jax.ShapeDtypeStruct((slots, width...]
    dot_general x6 -> x3, matrix products: 6.04 us -> 3.19 us  [the longest x1 1.15 us: on_device(): jnp.einsum('ski,skj->sij', own_cols, gradient, preferred_element_type=F32)]
    reshape x2 -> x0, local copies, waits for them, and re-layouts: 2.14 us -> none  [the longest x1 1.33 us: on_device(): terms.reshape(nb, halves, per, groups, GROUP).transpose(3, 1, 0, 2, 4)]
  transfers between devices with their start and end apart: 4 -> 8, of which waited for: 3 -> 8; matrix products, arithmetic and copies ran while one was open for 2% -> 2% of each run, Pallas kernels for 0% -> 0%
where the time goes in v3:
time: 157 us; the launch traced here: 156 us
  starting transfers between devices  75.9 us (48%)
  waiting for transfers between devices  57.8 us (37%)
  blocking collectives  9.46 us (6%)
  Pallas kernels  6.35 us (4%)
  matrix products  4.09 us (3%)
    all_to_all x1, waiting for transfers between devices, on_device(): lax.all_to_all(packed, 'fsdp', split_axis=0, concat_axis=0, tiled=True)  28.4 us
    all_to_all x1, starting transfers between devices, on_device(): lax.all_to_all(outgoing, 'fsdp', split_axis=0, concat_axis=0, tiled=True)  21.3 us
    all_to_all x1, starting transfers between devices, on_device(): lax.all_to_all(packed, 'fsdp', split_axis=0, concat_axis=0, tiled=True)  19.1 us
    all_to_all x1, starting transfers between devices, on_device(): lax.all_to_all(code_call(x, nrep), 'rep', split_axis=0, concat_axis=0, ti...  17.7 us
    ppermute x3, waiting for transfers between devices, on_device(): lax.ppermute(pair, 'rep', [(j, (j + halves * d) % nrep) for j in range(nr...  10 us
    all_to_all x1, blocking collectives, on_device(): lax.all_to_all(copies, 'rep', split_axis=0, concat_axis=0, axis_index_gro...  9.46 us
    all_to_all x1, waiting for transfers between devices, on_device(): lax.all_to_all(code_call(x, nrep), 'rep', split_axis=0, concat_axis=0, ti...  9.28 us
    ppermute x3, starting transfers between devices, on_device(): lax.ppermute(pair, 'rep', [(j, (j + halves * d) % nrep) for j in range(nr...  8.42 us
  transfers between devices with their start and end apart: 8, of which 8 were waited for; matrix products, arithmetic and copies ran while one was open for 2% of the time, Pallas kernels for 0%

profile of v3, /device:TPU:1, one launch (start us, length us, event | category | flops | bytes accessed | tf_op | source)
XLA Modules:
  0.0 155.9 jit_solution(17581089413626726184)
XLA Ops:
  0.6 0.0 copy-start
  0.6 1.0 copy-done
  1.7 1.6 %shard_map.85 = bf16[8,256,128]{2,1,0:T(8,128)(2,1)} custom-call(bf16[128,4,512]{2,1,0:T(4,128)(2,1)S(1)} %bitcast.32), custom_call_target="tpu_custom_call" | custom-call | tf_op jit(solution)/shard_map/pallas_call | solution.py:105
  3.3 0.0 copy-start.5
  3.3 17.7 %all-to-all-start = ((bf16[8,256,128]{2,1,0:T(8,128)(2,1)}), bf16[8,256,128]{2,1,0:T(8,128)(2,1)S(1)}, u32[]{:S(2)}, u32[]{:S(2)}) async-start(bf16[8,256,128]{2,1,0:T(8,128)(2,1)} %shard_map.85), calls=%async_computation | async-start | bytes 1048576 | tf_op jit(solution)/shard_map/all_to_all | solution.py:138
  21.0 0.0 copy-done.5
  21.0 0.2 convert_reduce_fusion
  21.2 9.3 %all-to-all-done = bf16[8,256,128]{2,1,0:T(8,128)(2,1)S(1)} async-done(((bf16[8,256,128]{2,1,0:T(8,128)(2,1)}), bf16[8,256,128]{2,1,0:T(8,128)(2,1)S(1)}, u32[]{:S(2)}, u32[]{:S(2)}) %all-to-all-start) | async-done | bytes 524320 | tf_op jit(solution)/shard_map/all_to_all | solution.py:138
  30.5 0.1 reduce_sum.22
  30.5 0.9 convolution_convert_fusion
  31.4 0.0 copy-start.4
  31.4 21.3 %all-to-all-start.1 = ((bf16[128,4,128]{2,1,0:T(4,128)(2,1)}), bf16[128,4,128]{2,1,0:T(4,128)(2,1)S(1)}, u32[]{:S(2)}, u32[]{:S(2)}) async-start(bf16[128,4,128]{2,1,0:T(4,128)(2,1)} %bitcast.2), calls=%async_computation.1 | async-start | bytes 262144 | tf_op jit(solution)/shard_map/all_to_all | solution.py:150
  52.7 0.0 copy-done.4
  52.7 3.1 %collective-permute-start = (bf16[128,512]{1,0:T(8,128)(2,1)S(1)}, bf16[128,512]{1,0:T(8,128)(2,1)S(1)}, u32[]{:S(2)}, u32[]{:S(2)}) collective-permute-start(bf16[128,512]{1,0:T(8,128)(2,1)S(1)} %bitcast.36), channel_id=1, source_target_pairs={{0,1},{1,0},{2,3},{3,2},{4,5},{5,4},{6,7},{7,6},{8,9},{9,8},{10,11... | collective-permute-start | bytes 393224 | tf_op jit(solution)/shard_map/ppermute | solution.py:153
  55.8 1.0 collective-permute-done
  56.8 2.2 %collective-permute-start.1 = (bf16[2,128,512]{2,1,0:T(8,128)(2,1)S(1)}, bf16[2,128,512]{2,1,0:T(8,128)(2,1)S(1)}, u32[]{:S(2)}, u32[]{:S(2)}) collective-permute-start(bf16[2,128,512]{2,1,0:T(8,128)(2,1)S(1)} %pad_maximum_fusion.refs_0_), channel_id=1, source_target_pairs={{0,2},{1,3},{2,4},{3,5},{4,6},{5,7},{6,0},{7,1},{8,10},{9,11},{10,... | collective-permute-start | bytes 786440 | tf_op jit(solution)/shard_map/ppermute | solution.py:156
  59.0 3.7 %collective-permute-start.2 = (bf16[2,128,512]{2,1,0:T(8,128)(2,1)S(1)}, bf16[2,128,512]{2,1,0:T(8,128)(2,1)S(1)}, u32[]{:S(2)}, u32[]{:S(2)}) collective-permute-start(bf16[2,128,512]{2,1,0:T(8,128)(2,1)S(1)} %pad_maximum_fusion.refs_0_), channel_id=1, source_target_pairs={{0,4},{1,5},{2,6},{3,7},{4,0},{5,1},{6,2},{7,3},{8,12},{9,13},{10,... | collective-permute-start | bytes 786440 | tf_op jit(solution)/shard_map/ppermute | solution.py:156
  62.7 2.5 %collective-permute-start.3 = (bf16[2,128,512]{2,1,0:T(8,128)(2,1)S(1)}, bf16[2,128,512]{2,1,0:T(8,128)(2,1)S(1)}, u32[]{:S(2)}, u32[]{:S(2)}) collective-permute-start(bf16[2,128,512]{2,1,0:T(8,128)(2,1)S(1)} %pad_maximum_fusion.refs_0_), channel_id=1, source_target_pairs={{0,6},{1,7},{2,0},{3,1},{4,2},{5,3},{6,4},{7,5},{8,14},{9,15},{10,... | collective-permute-start | bytes 786440 | tf_op jit(solution)/shard_map/ppermute | solution.py:156
  65.2 2.8 %collective-permute-done.1.refs_1_ = bf16[2,128,512]{2,1,0:T(8,128)(2,1)S(1)} collective-permute-done((bf16[2,128,512]{2,1,0:T(8,128)(2,1)S(1)}, bf16[2,128,512]{2,1,0:T(8,128)(2,1)S(1)}, u32[]{:S(2)}, u32[]{:S(2)}) %collective-permute-start.1) | collective-permute-done | bytes 262176 | tf_op jit(solution)/shard_map/ppermute | solution.py:156
  68.0 4.5 %collective-permute-done.2.refs_2_ = bf16[2,128,512]{2,1,0:T(8,128)(2,1)S(1)} collective-permute-done((bf16[2,128,512]{2,1,0:T(8,128)(2,1)S(1)}, bf16[2,128,512]{2,1,0:T(8,128)(2,1)S(1)}, u32[]{:S(2)}, u32[]{:S(2)}) %collective-permute-start.2) | collective-permute-done | bytes 262176 | tf_op jit(solution)/shard_map/ppermute | solution.py:156
  72.5 2.8 %collective-permute-done.3.refs_3_ = bf16[2,128,512]{2,1,0:T(8,128)(2,1)S(1)} collective-permute-done((bf16[2,128,512]{2,1,0:T(8,128)(2,1)S(1)}, bf16[2,128,512]{2,1,0:T(8,128)(2,1)S(1)}, u32[]{:S(2)}, u32[]{:S(2)}) %collective-permute-start.3) | collective-permute-done | bytes 262176 | tf_op jit(solution)/shard_map/ppermute | solution.py:156
  75.3 7.6 %all-to-all-done.1 = bf16[128,4,128]{2,1,0:T(4,128)(2,1)S(1)} async-done(((bf16[128,4,128]{2,1,0:T(4,128)(2,1)}), bf16[128,4,128]{2,1,0:T(4,128)(2,1)S(1)}, u32[]{:S(2)}, u32[]{:S(2)}) %all-to-all-start.1) | async-done | bytes 131104 | tf_op jit(solution)/shard_map/all_to_all | solution.py:150
  82.9 0.1 broadcast_in_dim.9
  83.0 0.0 copy-start.1
  83.0 9.5 %all_to_all.20.mine_ref = bf16[4,512,128]{2,1,0:T(8,128)(2,1)S(1)} all-to-all(bf16[4,512,128]{2,1,0:T(8,128)(2,1)S(1)} %broadcast_in_dim.9), channel_id=1, replica_groups={{0,2,4,6},{1,3,5,7},{8,10,12,14},{9,11,13,15},{16,18,20,22},{17,19,21,2..., dimensions={0} | all-to-all | bytes 1048576 | tf_op jit(solution)/shard_map/all_to_all | solution.py:161
  92.5 6.3 %collective-permute-start.4 = (bf16[4,512,128]{2,1,0:T(8,128)(2,1)S(1)}, bf16[4,512,128]{2,1,0:T(8,128)(2,1)S(1)}, u32[]{:S(2)}, u32[]{:S(2)}) collective-permute-start(bf16[4,512,128]{2,1,0:T(8,128)(2,1)S(1)} %all_to_all.20.mine_ref), channel_id=1, source_target_pairs={{0,1},{1,0},{2,3},{3,2},{4,5},{5,4},{6,7},{7,6},{8,9},{9,8},{10,11... | collective-permute-start | bytes 1572872 | tf_op jit(solution)/shard_map/ppermute | solution.py:162
  98.8 1.5 collective-permute-done.4.other_ref
  100.3 0.0 copy-done.1
  100.3 4.7 %shard_map.86 = (bf16[2,512,512]{2,1,0:T(8,128)(2,1)S(1)}, bf16[512,128]{1,0:T(8,128)(2,1)}) custom-call(s32[1]{0:T(128)} %bitcast.rank_ref, bf16[4,512,128]{2,1,0:T(8,128)(2,1)S(1)} %all_to_all.20.mine_ref, bf16[4,512,128]{2,1,0:T(8,128)(2,1)S(1)} %collective-permute-done.4.other_ref, bf16[2,64,512]{2,1,0:T(8,128)(2,1)S(1)} %bitcast.33, ...), custom_call_target="tpu_custom_call" | custom-call | tf_op jit(solution)/shard_map/pallas_call | solution.py:116
  105.1 0.0 copy-start.2
  105.1 19.1 %all-to-all-start.3 = ((bf16[128,4,128]{2,1,0:T(4,128)(2,1)}), bf16[128,4,128]{2,1,0:T(4,128)(2,1)S(1)}, u32[]{:S(2)}, u32[]{:S(2)}) async-start(bf16[128,4,128]{2,1,0:T(4,128)(2,1)} %bitcast.9), calls=%async_computation.3 | async-start | bytes 262144 | tf_op jit(solution)/shard_map/all_to_all | solution.py:165
  124.2 0.0 copy-done.2
  124.2 0.0 copy-start.3
  124.2 1.1 fusion.1
  125.4 0.0 copy-done.3
  125.4 1.1 fusion.3
  126.5 28.4 %all-to-all-done.3 = bf16[128,4,128]{2,1,0:T(4,128)(2,1)S(1)} async-done(((bf16[128,4,128]{2,1,0:T(4,128)(2,1)}), bf16[128,4,128]{2,1,0:T(4,128)(2,1)S(1)}, u32[]{:S(2)}, u32[]{:S(2)}) %all-to-all-start.3) | async-done | bytes 131104 | tf_op jit(solution)/shard_map/all_to_all | solution.py:165
  154.9 0.1 copy.12
  155.0 0.9 fusion.4
  (5 shorter events, 0.1 us)
Async XLA Ops:
  0.6 1.0 copy-start
  3.3 17.7 %copy-start.5 = (s32[128]{0:T(128)S(1)}, s32[128]{0:T(128)}, u32[]{:S(2)}) copy-start(s32[128]{0:T(128)} %param.7) | copy-start | bytes 1540
  3.3 27.2 %all-to-all-start = ((bf16[8,256,128]{2,1,0:T(8,128)(2,1)}), bf16[8,256,128]{2,1,0:T(8,128)(2,1)S(1)}, u32[]{:S(2)}, u32[]{:S(2)}) async-start(bf16[8,256,128]{2,1,0:T(8,128)(2,1)} %shard_map.85), calls=%async_computation | async-start | bytes 1048576 | tf_op jit(solution)/shard_map/all_to_all | solution.py:138
  31.4 21.3 %copy-start.4 = (bf16[1,2,64,512]{3,2,1,0:T(8,128)(2,1)S(1)}, bf16[1,2,64,512]{3,2,1,0:T(8,128)(2,1)}, u32[]{:S(2)}) copy-start(bf16[1,2,64,512]{3,2,1,0:T(8,128)(2,1)} %param.10) | copy-start | bytes 393220
  31.4 51.5 %all-to-all-start.1 = ((bf16[128,4,128]{2,1,0:T(4,128)(2,1)}), bf16[128,4,128]{2,1,0:T(4,128)(2,1)S(1)}, u32[]{:S(2)}, u32[]{:S(2)}) async-start(bf16[128,4,128]{2,1,0:T(4,128)(2,1)} %bitcast.2), calls=%async_computation.1 | async-start | bytes 262144 | tf_op jit(solution)/shard_map/all_to_all | solution.py:150
  52.7 4.0 %collective-permute-start = (bf16[128,512]{1,0:T(8,128)(2,1)S(1)}, bf16[128,512]{1,0:T(8,128)(2,1)S(1)}, u32[]{:S(2)}, u32[]{:S(2)}) collective-permute-start(bf16[128,512]{1,0:T(8,128)(2,1)S(1)} %bitcast.36), channel_id=1, source_target_pairs={{0,1},{1,0},{2,3},{3,2},{4,5},{5,4},{6,7},{7,6},{8,9},{9,8},{10,11... | collective-permute-start | bytes 393224 | tf_op jit(solution)/shard_map/ppermute | solution.py:153
  56.8 11.2 %collective-permute-start.1 = (bf16[2,128,512]{2,1,0:T(8,128)(2,1)S(1)}, bf16[2,128,512]{2,1,0:T(8,128)(2,1)S(1)}, u32[]{:S(2)}, u32[]{:S(2)}) collective-permute-start(bf16[2,128,512]{2,1,0:T(8,128)(2,1)S(1)} %pad_maximum_fusion.refs_0_), channel_id=1, source_target_pairs={{0,2},{1,3},{2,4},{3,5},{4,6},{5,7},{6,0},{7,1},{8,10},{9,11},{10,... | collective-permute-start | bytes 786440 | tf_op jit(solution)/shard_map/ppermute | solution.py:156
  59.0 13.5 %collective-permute-start.2 = (bf16[2,128,512]{2,1,0:T(8,128)(2,1)S(1)}, bf16[2,128,512]{2,1,0:T(8,128)(2,1)S(1)}, u32[]{:S(2)}, u32[]{:S(2)}) collective-permute-start(bf16[2,128,512]{2,1,0:T(8,128)(2,1)S(1)} %pad_maximum_fusion.refs_0_), channel_id=1, source_target_pairs={{0,4},{1,5},{2,6},{3,7},{4,0},{5,1},{6,2},{7,3},{8,12},{9,13},{10,... | collective-permute-start | bytes 786440 | tf_op jit(solution)/shard_map/ppermute | solution.py:156
  62.7 12.6 %collective-permute-start.3 = (bf16[2,128,512]{2,1,0:T(8,128)(2,1)S(1)}, bf16[2,128,512]{2,1,0:T(8,128)(2,1)S(1)}, u32[]{:S(2)}, u32[]{:S(2)}) collective-permute-start(bf16[2,128,512]{2,1,0:T(8,128)(2,1)S(1)} %pad_maximum_fusion.refs_0_), channel_id=1, source_target_pairs={{0,6},{1,7},{2,0},{3,1},{4,2},{5,3},{6,4},{7,5},{8,14},{9,15},{10,... | collective-permute-start | bytes 786440 | tf_op jit(solution)/shard_map/ppermute | solution.py:156
  83.0 17.3 %copy-start.1 = (bf16[1,2,64,512]{3,2,1,0:T(8,128)(2,1)S(1)}, bf16[1,2,64,512]{3,2,1,0:T(8,128)(2,1)}, u32[]{:S(2)}) copy-start(bf16[1,2,64,512]{3,2,1,0:T(8,128)(2,1)} %param.11) | copy-start | bytes 393220
  92.5 7.8 %collective-permute-start.4 = (bf16[4,512,128]{2,1,0:T(8,128)(2,1)S(1)}, bf16[4,512,128]{2,1,0:T(8,128)(2,1)S(1)}, u32[]{:S(2)}, u32[]{:S(2)}) collective-permute-start(bf16[4,512,128]{2,1,0:T(8,128)(2,1)S(1)} %all_to_all.20.mine_ref), channel_id=1, source_target_pairs={{0,1},{1,0},{2,3},{3,2},{4,5},{5,4},{6,7},{7,6},{8,9},{9,8},{10,11... | collective-permute-start | bytes 1572872 | tf_op jit(solution)/shard_map/ppermute | solution.py:162
  105.1 19.1 %copy-start.2 = (f32[1,2,64,512]{3,2,1,0:T(8,128)S(1)}, f32[1,2,64,512]{3,2,1,0:T(8,128)}, u32[]{:S(2)}) copy-start(f32[1,2,64,512]{3,2,1,0:T(8,128)} %param.9) | copy-start | bytes 786436
  105.1 49.8 %all-to-all-start.3 = ((bf16[128,4,128]{2,1,0:T(4,128)(2,1)}), bf16[128,4,128]{2,1,0:T(4,128)(2,1)S(1)}, u32[]{:S(2)}, u32[]{:S(2)}) async-start(bf16[128,4,128]{2,1,0:T(4,128)(2,1)} %bitcast.9), calls=%async_computation.3 | async-start | bytes 262144 | tf_op jit(solution)/shard_map/all_to_all | solution.py:165
  124.2 1.2 copy-start.3

commit v4 on v3

--- a/solution.py
+++ b/solution.py
@@ -58,37 +58,44 @@
                         terms[row:row + step])
 
 
-def root_kernel(rank_ref, mine_ref, other_ref, rroot_ref, *refs):
-    *hop_refs, grad_ref, out_ref = refs
+def root_kernel(rank_ref, mine_ref, other_ref, hops_ref, swapped_ref, rroot_ref, grad_ref, out_ref):
     groups, _, _ = mine_ref.shape
     slots, width, _ = grad_ref.shape
     slab = rroot_ref.shape[1]
     rank = rank_ref[0]
     core = rank % 2
     chip = rank // 2
-    signs = hadamard()
+    one = hadamard()
+    none = jnp.zeros_like(one)
+    signs = jnp.concatenate([jnp.concatenate([one, none], axis=1), jnp.concatenate([none, one], axis=1)], axis=0)
     o = lax.broadcasted_iota(I32, (256, 256), 0)
     i = lax.broadcasted_iota(I32, (256, 256), 1)
     half = jnp.where(i < 128, core, 1 - core)
     from_row = ((i % 128) // 4) * 4 + half * 2 + i % 2
     perm = ((o % 128 == from_row) & (o // 128 == (i // 2) % 2)).astype(F32).astype(BF)
-    for t in range(width // 128):
+    tiles = width // 128
+    placed = []
+    for t in range(tiles):
         rows = slice(t * 128, (t + 1) * 128)
-        for g in range(groups):
-            both = jnp.concatenate([mine_ref[g, rows, :], other_ref[g, rows, :]], axis=0)
-            placed = mm(perm, both).astype(BF)
-            block = (mm(placed, signs) * NORM).astype(BF)
-            for s in range(slots):
-                grad_ref[s, rows, g * GROUP:(g + 1) * GROUP] = block[s * 128:(s + 1) * 128]
+        both = jnp.concatenate([
+            jnp.concatenate([mine_ref[g, rows, :] for g in range(groups)], axis=1),
+            jnp.concatenate([other_ref[g, rows, :] for g in range(groups)], axis=1)], axis=0)
+        placed.append(mm(perm, both).astype(BF))
+    coded = [jnp.concatenate([p[s * 128:(s + 1) * 128] for p in placed], axis=0) for s in range(slots)]
+    middles = []
     for s in range(slots):
-        middle = mm_t(grad_ref[s], rroot_ref[s]).astype(BF)
-        for d, hop_ref in enumerate(hop_refs):
-            from_chip = (chip + groups - d) % groups
-            left = hop_ref[:, s * slab:(s + 1) * slab, :].reshape(2 * slab, width)
-            rows = mm(left, middle).astype(BF)
-            for k in range(2):
-                start = pl.multiple_of((from_chip * 2 + (core + k) % 2) * slab, slab)
-                out_ref[pl.ds(start, slab), s * slab:(s + 1) * slab] = rows[k * slab:(k + 1) * slab]
+        grad = jnp.concatenate(
+            [(mm(coded[s][:, c:c + 256], signs) * NORM).astype(BF) for c in range(0, width, 256)], axis=1)
+        grad_ref[s] = grad
+        middles.append(mm_t(grad, rroot_ref[s]).astype(BF))
+    for s in range(slots):
+        for k, ref in enumerate((hops_ref, swapped_ref)):
+            left = ref[:, s * slab:(s + 1) * slab, :].reshape(groups * slab, width)
+            rows = mm(left, middles[s]).astype(BF)
+            for d in range(groups):
+                start = ((chip + groups - d) % groups * 2 + (core + k) % 2) * slab
+                out_ref[pl.ds(pl.multiple_of(start, slab), slab), s * slab:(s + 1) * slab] = (
+                    rows[d * slab:(d + 1) * slab])
 
 
 def kernel_params():
@@ -111,16 +118,16 @@
     )(x)
 
 
-def root_call(rank, mine, other, hops, rroot):
+def root_call(rank, mine, other, hops, swapped, rroot):
     slots, slab, width = rroot.shape
     return pl.pallas_call(
         root_kernel,
         out_shape=(jax.ShapeDtypeStruct((slots, width, width), BF),
                    jax.ShapeDtypeStruct((width, slots * slab), BF)),
-        in_specs=[pl.BlockSpec(memory_space=pltpu.SMEM)] + [in_vmem()] * (3 + len(hops)),
+        in_specs=[pl.BlockSpec(memory_space=pltpu.SMEM)] + [in_vmem()] * 5,
         out_specs=(in_vmem(), in_vmem()),
         compiler_params=kernel_params(),
-    )(rank, mine, other, rroot, *hops)
+    )(rank, mine, other, hops, swapped, rroot)
 
 
 def on_device(grads, owner, left_stat, right_stat, left_root, right_root):
@@ -150,17 +157,18 @@
     arrived = lax.all_to_all(outgoing, "fsdp", split_axis=0, concat_axis=0, tiled=True)
     own = lroot_rows.reshape(SLOTS * slab, width)
     swap = [(j, j + 1 - 2 * (j % 2)) for j in range(nrep)]
-    pair = jnp.stack([own, lax.ppermute(own, "rep", swap)])
-    hops = [pair]
+    hops = [own]
     for d in range(1, groups):
-        hops.append(lax.ppermute(pair, "rep", [(j, (j + halves * d) % nrep) for j in range(nrep)]))
+        hops.append(lax.ppermute(own, "rep", [(j, (j + halves * d) % nrep) for j in range(nrep)]))
     arrived, hops = lax.optimization_barrier((arrived, hops))
+    hops = jnp.stack(hops)
+    swapped = lax.ppermute(hops, "rep", swap)
 
     chip_mates = [[h + halves * g for g in range(groups)] for h in range(halves)]
     copies = jnp.broadcast_to(arrived.reshape(1, part, GROUP), (groups, part, GROUP))
     mine = lax.all_to_all(copies, "rep", split_axis=0, concat_axis=0, axis_index_groups=chip_mates, tiled=True)
     other = lax.ppermute(mine, "rep", swap)
-    gradient, direction = root_call(rank.reshape(1), mine, other, hops, right_root[0])
+    gradient, direction = root_call(rank.reshape(1), mine, other, hops, swapped, right_root[0])
     packed = direction.reshape(nf, rows, SLOTS * slab)
     back = lax.all_to_all(packed, "fsdp", split_axis=0, concat_axis=0, tiled=True)
 

time: 157 us -> 144 us (0.917)
  blocking collectives: 9.46 us -> 0 us
  starting transfers between devices: 75.9 us -> 69.9 us
  waiting for transfers between devices: 57.8 us -> 62.5 us
  Pallas kernels: 6.35 us -> 3.71 us
    all_to_all x1, starting transfers between devices: 19.1 us -> 7.59 us  [on_device(): lax.all_to_all(packed, 'fsdp', split_axis=0, concat_axis=0, tiled=True)]
    all_to_all x1 -> x0, blocking collectives: 9.46 us -> none  [on_device(): lax.all_to_all(copies, 'rep', split_axis=0, concat_axis=0, axis_index_gro...]
    all_to_all x1, waiting for transfers between devices: 7.64 us -> 16.9 us  [on_device(): lax.all_to_all(outgoing, 'fsdp', split_axis=0, concat_axis=0, tiled=True)]
    ppermute x4, waiting for transfers between devices: 11 us -> 4.87 us  [the longest x3 4.86 us: on_device(): lax.ppermute(own, 'rep', [(j, (j + halves * d) % nrep) for j in range(nre...]
    all_to_all x0 -> x1, starting transfers between devices: none -> 3.47 us  [on_device(): lax.all_to_all(copies, 'rep', split_axis=0, concat_axis=0, axis_index_gro...]
    pallas_call x1, Pallas kernels: 4.75 us -> 2.11 us  [root_call(): pl.pallas_call(root_kernel, out_shape=(jax.ShapeDtypeStruct((slots, width...]
    ppermute x4, starting transfers between devices: 11.5 us -> 13.6 us  [the longest x3 8.42 us: on_device(): lax.ppermute(own, 'rep', [(j, (j + halves * d) % nrep) for j in range(nre...]
    all_to_all x0 -> x1, waiting for transfers between devices: none -> 1.62 us  [on_device(): lax.all_to_all(copies, 'rep', split_axis=0, concat_axis=0, axis_index_gro...]
  transfers between devices with their start and end apart: 8 -> 9, of which waited for: 8 -> 7; matrix products, arithmetic and copies ran while one was open for 2% -> 2% of each run, Pallas kernels for 0% -> 0%
where the time goes in v4:
time: 144 us; the launch traced here: 143 us
  starting transfers between devices  69.9 us (49%)
  waiting for transfers between devices  62.5 us (43%)
  matrix products  4.09 us (3%)
  Pallas kernels  3.71 us (3%)
  local copies, waits for them, and re-layouts  2.05 us (1%)
    all_to_all x1, waiting for transfers between devices, on_device(): lax.all_to_all(packed, 'fsdp', split_axis=0, concat_axis=0, tiled=True)  28.4 us
    all_to_all x1, starting transfers between devices, on_device(): lax.all_to_all(outgoing, 'fsdp', split_axis=0, concat_axis=0, tiled=True)  21.3 us
    all_to_all x1, starting transfers between devices, on_device(): lax.all_to_all(code_call(x, nrep), 'rep', split_axis=0, concat_axis=0, ti...  17.7 us
    all_to_all x1, waiting for transfers between devices, on_device(): lax.all_to_all(outgoing, 'fsdp', split_axis=0, concat_axis=0, tiled=True)  16.9 us
    all_to_all x1, waiting for transfers between devices, on_device(): lax.all_to_all(code_call(x, nrep), 'rep', split_axis=0, concat_axis=0, ti...  9.28 us
    ppermute x3, starting transfers between devices, on_device(): lax.ppermute(own, 'rep', [(j, (j + halves * d) % nrep) for j in range(nre...  8.42 us
    all_to_all x1, starting transfers between devices, on_device(): lax.all_to_all(packed, 'fsdp', split_axis=0, concat_axis=0, tiled=True)  7.59 us
    ppermute x1, starting transfers between devices, on_device(): other = lax.ppermute(mine, 'rep', swap)  6.31 us
  transfers between devices with their start and end apart: 9, of which 7 were waited for; matrix products, arithmetic and copies ran while one was open for 2% of the time, Pallas kernels for 0%

profile of v4, /device:TPU:1, one launch (start us, length us, event | category | flops | bytes accessed | tf_op | source)
XLA Modules:
  0.0 143.4 jit_solution(468588827288414600)
XLA Ops:
  0.6 0.0 copy-start
  0.6 1.0 copy-done
  1.7 1.6 %shard_map.85 = bf16[8,256,128]{2,1,0:T(8,128)(2,1)} custom-call(bf16[128,4,512]{2,1,0:T(4,128)(2,1)S(1)} %bitcast.34), custom_call_target="tpu_custom_call" | custom-call | tf_op jit(solution)/shard_map/pallas_call | solution.py:112
  3.3 0.0 copy-start.5
  3.3 17.7 %all-to-all-start = ((bf16[8,256,128]{2,1,0:T(8,128)(2,1)}), bf16[8,256,128]{2,1,0:T(8,128)(2,1)S(1)}, u32[]{:S(2)}, u32[]{:S(2)}) async-start(bf16[8,256,128]{2,1,0:T(8,128)(2,1)} %shard_map.85), calls=%async_computation | async-start | bytes 1048576 | tf_op jit(solution)/shard_map/all_to_all | solution.py:145
  21.0 0.0 copy-done.5
  21.0 0.2 convert_reduce_fusion
  21.2 9.3 %all-to-all-done = bf16[8,256,128]{2,1,0:T(8,128)(2,1)S(1)} async-done(((bf16[8,256,128]{2,1,0:T(8,128)(2,1)}), bf16[8,256,128]{2,1,0:T(8,128)(2,1)S(1)}, u32[]{:S(2)}, u32[]{:S(2)}) %all-to-all-start) | async-done | bytes 524320 | tf_op jit(solution)/shard_map/all_to_all | solution.py:145
  30.5 0.1 reduce_sum.22
  30.5 0.9 convolution_convert_fusion
  31.4 0.0 copy-start.4
  31.4 21.3 %all-to-all-start.1 = ((bf16[128,4,128]{2,1,0:T(4,128)(2,1)}), bf16[128,4,128]{2,1,0:T(4,128)(2,1)S(1)}, u32[]{:S(2)}, u32[]{:S(2)}) async-start(bf16[128,4,128]{2,1,0:T(4,128)(2,1)} %bitcast.2), calls=%async_computation.1 | async-start | bytes 262144 | tf_op jit(solution)/shard_map/all_to_all | solution.py:157
  52.7 0.0 copy-done.4
  52.7 2.2 %collective-permute-start = (bf16[128,512]{1,0:T(8,128)(2,1)S(1)}, bf16[128,512]{1,0:T(8,128)(2,1)S(1)}, u32[]{:S(2)}, u32[]{:S(2)}) collective-permute-start(bf16[128,512]{1,0:T(8,128)(2,1)S(1)} %bitcast.38), channel_id=1, source_target_pairs={{0,2},{1,3},{2,4},{3,5},{4,6},{5,7},{6,0},{7,1},{8,10},{9,11},{10,... | collective-permute-start | bytes 393224 | tf_op jit(solution)/shard_map/ppermute | solution.py:162
  54.9 3.7 %collective-permute-start.1 = (bf16[128,512]{1,0:T(8,128)(2,1)S(1)}, bf16[128,512]{1,0:T(8,128)(2,1)S(1)}, u32[]{:S(2)}, u32[]{:S(2)}) collective-permute-start(bf16[128,512]{1,0:T(8,128)(2,1)S(1)} %bitcast.39), channel_id=1, source_target_pairs={{0,4},{1,5},{2,6},{3,7},{4,0},{5,1},{6,2},{7,3},{8,12},{9,13},{10,... | collective-permute-start | bytes 393224 | tf_op jit(solution)/shard_map/ppermute | solution.py:162
  58.6 2.5 %collective-permute-start.2 = (bf16[128,512]{1,0:T(8,128)(2,1)S(1)}, bf16[128,512]{1,0:T(8,128)(2,1)S(1)}, u32[]{:S(2)}, u32[]{:S(2)}) collective-permute-start(bf16[128,512]{1,0:T(8,128)(2,1)S(1)} %bitcast.40), channel_id=1, source_target_pairs={{0,6},{1,7},{2,0},{3,1},{4,2},{5,3},{6,4},{7,5},{8,14},{9,15},{10,... | collective-permute-start | bytes 393224 | tf_op jit(solution)/shard_map/ppermute | solution.py:162
  61.2 0.0 collective-permute-done
  61.2 1.3 collective-permute-done.1
  62.5 3.6 %collective-permute-done.2 = bf16[128,512]{1,0:T(8,128)(2,1)S(1)} collective-permute-done((bf16[128,512]{1,0:T(8,128)(2,1)S(1)}, bf16[128,512]{1,0:T(8,128)(2,1)S(1)}, u32[]{:S(2)}, u32[]{:S(2)}) %collective-permute-start.2) | collective-permute-done | bytes 131104 | tf_op jit(solution)/shard_map/ppermute | solution.py:162
  66.0 16.9 %all-to-all-done.1 = bf16[128,4,128]{2,1,0:T(4,128)(2,1)S(1)} async-done(((bf16[128,4,128]{2,1,0:T(4,128)(2,1)}), bf16[128,4,128]{2,1,0:T(4,128)(2,1)S(1)}, u32[]{:S(2)}, u32[]{:S(2)}) %all-to-all-start.1) | async-done | bytes 131104 | tf_op jit(solution)/shard_map/all_to_all | solution.py:157
  82.9 0.9 broadcast_in_dim.9
  83.8 3.5 %all-to-all-start.2 = ((bf16[4,512,128]{2,1,0:T(8,128)(2,1)}), bf16[4,512,128]{2,1,0:T(8,128)(2,1)S(1)}, u32[]{:S(2)}, u32[]{:S(2)}) async-start(bf16[4,512,128]{2,1,0:T(8,128)(2,1)} %broadcast_in_dim.9), calls=%async_computation.2 | async-start | bytes 1048576 | tf_op jit(solution)/shard_map/all_to_all | solution.py:169
  87.2 0.0 copy-start.1
  87.3 0.1 pad_maximum_fusion.hops_ref
  87.3 5.2 %collective-permute-start.4 = (bf16[4,128,512]{2,1,0:T(8,128)(2,1)S(1)}, bf16[4,128,512]{2,1,0:T(8,128)(2,1)S(1)}, u32[]{:S(2)}, u32[]{:S(2)}) collective-permute-start(bf16[4,128,512]{2,1,0:T(8,128)(2,1)S(1)} %pad_maximum_fusion.hops_ref), channel_id=1, source_target_pairs={{0,1},{1,0},{2,3},{3,2},{4,5},{5,4},{6,7},{7,6},{8,9},{9,8},{10,11... | collective-permute-start | bytes 1572872 | tf_op jit(solution)/shard_map/ppermute | solution.py:165
  92.5 1.6 %all-to-all-done.2.mine_ref = bf16[4,512,128]{2,1,0:T(8,128)(2,1)S(1)} async-done(((bf16[4,512,128]{2,1,0:T(8,128)(2,1)}), bf16[4,512,128]{2,1,0:T(8,128)(2,1)S(1)}, u32[]{:S(2)}, u32[]{:S(2)}) %all-to-all-start.2) | async-done | bytes 524320 | tf_op jit(solution)/shard_map/all_to_all | solution.py:169
  94.1 6.3 %collective-permute-start.3 = (bf16[4,512,128]{2,1,0:T(8,128)(2,1)S(1)}, bf16[4,512,128]{2,1,0:T(8,128)(2,1)S(1)}, u32[]{:S(2)}, u32[]{:S(2)}) collective-permute-start(bf16[4,512,128]{2,1,0:T(8,128)(2,1)S(1)} %all-to-all-done.2.mine_ref), channel_id=1, source_target_pairs={{0,1},{1,0},{2,3},{3,2},{4,5},{5,4},{6,7},{7,6},{8,9},{9,8},{10,11... | collective-permute-start | bytes 1572872 | tf_op jit(solution)/shard_map/ppermute | solution.py:170
  100.5 0.0 collective-permute-done.4.swapped_ref
  100.5 1.5 %collective-permute-done.3.other_ref = bf16[4,512,128]{2,1,0:T(8,128)(2,1)S(1)} collective-permute-done((bf16[4,512,128]{2,1,0:T(8,128)(2,1)S(1)}, bf16[4,512,128]{2,1,0:T(8,128)(2,1)S(1)}, u32[]{:S(2)}, u32[]{:S(2)}) %collective-permute-start.3) | collective-permute-done | bytes 524320 | tf_op jit(solution)/shard_map/ppermute | solution.py:170
  102.0 0.0 copy-done.1
  102.0 2.1 %shard_map.86 = (bf16[2,512,512]{2,1,0:T(8,128)(2,1)S(1)}, bf16[512,128]{1,0:T(8,128)(2,1)}) custom-call(s32[1]{0:T(128)} %bitcast.rank_ref, bf16[4,512,128]{2,1,0:T(8,128)(2,1)S(1)} %all-to-all-done.2.mine_ref, bf16[4,512,128]{2,1,0:T(8,128)(2,1)S(1)} %collective-permute-done.3.other_ref, bf16[4,128,512]{2,1,0:T(8,128)(2,1)S(1)} %pad_maximum_fusion.hops_ref, ...), custom_call_target="tpu_custom_call" | custom-call | tf_op jit(solution)/shard_map/pallas_call | solution.py:123
  104.1 0.0 copy-start.2
  104.1 7.6 %all-to-all-start.3 = ((bf16[128,4,128]{2,1,0:T(4,128)(2,1)}), bf16[128,4,128]{2,1,0:T(4,128)(2,1)S(1)}, u32[]{:S(2)}, u32[]{:S(2)}) async-start(bf16[128,4,128]{2,1,0:T(4,128)(2,1)} %bitcast.11), calls=%async_computation.3 | async-start | bytes 262144 | tf_op jit(solution)/shard_map/all_to_all | solution.py:173
  111.7 0.0 copy-done.2
  111.7 0.0 copy-start.3
  111.7 1.1 fusion.1
  112.9 0.0 copy-done.3
  112.9 1.1 fusion.3
  114.0 28.4 %all-to-all-done.3 = bf16[128,4,128]{2,1,0:T(4,128)(2,1)S(1)} async-done(((bf16[128,4,128]{2,1,0:T(4,128)(2,1)}), bf16[128,4,128]{2,1,0:T(4,128)(2,1)S(1)}, u32[]{:S(2)}, u32[]{:S(2)}) %all-to-all-start.3) | async-done | bytes 131104 | tf_op jit(solution)/shard_map/all_to_all | solution.py:173
  142.4 0.1 copy.12
  142.5 0.9 fusion.4
  (4 shorter events, 0.0 us)
Async XLA Ops:
  0.6 1.0 copy-start
  3.3 17.7 %copy-start.5 = (s32[128]{0:T(128)S(1)}, s32[128]{0:T(128)}, u32[]{:S(2)}) copy-start(s32[128]{0:T(128)} %param.7) | copy-start | bytes 1540
  3.3 27.2 %all-to-all-start = ((bf16[8,256,128]{2,1,0:T(8,128)(2,1)}), bf16[8,256,128]{2,1,0:T(8,128)(2,1)S(1)}, u32[]{:S(2)}, u32[]{:S(2)}) async-start(bf16[8,256,128]{2,1,0:T(8,128)(2,1)} %shard_map.85), calls=%async_computation | async-start | bytes 1048576 | tf_op jit(solution)/shard_map/all_to_all | solution.py:145
  31.4 21.3 %copy-start.4 = (bf16[1,2,64,512]{3,2,1,0:T(8,128)(2,1)S(1)}, bf16[1,2,64,512]{3,2,1,0:T(8,128)(2,1)}, u32[]{:S(2)}) copy-start(bf16[1,2,64,512]{3,2,1,0:T(8,128)(2,1)} %param.10) | copy-start | bytes 393220
  31.4 51.5 %all-to-all-start.1 = ((bf16[128,4,128]{2,1,0:T(4,128)(2,1)}), bf16[128,4,128]{2,1,0:T(4,128)(2,1)S(1)}, u32[]{:S(2)}, u32[]{:S(2)}) async-start(bf16[128,4,128]{2,1,0:T(4,128)(2,1)} %bitcast.2), calls=%async_computation.1 | async-start | bytes 262144 | tf_op jit(solution)/shard_map/all_to_all | solution.py:157
  52.7 8.4 %collective-permute-start = (bf16[128,512]{1,0:T(8,128)(2,1)S(1)}, bf16[128,512]{1,0:T(8,128)(2,1)S(1)}, u32[]{:S(2)}, u32[]{:S(2)}) collective-permute-start(bf16[128,512]{1,0:T(8,128)(2,1)S(1)} %bitcast.38), channel_id=1, source_target_pairs={{0,2},{1,3},{2,4},{3,5},{4,6},{5,7},{6,0},{7,1},{8,10},{9,11},{10,... | collective-permute-start | bytes 393224 | tf_op jit(solution)/shard_map/ppermute | solution.py:162
  54.9 7.6 %collective-permute-start.1 = (bf16[128,512]{1,0:T(8,128)(2,1)S(1)}, bf16[128,512]{1,0:T(8,128)(2,1)S(1)}, u32[]{:S(2)}, u32[]{:S(2)}) collective-permute-start(bf16[128,512]{1,0:T(8,128)(2,1)S(1)} %bitcast.39), channel_id=1, source_target_pairs={{0,4},{1,5},{2,6},{3,7},{4,0},{5,1},{6,2},{7,3},{8,12},{9,13},{10,... | collective-permute-start | bytes 393224 | tf_op jit(solution)/shard_map/ppermute | solution.py:162
  58.6 7.4 %collective-permute-start.2 = (bf16[128,512]{1,0:T(8,128)(2,1)S(1)}, bf16[128,512]{1,0:T(8,128)(2,1)S(1)}, u32[]{:S(2)}, u32[]{:S(2)}) collective-permute-start(bf16[128,512]{1,0:T(8,128)(2,1)S(1)} %bitcast.40), channel_id=1, source_target_pairs={{0,6},{1,7},{2,0},{3,1},{4,2},{5,3},{6,4},{7,5},{8,14},{9,15},{10,... | collective-permute-start | bytes 393224 | tf_op jit(solution)/shard_map/ppermute | solution.py:162
  83.8 10.4 %all-to-all-start.2 = ((bf16[4,512,128]{2,1,0:T(8,128)(2,1)}), bf16[4,512,128]{2,1,0:T(8,128)(2,1)S(1)}, u32[]{:S(2)}, u32[]{:S(2)}) async-start(bf16[4,512,128]{2,1,0:T(8,128)(2,1)} %broadcast_in_dim.9), calls=%async_computation.2 | async-start | bytes 1048576 | tf_op jit(solution)/shard_map/all_to_all | solution.py:169
  87.2 14.7 %copy-start.1 = (bf16[1,2,64,512]{3,2,1,0:T(8,128)(2,1)S(1)}, bf16[1,2,64,512]{3,2,1,0:T(8,128)(2,1)}, u32[]{:S(2)}) copy-start(bf16[1,2,64,512]{3,2,1,0:T(8,128)(2,1)} %param.11) | copy-start | bytes 393220
  87.3 13.1 %collective-permute-start.4 = (bf16[4,128,512]{2,1,0:T(8,128)(2,1)S(1)}, bf16[4,128,512]{2,1,0:T(8,128)(2,1)S(1)}, u32[]{:S(2)}, u32[]{:S(2)}) collective-permute-start(bf16[4,128,512]{2,1,0:T(8,128)(2,1)S(1)} %pad_maximum_fusion.hops_ref), channel_id=1, source_target_pairs={{0,1},{1,0},{2,3},{3,2},{4,5},{5,4},{6,7},{7,6},{8,9},{9,8},{10,11... | collective-permute-start | bytes 1572872 | tf_op jit(solution)/shard_map/ppermute | solution.py:165
  94.1 7.8 %collective-permute-start.3 = (bf16[4,512,128]{2,1,0:T(8,128)(2,1)S(1)}, bf16[4,512,128]{2,1,0:T(8,128)(2,1)S(1)}, u32[]{:S(2)}, u32[]{:S(2)}) collective-permute-start(bf16[4,512,128]{2,1,0:T(8,128)(2,1)S(1)} %all-to-all-done.2.mine_ref), channel_id=1, source_target_pairs={{0,1},{1,0},{2,3},{3,2},{4,5},{5,4},{6,7},{7,6},{8,9},{9,8},{10,11... | collective-permute-start | bytes 1572872 | tf_op jit(solution)/shard_map/ppermute | solution.py:170
  104.1 7.6 %copy-start.2 = (f32[1,2,64,512]{3,2,1,0:T(8,128)S(1)}, f32[1,2,64,512]{3,2,1,0:T(8,128)}, u32[]{:S(2)}) copy-start(f32[1,2,64,512]{3,2,1,0:T(8,128)} %param.9) | copy-start | bytes 786436
  104.1 38.3 %all-to-all-start.3 = ((bf16[128,4,128]{2,1,0:T(4,128)(2,1)}), bf16[128,4,128]{2,1,0:T(4,128)(2,1)S(1)}, u32[]{:S(2)}, u32[]{:S(2)}) async-start(bf16[128,4,128]{2,1,0:T(4,128)(2,1)} %bitcast.11), calls=%async_computation.3 | async-start | bytes 262144 | tf_op jit(solution)/shard_map/all_to_all | solution.py:173
  111.7 1.2 copy-start.3

commit v5 on v4

--- a/solution.py
+++ b/solution.py
@@ -3,14 +3,15 @@
 from jax import lax
 from jax.experimental import pallas as pl
 from jax.experimental.pallas import tpu as pltpu
-from jax.sharding import PartitionSpec as P
+from jax.sharding import Mesh, PartitionSpec as P
 
 GROUP = 128
 SLOTS = 2
+FSDP, REP = ("x", "z"), ("y", "core")
 DECAY = 0.95
 NORM = GROUP ** (-0.5)
 BF, F32, I32 = jnp.bfloat16, jnp.float32, jnp.int32
-VMEM_BYTES = 48 * 1024 * 1024
+VMEM_BYTES = 24 * 1024 * 1024
 
 
 def hadamard():
@@ -58,8 +59,23 @@
                         terms[row:row + step])
 
 
+def route_kernel(got_ref, route_ref, out_ref):
+    total = got_ref[0].astype(F32)
+    for k in range(1, got_ref.shape[0]):
+        total += got_ref[k].astype(F32)
+    out_ref[...] = mm(route_ref[...], total.astype(BF)).astype(BF)
+
+
+def pick_kernel(back_ref, pick_ref, out_ref):
+    rows, slab, blocks = out_ref.shape
+    back = back_ref[...].astype(F32).T.astype(BF)
+    total = mm(back[:slab], pick_ref[0]) + mm(back[slab:], pick_ref[1])
+    for r in range(rows):
+        out_ref[r] = total[:, r * blocks:(r + 1) * blocks].astype(BF)
+
+
 def root_kernel(rank_ref, mine_ref, other_ref, hops_ref, swapped_ref, rroot_ref, grad_ref, out_ref):
-    groups, _, _ = mine_ref.shape
+    groups = hops_ref.shape[0]
     slots, width, _ = grad_ref.shape
     slab = rroot_ref.shape[1]
     rank = rank_ref[0]
@@ -76,10 +92,8 @@
     tiles = width // 128
     placed = []
     for t in range(tiles):
-        rows = slice(t * 128, (t + 1) * 128)
         both = jnp.concatenate([
-            jnp.concatenate([mine_ref[g, rows, :] for g in range(groups)], axis=1),
-            jnp.concatenate([other_ref[g, rows, :] for g in range(groups)], axis=1)], axis=0)
+            jnp.concatenate([ref[t * groups + g] for g in range(groups)], axis=1) for ref in (mine_ref, other_ref)], axis=0)
         placed.append(mm(perm, both).astype(BF))
     coded = [jnp.concatenate([p[s * 128:(s + 1) * 128] for p in placed], axis=0) for s in range(slots)]
     middles = []
@@ -118,6 +132,27 @@
     )(x)
 
 
+def route_call(got, route):
+    return pl.pallas_call(
+        route_kernel,
+        out_shape=jax.ShapeDtypeStruct((route.shape[0], got.shape[2]), BF),
+        in_specs=[in_vmem()] * 2,
+        out_specs=in_vmem(),
+        compiler_params=kernel_params(),
+    )(got, route)
+
+
+def pick_call(back, pick, rows):
+    nb = pick.shape[2] // rows
+    return pl.pallas_call(
+        pick_kernel,
+        out_shape=jax.ShapeDtypeStruct((rows, back.shape[1] // SLOTS, nb), BF),
+        in_specs=[in_vmem()] * 2,
+        out_specs=in_vmem(),
+        compiler_params=kernel_params(),
+    )(back, pick)
+
+
 def root_call(rank, mine, other, hops, swapped, rroot):
     slots, slab, width = rroot.shape
     return pl.pallas_call(
@@ -133,44 +168,44 @@
 def on_device(grads, owner, left_stat, right_stat, left_root, right_root):
     x = grads[0]
     nb, rows, width = x.shape
-    nf = lax.axis_size("fsdp")
-    nrep = lax.axis_size("rep")
-    groups = width // GROUP
-    halves = nrep // groups
+    nx, nz = lax.axis_size("x"), lax.axis_size("z")
+    nf = nx * nz
+    halves = lax.axis_size("core")
+    groups = lax.axis_size("y")
+    nrep = groups * halves
     per = rows // halves
     slab = width // nrep
-    part = nf * SLOTS * per
-    rank = lax.axis_index("rep")
-
-    got = lax.all_to_all(code_call(x, nrep), "rep", split_axis=0, concat_axis=0, tiled=True)
-    summed = jnp.sum(got.astype(F32), axis=0).astype(BF)
+    rank = lax.axis_index(REP)
+
+    got = lax.all_to_all(code_call(x, nrep), REP, split_axis=0, concat_axis=0, tiled=True)
 
     counter = jnp.arange(nb, dtype=I32)
     same = owner[:, None] == owner[None, :]
     slot_of = jnp.sum(same & (counter[None, :] < counter[:, None]), axis=1)
-    place = owner * SLOTS + slot_of
+    place = ((owner % nz) * nx + owner // nz) * SLOTS + slot_of
     key_in = jnp.concatenate([place * per + r for r in range(per)])
-    route = (jnp.arange(part, dtype=I32)[:, None] == key_in[None, :]).astype(BF)
-    outgoing = mm(route, summed).astype(BF).reshape(nf, SLOTS * per, GROUP)
-
-    outgoing, lroot_rows = lax.optimization_barrier((outgoing, left_root[0]))
-    arrived = lax.all_to_all(outgoing, "fsdp", split_axis=0, concat_axis=0, tiled=True)
-    own = lroot_rows.reshape(SLOTS * slab, width)
-    swap = [(j, j + 1 - 2 * (j % 2)) for j in range(nrep)]
+    route = (jnp.arange(nf * SLOTS * per, dtype=I32)[:, None] == key_in[None, :]).astype(BF)
+    outgoing = route_call(got, route).reshape(nz, nx * SLOTS * per, GROUP)
+
+    outgoing, own = lax.optimization_barrier((outgoing, left_root[0]))
+    arrived = lax.all_to_all(outgoing, "z", split_axis=0, concat_axis=0, tiled=True)
+    own = own.reshape(SLOTS * slab, width)
     hops = [own]
     for d in range(1, groups):
-        hops.append(lax.ppermute(own, "rep", [(j, (j + halves * d) % nrep) for j in range(nrep)]))
+        hops.append(lax.ppermute(own, "y", [(j, (j + d) % groups) for j in range(groups)]))
     arrived, hops = lax.optimization_barrier((arrived, hops))
+    swap = [(0, 1), (1, 0)]
     hops = jnp.stack(hops)
-    swapped = lax.ppermute(hops, "rep", swap)
-
-    chip_mates = [[h + halves * g for g in range(groups)] for h in range(halves)]
-    copies = jnp.broadcast_to(arrived.reshape(1, part, GROUP), (groups, part, GROUP))
-    mine = lax.all_to_all(copies, "rep", split_axis=0, concat_axis=0, axis_index_groups=chip_mates, tiled=True)
-    other = lax.ppermute(mine, "rep", swap)
+    swapped = lax.ppermute(hops, "core", swap)
+
+    tile = nz * SLOTS * per
+    pieces = arrived.reshape(nz, nx, SLOTS * per, GROUP).transpose(1, 0, 2, 3).reshape(nx, 1, tile, GROUP)
+    copies = jnp.broadcast_to(pieces, (nx, groups, tile, GROUP)).reshape(nx * groups, tile, GROUP)
+    mine = lax.all_to_all(copies, ("x", "y"), split_axis=0, concat_axis=0, tiled=True)
+    other = lax.ppermute(mine, "core", swap)
     gradient, direction = root_call(rank.reshape(1), mine, other, hops, swapped, right_root[0])
     packed = direction.reshape(nf, rows, SLOTS * slab)
-    back = lax.all_to_all(packed, "fsdp", split_axis=0, concat_axis=0, tiled=True)
+    back = lax.all_to_all(packed, FSDP, split_axis=0, concat_axis=0, tiled=True)
 
     own_rows = lax.dynamic_slice_in_dim(gradient, rank * slab, slab, axis=1)
     own_cols = lax.dynamic_slice_in_dim(gradient, rank * slab, slab, axis=2)
@@ -179,20 +214,21 @@
     left_new = DECAY * left_stat[0] + (1 - DECAY) * left_gram
     right_new = DECAY * right_stat[0] + (1 - DECAY) * right_gram
 
-    pick = (place[:, None] == jnp.arange(nf * SLOTS, dtype=I32)[None, :]).astype(BF).reshape(nb, nf, SLOTS)
-    update = jnp.einsum("bfs,frsc->brc", pick, back.reshape(nf, rows, SLOTS, slab),
-                        preferred_element_type=F32).astype(BF)
+    owner_row = jnp.arange(nf * rows, dtype=I32)
+    pick = []
+    for s in range(SLOTS):
+        key = jnp.where(slot_of == s, owner * rows, -rows)
+        key = jnp.concatenate([key + r for r in range(rows)])
+        pick.append((owner_row[:, None] == key[None, :]).astype(BF))
+    update = pick_call(back.reshape(nf * rows, SLOTS * slab), jnp.stack(pick), rows).transpose(2, 0, 1)
     return (left_new[None], right_new[None], update)
 
 
 def solution(mesh):
-    in_specs = (
-        P("rep", None, "fsdp", None),
-        P(),
-        P("fsdp", None, "rep", None),
-        P("fsdp", None, "rep", None),
-        P("fsdp", None, "rep", None),
-        P("fsdp", None, "rep", None),
-    )
-    out_specs = (P("fsdp", None, "rep", None), P("fsdp", None, "rep", None), P(None, "fsdp", "rep"))
-    return jax.shard_map(on_device, mesh=mesh, in_specs=in_specs, out_specs=out_specs, check_vma=False)
+    nz = 32
+    nf, nrep = mesh.shape["fsdp"], mesh.shape["rep"]
+    mesh = Mesh(mesh.devices.reshape(nf // nz, nz, nrep // 2, 2), FSDP + REP)
+    held = P(FSDP, None, REP, None)
+    return jax.shard_map(
+        on_device, mesh=mesh, in_specs=(P(REP, None, FSDP, None), P(), held, held, held, held),
+        out_specs=(held, held, P(None, FSDP, REP)), check_vma=False)

time: 144 us -> 142 us (0.986)
  starting transfers between devices: 69.9 us -> 66.3 us
  Pallas kernels: 3.71 us -> 5.62 us
  matrix products: 4.09 us -> 2.28 us
    all_to_all x4, starting transfers between devices: 50 us -> 46.9 us  [the longest x1 17.7 us: on_device(): lax.all_to_all(code_call(x, nrep), REP, split_axis=0, concat_axis=0, tile...]
    pallas_call x0 -> x2, Pallas kernels: none -> 1.91 us  [the longest x1 0.99 us: pick_call(): pl.pallas_call(pick_kernel, out_shape=jax.ShapeDtypeStruct((rows, back.sh...]
    dot_general x2 -> x0, matrix products: 1.79 us -> none  [the longest x1 0.9 us: on_device(): jnp.einsum('bfs,frsc->brc', pick, back.reshape(nf, rows, SLOTS, slab), pr...]
where the time goes in v5:
time: 142 us; the launch traced here: 141 us
  starting transfers between devices  66.3 us (47%)
  waiting for transfers between devices  62.6 us (44%)
  Pallas kernels  5.62 us (4%)
  local copies, waits for them, and re-layouts  2.75 us (2%)
  matrix products  2.28 us (2%)
    all_to_all x1, waiting for transfers between devices, on_device(): back = lax.all_to_all(packed, FSDP, split_axis=0, concat_axis=0, tiled=True)  27 us
    all_to_all x1, starting transfers between devices, on_device(): lax.all_to_all(code_call(x, nrep), REP, split_axis=0, concat_axis=0, tile...  17.7 us
    all_to_all x1, starting transfers between devices, on_device(): lax.all_to_all(outgoing, 'z', split_axis=0, concat_axis=0, tiled=True)  17 us
    all_to_all x1, waiting for transfers between devices, on_device(): lax.all_to_all(outgoing, 'z', split_axis=0, concat_axis=0, tiled=True)  16.1 us
    all_to_all x1, waiting for transfers between devices, on_device(): lax.all_to_all(code_call(x, nrep), REP, split_axis=0, concat_axis=0, tile...  9.2 us
    ppermute x3, starting transfers between devices, on_device(): lax.ppermute(own, 'y', [(j, (j + d) % groups) for j in range(groups)])  8.42 us
    all_to_all x1, starting transfers between devices, on_device(): back = lax.all_to_all(packed, FSDP, split_axis=0, concat_axis=0, tiled=True)  7.42 us
    ppermute x1, starting transfers between devices, on_device(): other = lax.ppermute(mine, 'core', swap)  6.06 us
  transfers between devices with their start and end apart: 9, of which 7 were waited for; matrix products, arithmetic and copies ran while one was open for 2% of the time, Pallas kernels for 0%

profile of v5, /device:TPU:1, one launch (start us, length us, event | category | flops | bytes accessed | tf_op | source)
XLA Modules:
  0.0 141.2 jit_solution(14507301520325715974)
XLA Ops:
  0.6 0.0 copy-start
  0.6 1.0 copy-done
  1.7 1.6 %shard_map.85 = bf16[8,256,128]{2,1,0:T(8,128)(2,1)} custom-call(bf16[128,4,512]{2,1,0:T(4,128)(2,1)S(1)} %bitcast.29), custom_call_target="tpu_custom_call" | custom-call | tf_op jit(solution)/shard_map/pallas_call | solution.py:126
  3.3 0.0 copy-start.5
  3.3 17.7 %all-to-all-start = ((bf16[8,256,128]{2,1,0:T(8,128)(2,1)}), bf16[8,256,128]{2,1,0:T(8,128)(2,1)S(1)}, u32[]{:S(2)}, u32[]{:S(2)}) async-start(bf16[8,256,128]{2,1,0:T(8,128)(2,1)} %shard_map.85), calls=%async_computation | async-start | bytes 1048576 | tf_op jit(solution)/shard_map/all_to_all | solution.py:180
  21.0 0.0 copy-done.5
  21.0 0.2 convert_reduce_fusion
  21.2 0.1 fusion.4.route_ref
  21.3 9.2 %all-to-all-done.got_ref = bf16[8,256,128]{2,1,0:T(8,128)(2,1)S(1)} async-done(((bf16[8,256,128]{2,1,0:T(8,128)(2,1)}), bf16[8,256,128]{2,1,0:T(8,128)(2,1)S(1)}, u32[]{:S(2)}, u32[]{:S(2)}) %all-to-all-start) | async-done | bytes 524320 | tf_op jit(solution)/shard_map/all_to_all | solution.py:180
  30.5 0.9 shard_map.86
  31.4 0.0 copy-start.4
  31.4 17.0 %all-to-all-start.1 = ((bf16[32,16,128]{2,1,0:T(8,128)(2,1)}), bf16[32,16,128]{2,1,0:T(8,128)(2,1)S(1)}, u32[]{:S(2)}, u32[]{:S(2)}) async-start(bf16[32,16,128]{2,1,0:T(8,128)(2,1)} %bitcast.3), calls=%async_computation.1 | async-start | bytes 262144 | tf_op jit(solution)/shard_map/all_to_all | solution.py:191
  48.4 0.0 copy-done.4
  48.4 2.2 %collective-permute-start = (bf16[128,512]{1,0:T(8,128)(2,1)S(1)}, bf16[128,512]{1,0:T(8,128)(2,1)S(1)}, u32[]{:S(2)}, u32[]{:S(2)}) collective-permute-start(bf16[128,512]{1,0:T(8,128)(2,1)S(1)} %bitcast.33), channel_id=1, source_target_pairs={{0,2},{2,4},{4,6},{6,0},{1,3},{3,5},{5,7},{7,1},{8,10},{10,12},{12... | collective-permute-start | bytes 393224 | tf_op jit(solution)/shard_map/ppermute | solution.py:195
  50.6 3.7 %collective-permute-start.1 = (bf16[128,512]{1,0:T(8,128)(2,1)S(1)}, bf16[128,512]{1,0:T(8,128)(2,1)S(1)}, u32[]{:S(2)}, u32[]{:S(2)}) collective-permute-start(bf16[128,512]{1,0:T(8,128)(2,1)S(1)} %bitcast.34), channel_id=1, source_target_pairs={{0,4},{2,6},{4,0},{6,2},{1,5},{3,7},{5,1},{7,3},{8,12},{10,14},{12... | collective-permute-start | bytes 393224 | tf_op jit(solution)/shard_map/ppermute | solution.py:195
  54.3 2.5 %collective-permute-start.2 = (bf16[128,512]{1,0:T(8,128)(2,1)S(1)}, bf16[128,512]{1,0:T(8,128)(2,1)S(1)}, u32[]{:S(2)}, u32[]{:S(2)}) collective-permute-start(bf16[128,512]{1,0:T(8,128)(2,1)S(1)} %bitcast.35), channel_id=1, source_target_pairs={{0,6},{2,0},{4,2},{6,4},{1,7},{3,1},{5,3},{7,5},{8,14},{10,8},{12,... | collective-permute-start | bytes 393224 | tf_op jit(solution)/shard_map/ppermute | solution.py:195
  56.8 0.0 collective-permute-done
  56.8 1.3 collective-permute-done.1
  58.2 3.6 %collective-permute-done.2 = bf16[128,512]{1,0:T(8,128)(2,1)S(1)} collective-permute-done((bf16[128,512]{1,0:T(8,128)(2,1)S(1)}, bf16[128,512]{1,0:T(8,128)(2,1)S(1)}, u32[]{:S(2)}, u32[]{:S(2)}) %collective-permute-start.2) | collective-permute-done | bytes 131104 | tf_op jit(solution)/shard_map/ppermute | solution.py:195
  61.7 16.1 %all-to-all-done.1 = bf16[32,16,128]{2,1,0:T(8,128)(2,1)S(1)} async-done(((bf16[32,16,128]{2,1,0:T(8,128)(2,1)}), bf16[32,16,128]{2,1,0:T(8,128)(2,1)S(1)}, u32[]{:S(2)}, u32[]{:S(2)}) %all-to-all-start.1) | async-done | bytes 131104 | tf_op jit(solution)/shard_map/all_to_all | solution.py:191
  77.9 0.9 broadcast_in_dim.14
  78.8 4.8 %all-to-all-start.2 = ((bf16[16,128,128]{2,1,0:T(8,128)(2,1)}), bf16[16,128,128]{2,1,0:T(8,128)(2,1)S(1)}, u32[]{:S(2)}, u32[]{:S(2)}) async-start(bf16[16,128,128]{2,1,0:T(8,128)(2,1)} %bitcast.9), calls=%async_computation.2 | async-start | bytes 1048576 | tf_op jit(solution)/shard_map/all_to_all | solution.py:204
  83.6 0.0 copy-start.1
  83.6 0.1 pad_maximum_fusion.hops_ref
  83.7 4.9 %collective-permute-start.4 = (bf16[4,128,512]{2,1,0:T(8,128)(2,1)S(1)}, bf16[4,128,512]{2,1,0:T(8,128)(2,1)S(1)}, u32[]{:S(2)}, u32[]{:S(2)}) collective-permute-start(bf16[4,128,512]{2,1,0:T(8,128)(2,1)S(1)} %pad_maximum_fusion.hops_ref), channel_id=1, source_target_pairs={{0,1},{1,0},{2,3},{3,2},{4,5},{5,4},{6,7},{7,6},{8,9},{9,8},{10,11... | collective-permute-start | bytes 1572872 | tf_op jit(solution)/shard_map/ppermute | solution.py:199
  88.6 3.9 %all-to-all-done.2.mine_ref = bf16[16,128,128]{2,1,0:T(8,128)(2,1)S(1)} async-done(((bf16[16,128,128]{2,1,0:T(8,128)(2,1)}), bf16[16,128,128]{2,1,0:T(8,128)(2,1)S(1)}, u32[]{:S(2)}, u32[]{:S(2)}) %all-to-all-start.2) | async-done | bytes 524320 | tf_op jit(solution)/shard_map/all_to_all | solution.py:204
  92.6 6.1 %collective-permute-start.3 = (bf16[16,128,128]{2,1,0:T(8,128)(2,1)S(1)}, bf16[16,128,128]{2,1,0:T(8,128)(2,1)S(1)}, u32[]{:S(2)}, u32[]{:S(2)}) collective-permute-start(bf16[16,128,128]{2,1,0:T(8,128)(2,1)S(1)} %all-to-all-done.2.mine_ref), channel_id=1, source_target_pairs={{0,1},{1,0},{2,3},{3,2},{4,5},{5,4},{6,7},{7,6},{8,9},{9,8},{10,11... | collective-permute-start | bytes 1572872 | tf_op jit(solution)/shard_map/ppermute | solution.py:205
  98.7 0.0 collective-permute-done.4.swapped_ref
  98.7 1.5 %collective-permute-done.3.other_ref = bf16[16,128,128]{2,1,0:T(8,128)(2,1)S(1)} collective-permute-done((bf16[16,128,128]{2,1,0:T(8,128)(2,1)S(1)}, bf16[16,128,128]{2,1,0:T(8,128)(2,1)S(1)}, u32[]{:S(2)}, u32[]{:S(2)}) %collective-permute-start.3) | collective-permute-done | bytes 524320 | tf_op jit(solution)/shard_map/ppermute | solution.py:205
  100.1 0.0 copy-done.1
  100.1 2.1 %shard_map.87 = (bf16[2,512,512]{2,1,0:T(8,128)(2,1)S(1)}, bf16[512,128]{1,0:T(8,128)(2,1)}) custom-call(s32[1]{0:T(128)} %bitcast.1.rank_ref, bf16[16,128,128]{2,1,0:T(8,128)(2,1)S(1)} %all-to-all-done.2.mine_ref, bf16[16,128,128]{2,1,0:T(8,128)(2,1)S(1)} %collective-permute-done.3.other_ref, bf16[4,128,512]{2,1,0:T(8,128)(2,1)S(1)} %pad_maximum_fusion.hops_ref, ...), custom_call_target="tpu_custom_call" | custom-call | tf_op jit(solution)/shard_map/pallas_call | solution.py:158
  102.2 7.4 %all-to-all-start.3 = ((bf16[128,4,128]{2,1,0:T(4,128)(2,1)}), bf16[128,4,128]{2,1,0:T(4,128)(2,1)S(1)}, u32[]{:S(2)}, u32[]{:S(2)}) async-start(bf16[128,4,128]{2,1,0:T(4,128)(2,1)} %bitcast.18), calls=%async_computation.3 | async-start | bytes 262144 | tf_op jit(solution)/shard_map/all_to_all | solution.py:208
  109.7 0.2 iota_compare_fusion
  109.9 0.2 iota_compare_fusion.1
  110.0 0.0 copy-start.2
  110.0 0.2 add_convert_fusion.pick_ref
  110.2 0.7 copy-done.2
  111.0 0.0 copy-start.3
  111.0 1.1 fusion.1
  112.1 0.0 copy-done.3
  112.1 1.1 fusion.3
  113.3 27.0 %all-to-all-done.3 = bf16[128,4,128]{2,1,0:T(4,128)(2,1)S(1)} async-done(((bf16[128,4,128]{2,1,0:T(4,128)(2,1)}), bf16[128,4,128]{2,1,0:T(4,128)(2,1)S(1)}, u32[]{:S(2)}, u32[]{:S(2)}) %all-to-all-start.3) | async-done | bytes 131104 | tf_op jit(solution)/shard_map/all_to_all | solution.py:208
  140.2 1.0 shard_map.88
  (6 shorter events, 0.1 us)
Async XLA Ops:
  0.6 1.0 copy-start
  3.3 17.7 %copy-start.5 = (s32[128]{0:T(128)S(1)}, s32[128]{0:T(128)}, u32[]{:S(2)}) copy-start(s32[128]{0:T(128)} %param.7) | copy-start | bytes 1540
  3.3 27.2 %all-to-all-start = ((bf16[8,256,128]{2,1,0:T(8,128)(2,1)}), bf16[8,256,128]{2,1,0:T(8,128)(2,1)S(1)}, u32[]{:S(2)}, u32[]{:S(2)}) async-start(bf16[8,256,128]{2,1,0:T(8,128)(2,1)} %shard_map.85), calls=%async_computation | async-start | bytes 1048576 | tf_op jit(solution)/shard_map/all_to_all | solution.py:180
  31.4 17.0 %copy-start.4 = (bf16[1,2,64,512]{3,2,1,0:T(8,128)(2,1)S(1)}, bf16[1,2,64,512]{3,2,1,0:T(8,128)(2,1)}, u32[]{:S(2)}) copy-start(bf16[1,2,64,512]{3,2,1,0:T(8,128)(2,1)} %param.10) | copy-start | bytes 393220
  31.4 46.5 %all-to-all-start.1 = ((bf16[32,16,128]{2,1,0:T(8,128)(2,1)}), bf16[32,16,128]{2,1,0:T(8,128)(2,1)S(1)}, u32[]{:S(2)}, u32[]{:S(2)}) async-start(bf16[32,16,128]{2,1,0:T(8,128)(2,1)} %bitcast.3), calls=%async_computation.1 | async-start | bytes 262144 | tf_op jit(solution)/shard_map/all_to_all | solution.py:191
  48.4 8.4 %collective-permute-start = (bf16[128,512]{1,0:T(8,128)(2,1)S(1)}, bf16[128,512]{1,0:T(8,128)(2,1)S(1)}, u32[]{:S(2)}, u32[]{:S(2)}) collective-permute-start(bf16[128,512]{1,0:T(8,128)(2,1)S(1)} %bitcast.33), channel_id=1, source_target_pairs={{0,2},{2,4},{4,6},{6,0},{1,3},{3,5},{5,7},{7,1},{8,10},{10,12},{12... | collective-permute-start | bytes 393224 | tf_op jit(solution)/shard_map/ppermute | solution.py:195
  50.6 7.6 %collective-permute-start.1 = (bf16[128,512]{1,0:T(8,128)(2,1)S(1)}, bf16[128,512]{1,0:T(8,128)(2,1)S(1)}, u32[]{:S(2)}, u32[]{:S(2)}) collective-permute-start(bf16[128,512]{1,0:T(8,128)(2,1)S(1)} %bitcast.34), channel_id=1, source_target_pairs={{0,4},{2,6},{4,0},{6,2},{1,5},{3,7},{5,1},{7,3},{8,12},{10,14},{12... | collective-permute-start | bytes 393224 | tf_op jit(solution)/shard_map/ppermute | solution.py:195
  54.3 7.4 %collective-permute-start.2 = (bf16[128,512]{1,0:T(8,128)(2,1)S(1)}, bf16[128,512]{1,0:T(8,128)(2,1)S(1)}, u32[]{:S(2)}, u32[]{:S(2)}) collective-permute-start(bf16[128,512]{1,0:T(8,128)(2,1)S(1)} %bitcast.35), channel_id=1, source_target_pairs={{0,6},{2,0},{4,2},{6,4},{1,7},{3,1},{5,3},{7,5},{8,14},{10,8},{12,... | collective-permute-start | bytes 393224 | tf_op jit(solution)/shard_map/ppermute | solution.py:195
  78.8 13.7 %all-to-all-start.2 = ((bf16[16,128,128]{2,1,0:T(8,128)(2,1)}), bf16[16,128,128]{2,1,0:T(8,128)(2,1)S(1)}, u32[]{:S(2)}, u32[]{:S(2)}) async-start(bf16[16,128,128]{2,1,0:T(8,128)(2,1)} %bitcast.9), calls=%async_computation.2 | async-start | bytes 1048576 | tf_op jit(solution)/shard_map/all_to_all | solution.py:204
  83.6 16.5 %copy-start.1 = (bf16[1,2,64,512]{3,2,1,0:T(8,128)(2,1)S(1)}, bf16[1,2,64,512]{3,2,1,0:T(8,128)(2,1)}, u32[]{:S(2)}) copy-start(bf16[1,2,64,512]{3,2,1,0:T(8,128)(2,1)} %param.11) | copy-start | bytes 393220
  83.7 15.0 %collective-permute-start.4 = (bf16[4,128,512]{2,1,0:T(8,128)(2,1)S(1)}, bf16[4,128,512]{2,1,0:T(8,128)(2,1)S(1)}, u32[]{:S(2)}, u32[]{:S(2)}) collective-permute-start(bf16[4,128,512]{2,1,0:T(8,128)(2,1)S(1)} %pad_maximum_fusion.hops_ref), channel_id=1, source_target_pairs={{0,1},{1,0},{2,3},{3,2},{4,5},{5,4},{6,7},{7,6},{8,9},{9,8},{10,11... | collective-permute-start | bytes 1572872 | tf_op jit(solution)/shard_map/ppermute | solution.py:199
  92.6 7.6 %collective-permute-start.3 = (bf16[16,128,128]{2,1,0:T(8,128)(2,1)S(1)}, bf16[16,128,128]{2,1,0:T(8,128)(2,1)S(1)}, u32[]{:S(2)}, u32[]{:S(2)}) collective-permute-start(bf16[16,128,128]{2,1,0:T(8,128)(2,1)S(1)} %all-to-all-done.2.mine_ref), channel_id=1, source_target_pairs={{0,1},{1,0},{2,3},{3,2},{4,5},{5,4},{6,7},{7,6},{8,9},{9,8},{10,11... | collective-permute-start | bytes 1572872 | tf_op jit(solution)/shard_map/ppermute | solution.py:205
  102.2 38.0 %all-to-all-start.3 = ((bf16[128,4,128]{2,1,0:T(4,128)(2,1)}), bf16[128,4,128]{2,1,0:T(4,128)(2,1)S(1)}, u32[]{:S(2)}, u32[]{:S(2)}) async-start(bf16[128,4,128]{2,1,0:T(4,128)(2,1)} %bitcast.18), calls=%async_computation.3 | async-start | bytes 262144 | tf_op jit(solution)/shard_map/all_to_all | solution.py:208
  110.0 1.0 copy-start.2
  111.0 1.1 copy-start.3

commit v6 on v5

--- a/solution.py
+++ b/solution.py
@@ -7,6 +7,7 @@
 
 GROUP = 128
 SLOTS = 2
+FAR = (16, 16)
 FSDP, REP = ("x", "z"), ("y", "core")
 DECAY = 0.95
 NORM = GROUP ** (-0.5)
@@ -87,7 +88,7 @@
     o = lax.broadcasted_iota(I32, (256, 256), 0)
     i = lax.broadcasted_iota(I32, (256, 256), 1)
     half = jnp.where(i < 128, core, 1 - core)
-    from_row = ((i % 128) // 4) * 4 + half * 2 + i % 2
+    from_row = (((i % 128) // 4) ^ FAR[0]) * 4 + half * 2 + i % 2
     perm = ((o % 128 == from_row) & (o // 128 == (i // 2) % 2)).astype(F32).astype(BF)
     tiles = width // 128
     placed = []
@@ -107,7 +108,7 @@
             left = ref[:, s * slab:(s + 1) * slab, :].reshape(groups * slab, width)
             rows = mm(left, middles[s]).astype(BF)
             for d in range(groups):
-                start = ((chip + groups - d) % groups * 2 + (core + k) % 2) * slab
+                start = ((chip + groups - d) % groups * 2 + (core + k + FAR[1] // 16) % 2) * slab
                 out_ref[pl.ds(pl.multiple_of(start, slab), slab), s * slab:(s + 1) * slab] = (
                     rows[d * slab:(d + 1) * slab])
 
@@ -182,13 +183,14 @@
     counter = jnp.arange(nb, dtype=I32)
     same = owner[:, None] == owner[None, :]
     slot_of = jnp.sum(same & (counter[None, :] < counter[:, None]), axis=1)
-    place = ((owner % nz) * nx + owner // nz) * SLOTS + slot_of
+    place = (((owner ^ FAR[0]) % nz) * nx + owner // nz) * SLOTS + slot_of
     key_in = jnp.concatenate([place * per + r for r in range(per)])
     route = (jnp.arange(nf * SLOTS * per, dtype=I32)[:, None] == key_in[None, :]).astype(BF)
     outgoing = route_call(got, route).reshape(nz, nx * SLOTS * per, GROUP)
 
     outgoing, own = lax.optimization_barrier((outgoing, left_root[0]))
-    arrived = lax.all_to_all(outgoing, "z", split_axis=0, concat_axis=0, tiled=True)
+    arrived = lax.all_to_all(outgoing, "z", split_axis=0, concat_axis=0, tiled=True,
+                             axis_index_groups=[[p ^ FAR[0] for p in range(nz)]])
     own = own.reshape(SLOTS * slab, width)
     hops = [own]
     for d in range(1, groups):
@@ -205,7 +207,8 @@
     other = lax.ppermute(mine, "core", swap)
     gradient, direction = root_call(rank.reshape(1), mine, other, hops, swapped, right_root[0])
     packed = direction.reshape(nf, rows, SLOTS * slab)
-    back = lax.all_to_all(packed, FSDP, split_axis=0, concat_axis=0, tiled=True)
+    back = lax.all_to_all(packed, FSDP, split_axis=0, concat_axis=0, tiled=True,
+                          axis_index_groups=[[p ^ FAR[1] for p in range(nf)]])
 
     own_rows = lax.dynamic_slice_in_dim(gradient, rank * slab, slab, axis=1)
     own_cols = lax.dynamic_slice_in_dim(gradient, rank * slab, slab, axis=2)
@@ -217,7 +220,7 @@
     owner_row = jnp.arange(nf * rows, dtype=I32)
     pick = []
     for s in range(SLOTS):
-        key = jnp.where(slot_of == s, owner * rows, -rows)
+        key = jnp.where(slot_of == s, (owner ^ FAR[1]) * rows, -rows)
         key = jnp.concatenate([key + r for r in range(rows)])
         pick.append((owner_row[:, None] == key[None, :]).astype(BF))
     update = pick_call(back.reshape(nf * rows, SLOTS * slab), jnp.stack(pick), rows).transpose(2, 0, 1)

time: 142 us -> 132 us (0.930)
  waiting for transfers between devices: 62.6 us -> 30.9 us
  starting transfers between devices: 66.3 us -> 87.9 us
    all_to_all x2, waiting for transfers between devices: 43.1 us -> 10.7 us  [the longest x1 10.7 us: on_device(): lax.all_to_all(packed, FSDP, split_axis=0, concat_axis=0, tiled=True, axi...]
    all_to_all x2, starting transfers between devices: 24.4 us -> 46.8 us  [the longest x1 23.9 us: on_device(): lax.all_to_all(outgoing, 'z', split_axis=0, concat_axis=0, tiled=True, ax...]
  transfers between devices with their start and end apart: 9 -> 9, of which waited for: 7 -> 6; matrix products, arithmetic and copies ran while one was open for 2% -> 2% of each run, Pallas kernels for 0% -> 0%
where the time goes in v6:
time: 132 us; the launch traced here: 131 us
  starting transfers between devices  87.9 us (67%)
  waiting for transfers between devices  30.9 us (23%)
  Pallas kernels  5.62 us (4%)
  local copies, waits for them, and re-layouts  2.75 us (2%)
  matrix products  2.28 us (2%)
    all_to_all x1, starting transfers between devices, on_device(): lax.all_to_all(outgoing, 'z', split_axis=0, concat_axis=0, tiled=True, ax...  23.9 us
    all_to_all x1, starting transfers between devices, on_device(): lax.all_to_all(packed, FSDP, split_axis=0, concat_axis=0, tiled=True, axi...  23 us
    all_to_all x1, starting transfers between devices, on_device(): lax.all_to_all(code_call(x, nrep), REP, split_axis=0, concat_axis=0, tile...  17.7 us
    all_to_all x1, waiting for transfers between devices, on_device(): lax.all_to_all(packed, FSDP, split_axis=0, concat_axis=0, tiled=True, axi...  10.7 us
    all_to_all x1, waiting for transfers between devices, on_device(): lax.all_to_all(code_call(x, nrep), REP, split_axis=0, concat_axis=0, tile...  9.2 us
    ppermute x3, starting transfers between devices, on_device(): lax.ppermute(own, 'y', [(j, (j + d) % groups) for j in range(groups)])  8.42 us
    ppermute x1, starting transfers between devices, on_device(): other = lax.ppermute(mine, 'core', swap)  5.34 us
    all_to_all x1, starting transfers between devices, on_device(): lax.all_to_all(copies, ('x', 'y'), split_axis=0, concat_axis=0, tiled=True)  5.17 us
  transfers between devices with their start and end apart: 9, of which 6 were waited for; matrix products, arithmetic and copies ran while one was open for 2% of the time, Pallas kernels for 0%

profile of v6, /device:TPU:1, one launch (start us, length us, event | category | flops | bytes accessed | tf_op | source)
XLA Modules:
  0.0 131.2 jit_solution(5113441996547264558)
XLA Ops:
  0.6 0.0 copy-start
  0.6 1.0 copy-done
  1.7 1.6 %shard_map.85 = bf16[8,256,128]{2,1,0:T(8,128)(2,1)} custom-call(bf16[128,4,512]{2,1,0:T(4,128)(2,1)S(1)} %bitcast.29), custom_call_target="tpu_custom_call" | custom-call | tf_op jit(solution)/shard_map/pallas_call | solution.py:127
  3.3 0.0 copy-start.5
  3.3 17.7 %all-to-all-start = ((bf16[8,256,128]{2,1,0:T(8,128)(2,1)}), bf16[8,256,128]{2,1,0:T(8,128)(2,1)S(1)}, u32[]{:S(2)}, u32[]{:S(2)}) async-start(bf16[8,256,128]{2,1,0:T(8,128)(2,1)} %shard_map.85), calls=%async_computation | async-start | bytes 1048576 | tf_op jit(solution)/shard_map/all_to_all | solution.py:181
  21.0 0.0 copy-done.5
  21.0 0.2 convert_reduce_fusion
  21.2 0.1 fusion.4.route_ref
  21.3 9.2 %all-to-all-done.got_ref = bf16[8,256,128]{2,1,0:T(8,128)(2,1)S(1)} async-done(((bf16[8,256,128]{2,1,0:T(8,128)(2,1)}), bf16[8,256,128]{2,1,0:T(8,128)(2,1)S(1)}, u32[]{:S(2)}, u32[]{:S(2)}) %all-to-all-start) | async-done | bytes 524320 | tf_op jit(solution)/shard_map/all_to_all | solution.py:181
  30.5 0.9 shard_map.86
  31.4 0.0 copy-start.4
  31.4 23.9 %all-to-all-start.1 = ((bf16[32,16,128]{2,1,0:T(8,128)(2,1)}), bf16[32,16,128]{2,1,0:T(8,128)(2,1)S(1)}, u32[]{:S(2)}, u32[]{:S(2)}) async-start(bf16[32,16,128]{2,1,0:T(8,128)(2,1)} %bitcast.3), calls=%async_computation.1 | async-start | bytes 262144 | tf_op jit(solution)/shard_map/all_to_all | solution.py:192
  55.3 0.0 copy-done.4
  55.3 2.2 %collective-permute-start = (bf16[128,512]{1,0:T(8,128)(2,1)S(1)}, bf16[128,512]{1,0:T(8,128)(2,1)S(1)}, u32[]{:S(2)}, u32[]{:S(2)}) collective-permute-start(bf16[128,512]{1,0:T(8,128)(2,1)S(1)} %bitcast.33), channel_id=1, source_target_pairs={{0,2},{2,4},{4,6},{6,0},{1,3},{3,5},{5,7},{7,1},{8,10},{10,12},{12... | collective-permute-start | bytes 393224 | tf_op jit(solution)/shard_map/ppermute | solution.py:197
  57.5 3.7 %collective-permute-start.1 = (bf16[128,512]{1,0:T(8,128)(2,1)S(1)}, bf16[128,512]{1,0:T(8,128)(2,1)S(1)}, u32[]{:S(2)}, u32[]{:S(2)}) collective-permute-start(bf16[128,512]{1,0:T(8,128)(2,1)S(1)} %bitcast.34), channel_id=1, source_target_pairs={{0,4},{2,6},{4,0},{6,2},{1,5},{3,7},{5,1},{7,3},{8,12},{10,14},{12... | collective-permute-start | bytes 393224 | tf_op jit(solution)/shard_map/ppermute | solution.py:197
  61.2 2.5 %collective-permute-start.2 = (bf16[128,512]{1,0:T(8,128)(2,1)S(1)}, bf16[128,512]{1,0:T(8,128)(2,1)S(1)}, u32[]{:S(2)}, u32[]{:S(2)}) collective-permute-start(bf16[128,512]{1,0:T(8,128)(2,1)S(1)} %bitcast.35), channel_id=1, source_target_pairs={{0,6},{2,0},{4,2},{6,4},{1,7},{3,1},{5,3},{7,5},{8,14},{10,8},{12,... | collective-permute-start | bytes 393224 | tf_op jit(solution)/shard_map/ppermute | solution.py:197
  63.7 0.0 collective-permute-done
  63.7 1.5 %collective-permute-done.1 = bf16[128,512]{1,0:T(8,128)(2,1)S(1)} collective-permute-done((bf16[128,512]{1,0:T(8,128)(2,1)S(1)}, bf16[128,512]{1,0:T(8,128)(2,1)S(1)}, u32[]{:S(2)}, u32[]{:S(2)}) %collective-permute-start.1) | collective-permute-done | bytes 131104 | tf_op jit(solution)/shard_map/ppermute | solution.py:197
  65.2 3.4 %collective-permute-done.2 = bf16[128,512]{1,0:T(8,128)(2,1)S(1)} collective-permute-done((bf16[128,512]{1,0:T(8,128)(2,1)S(1)}, bf16[128,512]{1,0:T(8,128)(2,1)S(1)}, u32[]{:S(2)}, u32[]{:S(2)}) %collective-permute-start.2) | collective-permute-done | bytes 131104 | tf_op jit(solution)/shard_map/ppermute | solution.py:197
  68.6 0.0 all-to-all-done.1
  68.6 0.9 broadcast_in_dim.14
  69.5 5.2 %all-to-all-start.2 = ((bf16[16,128,128]{2,1,0:T(8,128)(2,1)}), bf16[16,128,128]{2,1,0:T(8,128)(2,1)S(1)}, u32[]{:S(2)}, u32[]{:S(2)}) async-start(bf16[16,128,128]{2,1,0:T(8,128)(2,1)} %bitcast.9), calls=%async_computation.2 | async-start | bytes 1048576 | tf_op jit(solution)/shard_map/all_to_all | solution.py:206
  74.7 0.0 copy-start.1
  74.7 0.1 pad_maximum_fusion.hops_ref
  74.8 4.5 %collective-permute-start.4 = (bf16[4,128,512]{2,1,0:T(8,128)(2,1)S(1)}, bf16[4,128,512]{2,1,0:T(8,128)(2,1)S(1)}, u32[]{:S(2)}, u32[]{:S(2)}) collective-permute-start(bf16[4,128,512]{2,1,0:T(8,128)(2,1)S(1)} %pad_maximum_fusion.hops_ref), channel_id=1, source_target_pairs={{0,1},{1,0},{2,3},{3,2},{4,5},{5,4},{6,7},{7,6},{8,9},{9,8},{10,11... | collective-permute-start | bytes 1572872 | tf_op jit(solution)/shard_map/ppermute | solution.py:201
  79.3 4.6 %all-to-all-done.2.mine_ref = bf16[16,128,128]{2,1,0:T(8,128)(2,1)S(1)} async-done(((bf16[16,128,128]{2,1,0:T(8,128)(2,1)}), bf16[16,128,128]{2,1,0:T(8,128)(2,1)S(1)}, u32[]{:S(2)}, u32[]{:S(2)}) %all-to-all-start.2) | async-done | bytes 524320 | tf_op jit(solution)/shard_map/all_to_all | solution.py:206
  84.0 5.3 %collective-permute-start.3 = (bf16[16,128,128]{2,1,0:T(8,128)(2,1)S(1)}, bf16[16,128,128]{2,1,0:T(8,128)(2,1)S(1)}, u32[]{:S(2)}, u32[]{:S(2)}) collective-permute-start(bf16[16,128,128]{2,1,0:T(8,128)(2,1)S(1)} %all-to-all-done.2.mine_ref), channel_id=1, source_target_pairs={{0,1},{1,0},{2,3},{3,2},{4,5},{5,4},{6,7},{7,6},{8,9},{9,8},{10,11... | collective-permute-start | bytes 1572872 | tf_op jit(solution)/shard_map/ppermute | solution.py:207
  89.3 0.0 collective-permute-done.4.swapped_ref
  89.3 1.5 %collective-permute-done.3.other_ref = bf16[16,128,128]{2,1,0:T(8,128)(2,1)S(1)} collective-permute-done((bf16[16,128,128]{2,1,0:T(8,128)(2,1)S(1)}, bf16[16,128,128]{2,1,0:T(8,128)(2,1)S(1)}, u32[]{:S(2)}, u32[]{:S(2)}) %collective-permute-start.3) | collective-permute-done | bytes 524320 | tf_op jit(solution)/shard_map/ppermute | solution.py:207
  90.8 0.0 copy-done.1
  90.8 2.1 %shard_map.87 = (bf16[2,512,512]{2,1,0:T(8,128)(2,1)S(1)}, bf16[512,128]{1,0:T(8,128)(2,1)}) custom-call(s32[1]{0:T(128)} %bitcast.1.rank_ref, bf16[16,128,128]{2,1,0:T(8,128)(2,1)S(1)} %all-to-all-done.2.mine_ref, bf16[16,128,128]{2,1,0:T(8,128)(2,1)S(1)} %collective-permute-done.3.other_ref, bf16[4,128,512]{2,1,0:T(8,128)(2,1)S(1)} %pad_maximum_fusion.hops_ref, ...), custom_call_target="tpu_custom_call" | custom-call | tf_op jit(solution)/shard_map/pallas_call | solution.py:159
  92.9 23.0 %all-to-all-start.3 = ((bf16[128,4,128]{2,1,0:T(4,128)(2,1)}), bf16[128,4,128]{2,1,0:T(4,128)(2,1)S(1)}, u32[]{:S(2)}, u32[]{:S(2)}) async-start(bf16[128,4,128]{2,1,0:T(4,128)(2,1)} %bitcast.18), calls=%async_computation.3 | async-start | bytes 262144 | tf_op jit(solution)/shard_map/all_to_all | solution.py:210
  115.9 0.2 iota_compare_fusion
  116.1 0.2 iota_compare_fusion.1
  116.2 0.0 copy-start.2
  116.3 0.2 add_convert_fusion.pick_ref
  116.5 0.7 copy-done.2
  117.2 0.0 copy-start.3
  117.2 1.1 fusion.1
  118.3 0.0 copy-done.3
  118.3 1.1 fusion.3
  119.5 10.7 %all-to-all-done.3 = bf16[128,4,128]{2,1,0:T(4,128)(2,1)S(1)} async-done(((bf16[128,4,128]{2,1,0:T(4,128)(2,1)}), bf16[128,4,128]{2,1,0:T(4,128)(2,1)S(1)}, u32[]{:S(2)}, u32[]{:S(2)}) %all-to-all-start.3) | async-done | bytes 131104 | tf_op jit(solution)/shard_map/all_to_all | solution.py:210
  130.2 1.0 shard_map.88
  (6 shorter events, 0.1 us)
Async XLA Ops:
  0.6 1.0 copy-start
  3.3 17.7 %copy-start.5 = (s32[128]{0:T(128)S(1)}, s32[128]{0:T(128)}, u32[]{:S(2)}) copy-start(s32[128]{0:T(128)} %param.7) | copy-start | bytes 1540
  3.3 27.2 %all-to-all-start = ((bf16[8,256,128]{2,1,0:T(8,128)(2,1)}), bf16[8,256,128]{2,1,0:T(8,128)(2,1)S(1)}, u32[]{:S(2)}, u32[]{:S(2)}) async-start(bf16[8,256,128]{2,1,0:T(8,128)(2,1)} %shard_map.85), calls=%async_computation | async-start | bytes 1048576 | tf_op jit(solution)/shard_map/all_to_all | solution.py:181
  31.4 23.9 %copy-start.4 = (bf16[1,2,64,512]{3,2,1,0:T(8,128)(2,1)S(1)}, bf16[1,2,64,512]{3,2,1,0:T(8,128)(2,1)}, u32[]{:S(2)}) copy-start(bf16[1,2,64,512]{3,2,1,0:T(8,128)(2,1)} %param.10) | copy-start | bytes 393220
  31.4 37.2 %all-to-all-start.1 = ((bf16[32,16,128]{2,1,0:T(8,128)(2,1)}), bf16[32,16,128]{2,1,0:T(8,128)(2,1)S(1)}, u32[]{:S(2)}, u32[]{:S(2)}) async-start(bf16[32,16,128]{2,1,0:T(8,128)(2,1)} %bitcast.3), calls=%async_computation.1 | async-start | bytes 262144 | tf_op jit(solution)/shard_map/all_to_all | solution.py:192
  55.3 8.5 %collective-permute-start = (bf16[128,512]{1,0:T(8,128)(2,1)S(1)}, bf16[128,512]{1,0:T(8,128)(2,1)S(1)}, u32[]{:S(2)}, u32[]{:S(2)}) collective-permute-start(bf16[128,512]{1,0:T(8,128)(2,1)S(1)} %bitcast.33), channel_id=1, source_target_pairs={{0,2},{2,4},{4,6},{6,0},{1,3},{3,5},{5,7},{7,1},{8,10},{10,12},{12... | collective-permute-start | bytes 393224 | tf_op jit(solution)/shard_map/ppermute | solution.py:197
  57.5 7.7 %collective-permute-start.1 = (bf16[128,512]{1,0:T(8,128)(2,1)S(1)}, bf16[128,512]{1,0:T(8,128)(2,1)S(1)}, u32[]{:S(2)}, u32[]{:S(2)}) collective-permute-start(bf16[128,512]{1,0:T(8,128)(2,1)S(1)} %bitcast.34), channel_id=1, source_target_pairs={{0,4},{2,6},{4,0},{6,2},{1,5},{3,7},{5,1},{7,3},{8,12},{10,14},{12... | collective-permute-start | bytes 393224 | tf_op jit(solution)/shard_map/ppermute | solution.py:197
  61.2 7.4 %collective-permute-start.2 = (bf16[128,512]{1,0:T(8,128)(2,1)S(1)}, bf16[128,512]{1,0:T(8,128)(2,1)S(1)}, u32[]{:S(2)}, u32[]{:S(2)}) collective-permute-start(bf16[128,512]{1,0:T(8,128)(2,1)S(1)} %bitcast.35), channel_id=1, source_target_pairs={{0,6},{2,0},{4,2},{6,4},{1,7},{3,1},{5,3},{7,5},{8,14},{10,8},{12,... | collective-permute-start | bytes 393224 | tf_op jit(solution)/shard_map/ppermute | solution.py:197
  69.5 14.4 %all-to-all-start.2 = ((bf16[16,128,128]{2,1,0:T(8,128)(2,1)}), bf16[16,128,128]{2,1,0:T(8,128)(2,1)S(1)}, u32[]{:S(2)}, u32[]{:S(2)}) async-start(bf16[16,128,128]{2,1,0:T(8,128)(2,1)} %bitcast.9), calls=%async_computation.2 | async-start | bytes 1048576 | tf_op jit(solution)/shard_map/all_to_all | solution.py:206
  74.7 16.1 %copy-start.1 = (bf16[1,2,64,512]{3,2,1,0:T(8,128)(2,1)S(1)}, bf16[1,2,64,512]{3,2,1,0:T(8,128)(2,1)}, u32[]{:S(2)}) copy-start(bf16[1,2,64,512]{3,2,1,0:T(8,128)(2,1)} %param.11) | copy-start | bytes 393220
  74.8 14.5 %collective-permute-start.4 = (bf16[4,128,512]{2,1,0:T(8,128)(2,1)S(1)}, bf16[4,128,512]{2,1,0:T(8,128)(2,1)S(1)}, u32[]{:S(2)}, u32[]{:S(2)}) collective-permute-start(bf16[4,128,512]{2,1,0:T(8,128)(2,1)S(1)} %pad_maximum_fusion.hops_ref), channel_id=1, source_target_pairs={{0,1},{1,0},{2,3},{3,2},{4,5},{5,4},{6,7},{7,6},{8,9},{9,8},{10,11... | collective-permute-start | bytes 1572872 | tf_op jit(solution)/shard_map/ppermute | solution.py:201
  84.0 6.9 %collective-permute-start.3 = (bf16[16,128,128]{2,1,0:T(8,128)(2,1)S(1)}, bf16[16,128,128]{2,1,0:T(8,128)(2,1)S(1)}, u32[]{:S(2)}, u32[]{:S(2)}) collective-permute-start(bf16[16,128,128]{2,1,0:T(8,128)(2,1)S(1)} %all-to-all-done.2.mine_ref), channel_id=1, source_target_pairs={{0,1},{1,0},{2,3},{3,2},{4,5},{5,4},{6,7},{7,6},{8,9},{9,8},{10,11... | collective-permute-start | bytes 1572872 | tf_op jit(solution)/shard_map/ppermute | solution.py:207
  92.9 37.3 %all-to-all-start.3 = ((bf16[128,4,128]{2,1,0:T(4,128)(2,1)}), bf16[128,4,128]{2,1,0:T(4,128)(2,1)S(1)}, u32[]{:S(2)}, u32[]{:S(2)}) async-start(bf16[128,4,128]{2,1,0:T(4,128)(2,1)} %bitcast.18), calls=%async_computation.3 | async-start | bytes 262144 | tf_op jit(solution)/shard_map/all_to_all | solution.py:210
  116.2 1.0 copy-start.2
  117.2 1.1 copy-start.3

commit v7 on v6

--- a/solution.py
+++ b/solution.py
@@ -7,7 +7,7 @@
 
 GROUP = 128
 SLOTS = 2
-FAR = (16, 16)
+FAR = (20, 20)
 FSDP, REP = ("x", "z"), ("y", "core")
 DECAY = 0.95
 NORM = GROUP ** (-0.5)
@@ -109,8 +109,9 @@
             rows = mm(left, middles[s]).astype(BF)
             for d in range(groups):
                 start = ((chip + groups - d) % groups * 2 + (core + k + FAR[1] // 16) % 2) * slab
-                out_ref[pl.ds(pl.multiple_of(start, slab), slab), s * slab:(s + 1) * slab] = (
-                    rows[d * slab:(d + 1) * slab])
+                for b in range(slab // 16):
+                    place = pl.multiple_of(start + (b ^ (FAR[1] % 16 // 4)) * 16, 16)
+                    out_ref[pl.ds(place, 16), s * slab:(s + 1) * slab] = rows[d * slab + b * 16:d * slab + (b + 1) * 16]
 
 
 def kernel_params():

time: 132 us -> 131 us (level)
  starting transfers between devices: 87.9 us -> 80.1 us
  waiting for transfers between devices: 30.9 us -> 37.7 us
    all_to_all x1, starting transfers between devices: 23.9 us -> 19.1 us  [on_device(): lax.all_to_all(outgoing, 'z', split_axis=0, concat_axis=0, tiled=True, ax...]
    all_to_all x1, waiting for transfers between devices: 10.7 us -> 14.4 us  [on_device(): lax.all_to_all(packed, FSDP, split_axis=0, concat_axis=0, tiled=True, axi...]
    all_to_all x1, waiting for transfers between devices: 0.01 us -> 2.62 us  [on_device(): lax.all_to_all(outgoing, 'z', split_axis=0, concat_axis=0, tiled=True, ax...]
    all_to_all x1, starting transfers between devices: 23 us -> 21 us  [on_device(): lax.all_to_all(packed, FSDP, split_axis=0, concat_axis=0, tiled=True, axi...]
  transfers between devices with their start and end apart: 9 -> 9, of which waited for: 6 -> 7; matrix products, arithmetic and copies ran while one was open for 2% -> 2% of each run, Pallas kernels for 0% -> 0%
where the time goes in v7:
time: 131 us; the launch traced here: 130 us
  starting transfers between devices  80.1 us (61%)
  waiting for transfers between devices  37.7 us (29%)
  Pallas kernels  5.62 us (4%)
  local copies, waits for them, and re-layouts  2.75 us (2%)
  matrix products  2.28 us (2%)
    all_to_all x1, starting transfers between devices, on_device(): lax.all_to_all(packed, FSDP, split_axis=0, concat_axis=0, tiled=True, axi...  21 us
    all_to_all x1, starting transfers between devices, on_device(): lax.all_to_all(outgoing, 'z', split_axis=0, concat_axis=0, tiled=True, ax...  19.1 us
    all_to_all x1, starting transfers between devices, on_device(): lax.all_to_all(code_call(x, nrep), REP, split_axis=0, concat_axis=0, tile...  17.7 us
    all_to_all x1, waiting for transfers between devices, on_device(): lax.all_to_all(packed, FSDP, split_axis=0, concat_axis=0, tiled=True, axi...  14.4 us
    all_to_all x1, waiting for transfers between devices, on_device(): lax.all_to_all(code_call(x, nrep), REP, split_axis=0, concat_axis=0, tile...  9.2 us
    ppermute x3, starting transfers between devices, on_device(): lax.ppermute(own, 'y', [(j, (j + d) % groups) for j in range(groups)])  8.42 us
    ppermute x1, starting transfers between devices, on_device(): other = lax.ppermute(mine, 'core', swap)  5.13 us
    all_to_all x1, waiting for transfers between devices, on_device(): lax.all_to_all(copies, ('x', 'y'), split_axis=0, concat_axis=0, tiled=True)  5.08 us
  transfers between devices with their start and end apart: 9, of which 7 were waited for; matrix products, arithmetic and copies ran while one was open for 2% of the time, Pallas kernels for 0%

profile of v7, /device:TPU:1, one launch (start us, length us, event | category | flops | bytes accessed | tf_op | source)
XLA Modules:
  0.0 130.1 jit_solution(15198136476195084498)
XLA Ops:
  0.6 0.0 copy-start
  0.6 1.0 copy-done
  1.7 1.6 %shard_map.85 = bf16[8,256,128]{2,1,0:T(8,128)(2,1)} custom-call(bf16[128,4,512]{2,1,0:T(4,128)(2,1)S(1)} %bitcast.29), custom_call_target="tpu_custom_call" | custom-call | tf_op jit(solution)/shard_map/pallas_call | solution.py:128
  3.3 0.0 copy-start.5
  3.3 17.7 %all-to-all-start = ((bf16[8,256,128]{2,1,0:T(8,128)(2,1)}), bf16[8,256,128]{2,1,0:T(8,128)(2,1)S(1)}, u32[]{:S(2)}, u32[]{:S(2)}) async-start(bf16[8,256,128]{2,1,0:T(8,128)(2,1)} %shard_map.85), calls=%async_computation | async-start | bytes 1048576 | tf_op jit(solution)/shard_map/all_to_all | solution.py:182
  21.0 0.0 copy-done.5
  21.0 0.2 convert_reduce_fusion
  21.2 0.1 fusion.4.route_ref
  21.3 9.2 %all-to-all-done.got_ref = bf16[8,256,128]{2,1,0:T(8,128)(2,1)S(1)} async-done(((bf16[8,256,128]{2,1,0:T(8,128)(2,1)}), bf16[8,256,128]{2,1,0:T(8,128)(2,1)S(1)}, u32[]{:S(2)}, u32[]{:S(2)}) %all-to-all-start) | async-done | bytes 524320 | tf_op jit(solution)/shard_map/all_to_all | solution.py:182
  30.5 0.9 shard_map.86
  31.4 0.0 copy-start.4
  31.4 19.1 %all-to-all-start.1 = ((bf16[32,16,128]{2,1,0:T(8,128)(2,1)}), bf16[32,16,128]{2,1,0:T(8,128)(2,1)S(1)}, u32[]{:S(2)}, u32[]{:S(2)}) async-start(bf16[32,16,128]{2,1,0:T(8,128)(2,1)} %bitcast.3), calls=%async_computation.1 | async-start | bytes 262144 | tf_op jit(solution)/shard_map/all_to_all | solution.py:193
  50.5 0.0 copy-done.4
  50.5 2.2 %collective-permute-start = (bf16[128,512]{1,0:T(8,128)(2,1)S(1)}, bf16[128,512]{1,0:T(8,128)(2,1)S(1)}, u32[]{:S(2)}, u32[]{:S(2)}) collective-permute-start(bf16[128,512]{1,0:T(8,128)(2,1)S(1)} %bitcast.33), channel_id=1, source_target_pairs={{0,2},{2,4},{4,6},{6,0},{1,3},{3,5},{5,7},{7,1},{8,10},{10,12},{12... | collective-permute-start | bytes 393224 | tf_op jit(solution)/shard_map/ppermute | solution.py:198
  52.7 3.7 %collective-permute-start.1 = (bf16[128,512]{1,0:T(8,128)(2,1)S(1)}, bf16[128,512]{1,0:T(8,128)(2,1)S(1)}, u32[]{:S(2)}, u32[]{:S(2)}) collective-permute-start(bf16[128,512]{1,0:T(8,128)(2,1)S(1)} %bitcast.34), channel_id=1, source_target_pairs={{0,4},{2,6},{4,0},{6,2},{1,5},{3,7},{5,1},{7,3},{8,12},{10,14},{12... | collective-permute-start | bytes 393224 | tf_op jit(solution)/shard_map/ppermute | solution.py:198
  56.4 2.5 %collective-permute-start.2 = (bf16[128,512]{1,0:T(8,128)(2,1)S(1)}, bf16[128,512]{1,0:T(8,128)(2,1)S(1)}, u32[]{:S(2)}, u32[]{:S(2)}) collective-permute-start(bf16[128,512]{1,0:T(8,128)(2,1)S(1)} %bitcast.35), channel_id=1, source_target_pairs={{0,6},{2,0},{4,2},{6,4},{1,7},{3,1},{5,3},{7,5},{8,14},{10,8},{12,... | collective-permute-start | bytes 393224 | tf_op jit(solution)/shard_map/ppermute | solution.py:198
  58.9 0.0 collective-permute-done
  58.9 1.5 %collective-permute-done.1 = bf16[128,512]{1,0:T(8,128)(2,1)S(1)} collective-permute-done((bf16[128,512]{1,0:T(8,128)(2,1)S(1)}, bf16[128,512]{1,0:T(8,128)(2,1)S(1)}, u32[]{:S(2)}, u32[]{:S(2)}) %collective-permute-start.1) | collective-permute-done | bytes 131104 | tf_op jit(solution)/shard_map/ppermute | solution.py:198
  60.4 3.4 %collective-permute-done.2 = bf16[128,512]{1,0:T(8,128)(2,1)S(1)} collective-permute-done((bf16[128,512]{1,0:T(8,128)(2,1)S(1)}, bf16[128,512]{1,0:T(8,128)(2,1)S(1)}, u32[]{:S(2)}, u32[]{:S(2)}) %collective-permute-start.2) | collective-permute-done | bytes 131104 | tf_op jit(solution)/shard_map/ppermute | solution.py:198
  63.8 2.6 %all-to-all-done.1 = bf16[32,16,128]{2,1,0:T(8,128)(2,1)S(1)} async-done(((bf16[32,16,128]{2,1,0:T(8,128)(2,1)}), bf16[32,16,128]{2,1,0:T(8,128)(2,1)S(1)}, u32[]{:S(2)}, u32[]{:S(2)}) %all-to-all-start.1) | async-done | bytes 131104 | tf_op jit(solution)/shard_map/all_to_all | solution.py:193
  66.5 0.9 broadcast_in_dim.14
  67.4 4.7 %all-to-all-start.2 = ((bf16[16,128,128]{2,1,0:T(8,128)(2,1)}), bf16[16,128,128]{2,1,0:T(8,128)(2,1)S(1)}, u32[]{:S(2)}, u32[]{:S(2)}) async-start(bf16[16,128,128]{2,1,0:T(8,128)(2,1)} %bitcast.9), calls=%async_computation.2 | async-start | bytes 1048576 | tf_op jit(solution)/shard_map/all_to_all | solution.py:207
  72.1 0.0 copy-start.1
  72.1 0.1 pad_maximum_fusion.hops_ref
  72.2 4.0 %collective-permute-start.4 = (bf16[4,128,512]{2,1,0:T(8,128)(2,1)S(1)}, bf16[4,128,512]{2,1,0:T(8,128)(2,1)S(1)}, u32[]{:S(2)}, u32[]{:S(2)}) collective-permute-start(bf16[4,128,512]{2,1,0:T(8,128)(2,1)S(1)} %pad_maximum_fusion.hops_ref), channel_id=1, source_target_pairs={{0,1},{1,0},{2,3},{3,2},{4,5},{5,4},{6,7},{7,6},{8,9},{9,8},{10,11... | collective-permute-start | bytes 1572872 | tf_op jit(solution)/shard_map/ppermute | solution.py:202
  76.2 5.1 %all-to-all-done.2.mine_ref = bf16[16,128,128]{2,1,0:T(8,128)(2,1)S(1)} async-done(((bf16[16,128,128]{2,1,0:T(8,128)(2,1)}), bf16[16,128,128]{2,1,0:T(8,128)(2,1)S(1)}, u32[]{:S(2)}, u32[]{:S(2)}) %all-to-all-start.2) | async-done | bytes 524320 | tf_op jit(solution)/shard_map/all_to_all | solution.py:207
  81.3 5.1 %collective-permute-start.3 = (bf16[16,128,128]{2,1,0:T(8,128)(2,1)S(1)}, bf16[16,128,128]{2,1,0:T(8,128)(2,1)S(1)}, u32[]{:S(2)}, u32[]{:S(2)}) collective-permute-start(bf16[16,128,128]{2,1,0:T(8,128)(2,1)S(1)} %all-to-all-done.2.mine_ref), channel_id=1, source_target_pairs={{0,1},{1,0},{2,3},{3,2},{4,5},{5,4},{6,7},{7,6},{8,9},{9,8},{10,11... | collective-permute-start | bytes 1572872 | tf_op jit(solution)/shard_map/ppermute | solution.py:208
  86.5 0.0 collective-permute-done.4.swapped_ref
  86.5 1.5 %collective-permute-done.3.other_ref = bf16[16,128,128]{2,1,0:T(8,128)(2,1)S(1)} collective-permute-done((bf16[16,128,128]{2,1,0:T(8,128)(2,1)S(1)}, bf16[16,128,128]{2,1,0:T(8,128)(2,1)S(1)}, u32[]{:S(2)}, u32[]{:S(2)}) %collective-permute-start.3) | collective-permute-done | bytes 524320 | tf_op jit(solution)/shard_map/ppermute | solution.py:208
  88.0 0.0 copy-done.1
  88.0 2.1 %shard_map.87 = (bf16[2,512,512]{2,1,0:T(8,128)(2,1)S(1)}, bf16[512,128]{1,0:T(8,128)(2,1)}) custom-call(s32[1]{0:T(128)} %bitcast.1.rank_ref, bf16[16,128,128]{2,1,0:T(8,128)(2,1)S(1)} %all-to-all-done.2.mine_ref, bf16[16,128,128]{2,1,0:T(8,128)(2,1)S(1)} %collective-permute-done.3.other_ref, bf16[4,128,512]{2,1,0:T(8,128)(2,1)S(1)} %pad_maximum_fusion.hops_ref, ...), custom_call_target="tpu_custom_call" | custom-call | tf_op jit(solution)/shard_map/pallas_call | solution.py:160
  90.1 21.0 %all-to-all-start.3 = ((bf16[128,4,128]{2,1,0:T(4,128)(2,1)}), bf16[128,4,128]{2,1,0:T(4,128)(2,1)S(1)}, u32[]{:S(2)}, u32[]{:S(2)}) async-start(bf16[128,4,128]{2,1,0:T(4,128)(2,1)} %bitcast.18), calls=%async_computation.3 | async-start | bytes 262144 | tf_op jit(solution)/shard_map/all_to_all | solution.py:211
  111.1 0.2 iota_compare_fusion
  111.3 0.2 iota_compare_fusion.1
  111.4 0.0 copy-start.2
  111.5 0.2 add_convert_fusion.pick_ref
  111.7 0.7 copy-done.2
  112.4 0.0 copy-start.3
  112.4 1.1 fusion.1
  113.5 0.0 copy-done.3
  113.5 1.1 fusion.3
  114.7 14.4 %all-to-all-done.3 = bf16[128,4,128]{2,1,0:T(4,128)(2,1)S(1)} async-done(((bf16[128,4,128]{2,1,0:T(4,128)(2,1)}), bf16[128,4,128]{2,1,0:T(4,128)(2,1)S(1)}, u32[]{:S(2)}, u32[]{:S(2)}) %all-to-all-start.3) | async-done | bytes 131104 | tf_op jit(solution)/shard_map/all_to_all | solution.py:211
  129.1 1.0 shard_map.88
  (6 shorter events, 0.1 us)
Async XLA Ops:
  0.6 1.0 copy-start
  3.3 17.7 %copy-start.5 = (s32[128]{0:T(128)S(1)}, s32[128]{0:T(128)}, u32[]{:S(2)}) copy-start(s32[128]{0:T(128)} %param.7) | copy-start | bytes 1540
  3.3 27.2 %all-to-all-start = ((bf16[8,256,128]{2,1,0:T(8,128)(2,1)}), bf16[8,256,128]{2,1,0:T(8,128)(2,1)S(1)}, u32[]{:S(2)}, u32[]{:S(2)}) async-start(bf16[8,256,128]{2,1,0:T(8,128)(2,1)} %shard_map.85), calls=%async_computation | async-start | bytes 1048576 | tf_op jit(solution)/shard_map/all_to_all | solution.py:182
  31.4 19.1 %copy-start.4 = (bf16[1,2,64,512]{3,2,1,0:T(8,128)(2,1)S(1)}, bf16[1,2,64,512]{3,2,1,0:T(8,128)(2,1)}, u32[]{:S(2)}) copy-start(bf16[1,2,64,512]{3,2,1,0:T(8,128)(2,1)} %param.10) | copy-start | bytes 393220
  31.4 35.0 %all-to-all-start.1 = ((bf16[32,16,128]{2,1,0:T(8,128)(2,1)}), bf16[32,16,128]{2,1,0:T(8,128)(2,1)S(1)}, u32[]{:S(2)}, u32[]{:S(2)}) async-start(bf16[32,16,128]{2,1,0:T(8,128)(2,1)} %bitcast.3), calls=%async_computation.1 | async-start | bytes 262144 | tf_op jit(solution)/shard_map/all_to_all | solution.py:193
  50.5 8.5 %collective-permute-start = (bf16[128,512]{1,0:T(8,128)(2,1)S(1)}, bf16[128,512]{1,0:T(8,128)(2,1)S(1)}, u32[]{:S(2)}, u32[]{:S(2)}) collective-permute-start(bf16[128,512]{1,0:T(8,128)(2,1)S(1)} %bitcast.33), channel_id=1, source_target_pairs={{0,2},{2,4},{4,6},{6,0},{1,3},{3,5},{5,7},{7,1},{8,10},{10,12},{12... | collective-permute-start | bytes 393224 | tf_op jit(solution)/shard_map/ppermute | solution.py:198
  52.7 7.7 %collective-permute-start.1 = (bf16[128,512]{1,0:T(8,128)(2,1)S(1)}, bf16[128,512]{1,0:T(8,128)(2,1)S(1)}, u32[]{:S(2)}, u32[]{:S(2)}) collective-permute-start(bf16[128,512]{1,0:T(8,128)(2,1)S(1)} %bitcast.34), channel_id=1, source_target_pairs={{0,4},{2,6},{4,0},{6,2},{1,5},{3,7},{5,1},{7,3},{8,12},{10,14},{12... | collective-permute-start | bytes 393224 | tf_op jit(solution)/shard_map/ppermute | solution.py:198
  56.4 7.4 %collective-permute-start.2 = (bf16[128,512]{1,0:T(8,128)(2,1)S(1)}, bf16[128,512]{1,0:T(8,128)(2,1)S(1)}, u32[]{:S(2)}, u32[]{:S(2)}) collective-permute-start(bf16[128,512]{1,0:T(8,128)(2,1)S(1)} %bitcast.35), channel_id=1, source_target_pairs={{0,6},{2,0},{4,2},{6,4},{1,7},{3,1},{5,3},{7,5},{8,14},{10,8},{12,... | collective-permute-start | bytes 393224 | tf_op jit(solution)/shard_map/ppermute | solution.py:198
  67.4 14.0 %all-to-all-start.2 = ((bf16[16,128,128]{2,1,0:T(8,128)(2,1)}), bf16[16,128,128]{2,1,0:T(8,128)(2,1)S(1)}, u32[]{:S(2)}, u32[]{:S(2)}) async-start(bf16[16,128,128]{2,1,0:T(8,128)(2,1)} %bitcast.9), calls=%async_computation.2 | async-start | bytes 1048576 | tf_op jit(solution)/shard_map/all_to_all | solution.py:207
  72.1 15.9 %copy-start.1 = (bf16[1,2,64,512]{3,2,1,0:T(8,128)(2,1)S(1)}, bf16[1,2,64,512]{3,2,1,0:T(8,128)(2,1)}, u32[]{:S(2)}) copy-start(bf16[1,2,64,512]{3,2,1,0:T(8,128)(2,1)} %param.11) | copy-start | bytes 393220
  72.2 14.3 %collective-permute-start.4 = (bf16[4,128,512]{2,1,0:T(8,128)(2,1)S(1)}, bf16[4,128,512]{2,1,0:T(8,128)(2,1)S(1)}, u32[]{:S(2)}, u32[]{:S(2)}) collective-permute-start(bf16[4,128,512]{2,1,0:T(8,128)(2,1)S(1)} %pad_maximum_fusion.hops_ref), channel_id=1, source_target_pairs={{0,1},{1,0},{2,3},{3,2},{4,5},{5,4},{6,7},{7,6},{8,9},{9,8},{10,11... | collective-permute-start | bytes 1572872 | tf_op jit(solution)/shard_map/ppermute | solution.py:202
  81.3 6.7 %collective-permute-start.3 = (bf16[16,128,128]{2,1,0:T(8,128)(2,1)S(1)}, bf16[16,128,128]{2,1,0:T(8,128)(2,1)S(1)}, u32[]{:S(2)}, u32[]{:S(2)}) collective-permute-start(bf16[16,128,128]{2,1,0:T(8,128)(2,1)S(1)} %all-to-all-done.2.mine_ref), channel_id=1, source_target_pairs={{0,1},{1,0},{2,3},{3,2},{4,5},{5,4},{6,7},{7,6},{8,9},{9,8},{10,11... | collective-permute-start | bytes 1572872 | tf_op jit(solution)/shard_map/ppermute | solution.py:208
  90.1 39.0 %all-to-all-start.3 = ((bf16[128,4,128]{2,1,0:T(4,128)(2,1)}), bf16[128,4,128]{2,1,0:T(4,128)(2,1)S(1)}, u32[]{:S(2)}, u32[]{:S(2)}) async-start(bf16[128,4,128]{2,1,0:T(4,128)(2,1)} %bitcast.18), calls=%async_computation.3 | async-start | bytes 262144 | tf_op jit(solution)/shard_map/all_to_all | solution.py:211
  111.4 1.0 copy-start.2
  112.4 1.1 copy-start.3

commit v8 on v7

--- a/solution.py
+++ b/solution.py
@@ -56,7 +56,7 @@
             for h in range(halves):
                 for r in range(per):
                     row = (h * per + r) * step
-                    out_ref[g * halves + h, r * blocks + t * step:r * blocks + (t + 1) * step, :] = (
+                    out_ref[(g * halves + h) ^ (nrep // 2), r * blocks + t * step:r * blocks + (t + 1) * step, :] = (
                         terms[row:row + step])
 
 
@@ -179,7 +179,8 @@
     slab = width // nrep
     rank = lax.axis_index(REP)
 
-    got = lax.all_to_all(code_call(x, nrep), REP, split_axis=0, concat_axis=0, tiled=True)
+    got = lax.all_to_all(code_call(x, nrep), REP, split_axis=0, concat_axis=0, tiled=True,
+                         axis_index_groups=[[p ^ (nrep // 2) for p in range(nrep)]])
 
     counter = jnp.arange(nb, dtype=I32)
     same = owner[:, None] == owner[None, :]

time: 131 us -> 132 us (level)
  starting transfers between devices: 80.1 us -> 85.2 us
  waiting for transfers between devices: 37.7 us -> 33.4 us
    all_to_all x1, waiting for transfers between devices: 9.2 us -> 6.67 us  [on_device(): lax.all_to_all(code_call(x, nrep), REP, split_axis=0, concat_axis=0, tile...]
    ppermute x3, waiting for transfers between devices: 4.86 us -> 2.54 us  [on_device(): lax.ppermute(own, 'y', [(j, (j + d) % groups) for j in range(groups)])]
    ppermute x3, starting transfers between devices: 8.42 us -> 10.5 us  [on_device(): lax.ppermute(own, 'y', [(j, (j + d) % groups) for j in range(groups)])]
    all_to_all x1, starting transfers between devices: 4.73 us -> 6.16 us  [on_device(): lax.all_to_all(copies, ('x', 'y'), split_axis=0, concat_axis=0, tiled=True)]
where the time goes in v8:
time: 132 us; the launch traced here: 131 us
  starting transfers between devices  85.2 us (65%)
  waiting for transfers between devices  33.4 us (25%)
  Pallas kernels  5.62 us (4%)
  local copies, waits for them, and re-layouts  2.75 us (2%)
  matrix products  2.28 us (2%)
    all_to_all x1, starting transfers between devices, on_device(): lax.all_to_all(packed, FSDP, split_axis=0, concat_axis=0, tiled=True, axi...  20.9 us
    all_to_all x1, starting transfers between devices, on_device(): lax.all_to_all(outgoing, 'z', split_axis=0, concat_axis=0, tiled=True, ax...  19.7 us
    all_to_all x1, starting transfers between devices, on_device(): lax.all_to_all(code_call(x, nrep), REP, split_axis=0, concat_axis=0, tile...  18.7 us
    all_to_all x1, waiting for transfers between devices, on_device(): lax.all_to_all(packed, FSDP, split_axis=0, concat_axis=0, tiled=True, axi...  14.4 us
    ppermute x3, starting transfers between devices, on_device(): lax.ppermute(own, 'y', [(j, (j + d) % groups) for j in range(groups)])  10.5 us
    all_to_all x1, waiting for transfers between devices, on_device(): lax.all_to_all(code_call(x, nrep), REP, split_axis=0, concat_axis=0, tile...  6.67 us
    all_to_all x1, starting transfers between devices, on_device(): lax.all_to_all(copies, ('x', 'y'), split_axis=0, concat_axis=0, tiled=True)  6.16 us
    ppermute x1, starting transfers between devices, on_device(): other = lax.ppermute(mine, 'core', swap)  5.13 us
  transfers between devices with their start and end apart: 9, of which 7 were waited for; matrix products, arithmetic and copies ran while one was open for 2% of the time, Pallas kernels for 0%

profile of v8, /device:TPU:1, one launch (start us, length us, event | category | flops | bytes accessed | tf_op | source)
XLA Modules:
  0.0 131.0 jit_solution(13060927267102664563)
XLA Ops:
  0.6 0.0 copy-start
  0.6 1.0 copy-done
  1.7 1.6 %shard_map.85 = bf16[8,256,128]{2,1,0:T(8,128)(2,1)} custom-call(bf16[128,4,512]{2,1,0:T(4,128)(2,1)S(1)} %bitcast.29), custom_call_target="tpu_custom_call" | custom-call | tf_op jit(solution)/shard_map/pallas_call | solution.py:128
  3.3 0.0 copy-start.5
  3.3 18.7 %all-to-all-start = ((bf16[8,256,128]{2,1,0:T(8,128)(2,1)}), bf16[8,256,128]{2,1,0:T(8,128)(2,1)S(1)}, u32[]{:S(2)}, u32[]{:S(2)}) async-start(bf16[8,256,128]{2,1,0:T(8,128)(2,1)} %shard_map.85), calls=%async_computation | async-start | bytes 1048576 | tf_op jit(solution)/shard_map/all_to_all | solution.py:182
  22.0 0.0 copy-done.5
  22.0 0.2 convert_reduce_fusion
  22.2 0.1 fusion.4.route_ref
  22.3 6.7 %all-to-all-done.got_ref = bf16[8,256,128]{2,1,0:T(8,128)(2,1)S(1)} async-done(((bf16[8,256,128]{2,1,0:T(8,128)(2,1)}), bf16[8,256,128]{2,1,0:T(8,128)(2,1)S(1)}, u32[]{:S(2)}, u32[]{:S(2)}) %all-to-all-start) | async-done | bytes 524320 | tf_op jit(solution)/shard_map/all_to_all | solution.py:182
  29.0 0.9 shard_map.86
  29.9 0.0 copy-start.4
  29.9 19.7 %all-to-all-start.1 = ((bf16[32,16,128]{2,1,0:T(8,128)(2,1)}), bf16[32,16,128]{2,1,0:T(8,128)(2,1)S(1)}, u32[]{:S(2)}, u32[]{:S(2)}) async-start(bf16[32,16,128]{2,1,0:T(8,128)(2,1)} %bitcast.3), calls=%async_computation.1 | async-start | bytes 262144 | tf_op jit(solution)/shard_map/all_to_all | solution.py:194
  49.7 0.0 copy-done.4
  49.7 2.5 %collective-permute-start = (bf16[128,512]{1,0:T(8,128)(2,1)S(1)}, bf16[128,512]{1,0:T(8,128)(2,1)S(1)}, u32[]{:S(2)}, u32[]{:S(2)}) collective-permute-start(bf16[128,512]{1,0:T(8,128)(2,1)S(1)} %bitcast.33), channel_id=1, source_target_pairs={{0,2},{2,4},{4,6},{6,0},{1,3},{3,5},{5,7},{7,1},{8,10},{10,12},{12... | collective-permute-start | bytes 393224 | tf_op jit(solution)/shard_map/ppermute | solution.py:199
  52.1 4.3 %collective-permute-start.1 = (bf16[128,512]{1,0:T(8,128)(2,1)S(1)}, bf16[128,512]{1,0:T(8,128)(2,1)S(1)}, u32[]{:S(2)}, u32[]{:S(2)}) collective-permute-start(bf16[128,512]{1,0:T(8,128)(2,1)S(1)} %bitcast.34), channel_id=1, source_target_pairs={{0,4},{2,6},{4,0},{6,2},{1,5},{3,7},{5,1},{7,3},{8,12},{10,14},{12... | collective-permute-start | bytes 393224 | tf_op jit(solution)/shard_map/ppermute | solution.py:199
  56.5 3.7 %collective-permute-start.2 = (bf16[128,512]{1,0:T(8,128)(2,1)S(1)}, bf16[128,512]{1,0:T(8,128)(2,1)S(1)}, u32[]{:S(2)}, u32[]{:S(2)}) collective-permute-start(bf16[128,512]{1,0:T(8,128)(2,1)S(1)} %bitcast.35), channel_id=1, source_target_pairs={{0,6},{2,0},{4,2},{6,4},{1,7},{3,1},{5,3},{7,5},{8,14},{10,8},{12,... | collective-permute-start | bytes 393224 | tf_op jit(solution)/shard_map/ppermute | solution.py:199
  60.2 0.0 collective-permute-done
  60.2 0.4 collective-permute-done.1
  60.6 2.1 %collective-permute-done.2 = bf16[128,512]{1,0:T(8,128)(2,1)S(1)} collective-permute-done((bf16[128,512]{1,0:T(8,128)(2,1)S(1)}, bf16[128,512]{1,0:T(8,128)(2,1)S(1)}, u32[]{:S(2)}, u32[]{:S(2)}) %collective-permute-start.2) | collective-permute-done | bytes 131104 | tf_op jit(solution)/shard_map/ppermute | solution.py:199
  62.7 3.2 %all-to-all-done.1 = bf16[32,16,128]{2,1,0:T(8,128)(2,1)S(1)} async-done(((bf16[32,16,128]{2,1,0:T(8,128)(2,1)}), bf16[32,16,128]{2,1,0:T(8,128)(2,1)S(1)}, u32[]{:S(2)}, u32[]{:S(2)}) %all-to-all-start.1) | async-done | bytes 131104 | tf_op jit(solution)/shard_map/all_to_all | solution.py:194
  66.0 0.9 broadcast_in_dim.14
  66.9 6.2 %all-to-all-start.2 = ((bf16[16,128,128]{2,1,0:T(8,128)(2,1)}), bf16[16,128,128]{2,1,0:T(8,128)(2,1)S(1)}, u32[]{:S(2)}, u32[]{:S(2)}) async-start(bf16[16,128,128]{2,1,0:T(8,128)(2,1)} %bitcast.9), calls=%async_computation.2 | async-start | bytes 1048576 | tf_op jit(solution)/shard_map/all_to_all | solution.py:208
  73.1 0.0 copy-start.1
  73.1 0.1 pad_maximum_fusion.hops_ref
  73.2 4.0 %collective-permute-start.4 = (bf16[4,128,512]{2,1,0:T(8,128)(2,1)S(1)}, bf16[4,128,512]{2,1,0:T(8,128)(2,1)S(1)}, u32[]{:S(2)}, u32[]{:S(2)}) collective-permute-start(bf16[4,128,512]{2,1,0:T(8,128)(2,1)S(1)} %pad_maximum_fusion.hops_ref), channel_id=1, source_target_pairs={{0,1},{1,0},{2,3},{3,2},{4,5},{5,4},{6,7},{7,6},{8,9},{9,8},{10,11... | collective-permute-start | bytes 1572872 | tf_op jit(solution)/shard_map/ppermute | solution.py:203
  77.2 5.1 %all-to-all-done.2.mine_ref = bf16[16,128,128]{2,1,0:T(8,128)(2,1)S(1)} async-done(((bf16[16,128,128]{2,1,0:T(8,128)(2,1)}), bf16[16,128,128]{2,1,0:T(8,128)(2,1)S(1)}, u32[]{:S(2)}, u32[]{:S(2)}) %all-to-all-start.2) | async-done | bytes 524320 | tf_op jit(solution)/shard_map/all_to_all | solution.py:208
  82.3 5.1 %collective-permute-start.3 = (bf16[16,128,128]{2,1,0:T(8,128)(2,1)S(1)}, bf16[16,128,128]{2,1,0:T(8,128)(2,1)S(1)}, u32[]{:S(2)}, u32[]{:S(2)}) collective-permute-start(bf16[16,128,128]{2,1,0:T(8,128)(2,1)S(1)} %all-to-all-done.2.mine_ref), channel_id=1, source_target_pairs={{0,1},{1,0},{2,3},{3,2},{4,5},{5,4},{6,7},{7,6},{8,9},{9,8},{10,11... | collective-permute-start | bytes 1572872 | tf_op jit(solution)/shard_map/ppermute | solution.py:209
  87.5 0.0 collective-permute-done.4.swapped_ref
  87.5 1.5 %collective-permute-done.3.other_ref = bf16[16,128,128]{2,1,0:T(8,128)(2,1)S(1)} collective-permute-done((bf16[16,128,128]{2,1,0:T(8,128)(2,1)S(1)}, bf16[16,128,128]{2,1,0:T(8,128)(2,1)S(1)}, u32[]{:S(2)}, u32[]{:S(2)}) %collective-permute-start.3) | collective-permute-done | bytes 524320 | tf_op jit(solution)/shard_map/ppermute | solution.py:209
  88.9 0.0 copy-done.1
  88.9 2.1 %shard_map.87 = (bf16[2,512,512]{2,1,0:T(8,128)(2,1)S(1)}, bf16[512,128]{1,0:T(8,128)(2,1)}) custom-call(s32[1]{0:T(128)} %bitcast.1.rank_ref, bf16[16,128,128]{2,1,0:T(8,128)(2,1)S(1)} %all-to-all-done.2.mine_ref, bf16[16,128,128]{2,1,0:T(8,128)(2,1)S(1)} %collective-permute-done.3.other_ref, bf16[4,128,512]{2,1,0:T(8,128)(2,1)S(1)} %pad_maximum_fusion.hops_ref, ...), custom_call_target="tpu_custom_call" | custom-call | tf_op jit(solution)/shard_map/pallas_call | solution.py:160
  91.0 20.9 %all-to-all-start.3 = ((bf16[128,4,128]{2,1,0:T(4,128)(2,1)}), bf16[128,4,128]{2,1,0:T(4,128)(2,1)S(1)}, u32[]{:S(2)}, u32[]{:S(2)}) async-start(bf16[128,4,128]{2,1,0:T(4,128)(2,1)} %bitcast.18), calls=%async_computation.3 | async-start | bytes 262144 | tf_op jit(solution)/shard_map/all_to_all | solution.py:212
  112.0 0.2 iota_compare_fusion
  112.2 0.2 iota_compare_fusion.1
  112.3 0.0 copy-start.2
  112.3 0.2 add_convert_fusion.pick_ref
  112.5 0.7 copy-done.2
  113.3 0.0 copy-start.3
  113.3 1.1 fusion.1
  114.4 0.0 copy-done.3
  114.4 1.1 fusion.3
  115.6 14.4 %all-to-all-done.3 = bf16[128,4,128]{2,1,0:T(4,128)(2,1)S(1)} async-done(((bf16[128,4,128]{2,1,0:T(4,128)(2,1)}), bf16[128,4,128]{2,1,0:T(4,128)(2,1)S(1)}, u32[]{:S(2)}, u32[]{:S(2)}) %all-to-all-start.3) | async-done | bytes 131104 | tf_op jit(solution)/shard_map/all_to_all | solution.py:212
  130.0 1.0 shard_map.88
  (6 shorter events, 0.1 us)
Async XLA Ops:
  0.6 1.0 copy-start
  3.3 18.7 %copy-start.5 = (s32[128]{0:T(128)S(1)}, s32[128]{0:T(128)}, u32[]{:S(2)}) copy-start(s32[128]{0:T(128)} %param.7) | copy-start | bytes 1540
  3.3 25.7 %all-to-all-start = ((bf16[8,256,128]{2,1,0:T(8,128)(2,1)}), bf16[8,256,128]{2,1,0:T(8,128)(2,1)S(1)}, u32[]{:S(2)}, u32[]{:S(2)}) async-start(bf16[8,256,128]{2,1,0:T(8,128)(2,1)} %shard_map.85), calls=%async_computation | async-start | bytes 1048576 | tf_op jit(solution)/shard_map/all_to_all | solution.py:182
  29.9 19.8 %copy-start.4 = (bf16[1,2,64,512]{3,2,1,0:T(8,128)(2,1)S(1)}, bf16[1,2,64,512]{3,2,1,0:T(8,128)(2,1)}, u32[]{:S(2)}) copy-start(bf16[1,2,64,512]{3,2,1,0:T(8,128)(2,1)} %param.10) | copy-start | bytes 393220
  29.9 36.0 %all-to-all-start.1 = ((bf16[32,16,128]{2,1,0:T(8,128)(2,1)}), bf16[32,16,128]{2,1,0:T(8,128)(2,1)S(1)}, u32[]{:S(2)}, u32[]{:S(2)}) async-start(bf16[32,16,128]{2,1,0:T(8,128)(2,1)} %bitcast.3), calls=%async_computation.1 | async-start | bytes 262144 | tf_op jit(solution)/shard_map/all_to_all | solution.py:194
  49.7 10.5 %collective-permute-start = (bf16[128,512]{1,0:T(8,128)(2,1)S(1)}, bf16[128,512]{1,0:T(8,128)(2,1)S(1)}, u32[]{:S(2)}, u32[]{:S(2)}) collective-permute-start(bf16[128,512]{1,0:T(8,128)(2,1)S(1)} %bitcast.33), channel_id=1, source_target_pairs={{0,2},{2,4},{4,6},{6,0},{1,3},{3,5},{5,7},{7,1},{8,10},{10,12},{12... | collective-permute-start | bytes 393224 | tf_op jit(solution)/shard_map/ppermute | solution.py:199
  52.1 8.4 %collective-permute-start.1 = (bf16[128,512]{1,0:T(8,128)(2,1)S(1)}, bf16[128,512]{1,0:T(8,128)(2,1)S(1)}, u32[]{:S(2)}, u32[]{:S(2)}) collective-permute-start(bf16[128,512]{1,0:T(8,128)(2,1)S(1)} %bitcast.34), channel_id=1, source_target_pairs={{0,4},{2,6},{4,0},{6,2},{1,5},{3,7},{5,1},{7,3},{8,12},{10,14},{12... | collective-permute-start | bytes 393224 | tf_op jit(solution)/shard_map/ppermute | solution.py:199
  56.5 6.2 %collective-permute-start.2 = (bf16[128,512]{1,0:T(8,128)(2,1)S(1)}, bf16[128,512]{1,0:T(8,128)(2,1)S(1)}, u32[]{:S(2)}, u32[]{:S(2)}) collective-permute-start(bf16[128,512]{1,0:T(8,128)(2,1)S(1)} %bitcast.35), channel_id=1, source_target_pairs={{0,6},{2,0},{4,2},{6,4},{1,7},{3,1},{5,3},{7,5},{8,14},{10,8},{12,... | collective-permute-start | bytes 393224 | tf_op jit(solution)/shard_map/ppermute | solution.py:199
  66.9 15.4 %all-to-all-start.2 = ((bf16[16,128,128]{2,1,0:T(8,128)(2,1)}), bf16[16,128,128]{2,1,0:T(8,128)(2,1)S(1)}, u32[]{:S(2)}, u32[]{:S(2)}) async-start(bf16[16,128,128]{2,1,0:T(8,128)(2,1)} %bitcast.9), calls=%async_computation.2 | async-start | bytes 1048576 | tf_op jit(solution)/shard_map/all_to_all | solution.py:208
  73.1 15.9 %copy-start.1 = (bf16[1,2,64,512]{3,2,1,0:T(8,128)(2,1)S(1)}, bf16[1,2,64,512]{3,2,1,0:T(8,128)(2,1)}, u32[]{:S(2)}) copy-start(bf16[1,2,64,512]{3,2,1,0:T(8,128)(2,1)} %param.11) | copy-start | bytes 393220
  73.2 14.3 %collective-permute-start.4 = (bf16[4,128,512]{2,1,0:T(8,128)(2,1)S(1)}, bf16[4,128,512]{2,1,0:T(8,128)(2,1)S(1)}, u32[]{:S(2)}, u32[]{:S(2)}) collective-permute-start(bf16[4,128,512]{2,1,0:T(8,128)(2,1)S(1)} %pad_maximum_fusion.hops_ref), channel_id=1, source_target_pairs={{0,1},{1,0},{2,3},{3,2},{4,5},{5,4},{6,7},{7,6},{8,9},{9,8},{10,11... | collective-permute-start | bytes 1572872 | tf_op jit(solution)/shard_map/ppermute | solution.py:203
  82.3 6.7 %collective-permute-start.3 = (bf16[16,128,128]{2,1,0:T(8,128)(2,1)S(1)}, bf16[16,128,128]{2,1,0:T(8,128)(2,1)S(1)}, u32[]{:S(2)}, u32[]{:S(2)}) collective-permute-start(bf16[16,128,128]{2,1,0:T(8,128)(2,1)S(1)} %all-to-all-done.2.mine_ref), channel_id=1, source_target_pairs={{0,1},{1,0},{2,3},{3,2},{4,5},{5,4},{6,7},{7,6},{8,9},{9,8},{10,11... | collective-permute-start | bytes 1572872 | tf_op jit(solution)/shard_map/ppermute | solution.py:209
  91.0 39.0 %all-to-all-start.3 = ((bf16[128,4,128]{2,1,0:T(4,128)(2,1)}), bf16[128,4,128]{2,1,0:T(4,128)(2,1)S(1)}, u32[]{:S(2)}, u32[]{:S(2)}) async-start(bf16[128,4,128]{2,1,0:T(4,128)(2,1)} %bitcast.18), calls=%async_computation.3 | async-start | bytes 262144 | tf_op jit(solution)/shard_map/all_to_all | solution.py:212
  112.3 1.0 copy-start.2
  113.3 1.1 copy-start.3
